TPU v7x, 512 devices: a whole 4x4x16 slice. The times are simulated.
512 devices in a mesh: ctx: 64 (over y, z), tp: 8 (over x, core).
Axes of the slice: x: 4, y: 4, z: 16, core: 2. Of those that a mesh axis runs over, the one named last changes fastest.
Arguments:
- queries: bfloat16 [8192, 16384], P('ctx', 'tp'), may hold values from -16 to 16
- keys: bfloat16 [8192, 1024], P('ctx', 'tp'), may hold values from -16 to 16
- values: bfloat16 [8192, 1024], P('ctx', 'tp'), may hold values from -6 to 6
- grad_out: bfloat16 [8192, 16384], P('ctx', 'tp'), may hold values from -6 to 6
- doc_lengths: int32 [32], replicated, may hold values from 1 to 512, 8192 in all
Outputs:
- grad_q: bfloat16 [8192, 16384], P('ctx', 'tp')
- grad_k: bfloat16 [8192, 1024], P('ctx', 'tp')
- grad_v: bfloat16 [8192, 1024], P('ctx', 'tp')
Inputs may be any that keep to these rules, and one draw needn't show every extreme that they name: `doc_lengths`: 32 lengths that sum to 8192; the longest is exactly 512.
All inputs are finite; a program needn't handle non-finite values.
Results may differ from a plain program's by a relative error of at most 0.035.
Values may be sent and summed in bfloat16 or wider, within the bound.
No kernel may reach another device: no remote copies, remote signals or barrier semaphores. Data moves between devices by JAX's collectives and lax.ppermute only.
A program may use at most 64 MiB of HBM per device.

v0:
```python
import math

import jax
import jax.numpy as jnp
from jax import lax
from jax.sharding import PartitionSpec as P

HEADS = 128
KV_HEADS = 8
HEAD_DIM = 128
REACH = 4


def passed_along(array, axis, by):
    devices = lax.axis_size(axis)
    pairs = [(i, i + by) for i in range(devices) if 0 <= i + by < devices]
    return lax.ppermute(array, axis, pairs)


def segment_of(positions, ends):
    return jnp.sum((positions[:, None] >= ends[None, :]).astype(jnp.int32), axis=1)


def make_mask(query_pos, key_pos, ends):
    query_seg = segment_of(query_pos, ends)
    key_seg = segment_of(key_pos, ends)
    visible = (key_pos[None, :] <= query_pos[:, None]) & (key_pos[None, :] >= 0)
    visible = visible & (key_seg[None, :] == query_seg[:, None])
    return visible[None, None, :, :]


def attend(query_blk, key_win, value_win, grad_blk, mask):
    scale = 1.0 / math.sqrt(key_win.shape[-1])
    scores = (
        jnp.einsum("qghd,kgd->ghqk", query_blk, key_win, preferred_element_type=jnp.float32) * scale
    )
    scores = jnp.where(mask, scores, -1e30)
    peak = jnp.max(scores, axis=-1, keepdims=True)
    total = jnp.sum(jnp.where(mask, jnp.exp(scores - peak), 0.0), axis=-1, keepdims=True)
    lse = peak + jnp.log(total)
    probs = jnp.where(mask, jnp.exp(scores - lse), 0.0)
    probs_b = probs.astype(jnp.bfloat16)
    output = jnp.einsum(
        "ghqk,kgd->qghd", probs_b, value_win, preferred_element_type=jnp.float32
    ).astype(jnp.bfloat16)
    delta = jnp.einsum("qghd,qghd->ghq", grad_blk.astype(jnp.float32), output.astype(jnp.float32))
    dprobs = jnp.einsum("qghd,kgd->ghqk", grad_blk, value_win, preferred_element_type=jnp.float32)
    dscore = (probs * (dprobs - delta[..., None])).astype(jnp.bfloat16)
    grad_query = (
        jnp.einsum("ghqk,kgd->qghd", dscore, key_win, preferred_element_type=jnp.float32) * scale
    ).astype(jnp.bfloat16)
    grad_key = (
        jnp.einsum("ghqk,qghd->kgd", dscore, query_blk, preferred_element_type=jnp.float32) * scale
    )
    grad_value = jnp.einsum("ghqk,qghd->kgd", probs_b, grad_blk, preferred_element_type=jnp.float32)
    return (grad_query, grad_key, grad_value)


def local(queries, keys, values, grad_out, doc_lengths):
    tok = keys.shape[0]
    kv_local = keys.shape[1] // HEAD_DIM
    group = HEADS // KV_HEADS
    head_block = math.gcd(4, group)
    turns = group // head_block
    index = lax.axis_index("ctx")
    stacked = jnp.stack([keys, values])
    pieces = [stacked]
    current = stacked
    for offset in range(1, REACH + 1):
        current = passed_along(current, "ctx", 1)
        pieces.append(current)
    window = jnp.concatenate([pieces[REACH - offset] for offset in range(REACH + 1)], axis=1)
    width = window.shape[1]
    key_win = window[0].reshape(width, kv_local, HEAD_DIM)
    value_win = window[1].reshape(width, kv_local, HEAD_DIM)
    ends = jnp.cumsum(doc_lengths)
    query_pos = index * tok + jnp.arange(tok, dtype=jnp.int32)
    key_pos = (index - REACH) * tok + jnp.arange(width, dtype=jnp.int32)
    mask = make_mask(query_pos, key_pos, ends)
    query_turns = jnp.moveaxis(queries.reshape(tok, kv_local, turns, head_block, HEAD_DIM), 2, 0)
    grad_turns = jnp.moveaxis(grad_out.reshape(tok, kv_local, turns, head_block, HEAD_DIM), 2, 0)

    def turn(carry, inputs):
        query_blk, grad_blk = inputs
        grad_query, grad_key, grad_value = attend(query_blk, key_win, value_win, grad_blk, mask)
        return ((carry[0] + grad_key, carry[1] + grad_value), grad_query)

    zeros = jnp.zeros((width, kv_local, HEAD_DIM), jnp.float32)
    (grad_key, grad_value), grad_queries = lax.scan(turn, (zeros, zeros), (query_turns, grad_turns))
    grad_q = jnp.moveaxis(grad_queries, 0, 2).reshape(tok, kv_local * group * HEAD_DIM)
    partial_sums = jnp.stack([grad_key, grad_value]).reshape(2, width, kv_local * HEAD_DIM)

    def share(offset):
        return partial_sums[:, (REACH - offset) * tok : (REACH - offset + 1) * tok]

    running = share(REACH)
    for offset in range(REACH - 1, -1, -1):
        running = passed_along(running, "ctx", -1) + share(offset)
    return (grad_q, running[0].astype(jnp.bfloat16), running[1].astype(jnp.bfloat16))


def solution(mesh):
    placed = (P("ctx", "tp"), P("ctx", "tp"), P("ctx", "tp"), P("ctx", "tp"), P())
    return jax.shard_map(
        local,
        mesh=mesh,
        in_specs=placed,
        out_specs=(P("ctx", "tp"), P("ctx", "tp"), P("ctx", "tp")),
        check_vma=False,
    )
```

profile of v0, /device:TPU:24, one launch (start us, length us, event | category | flops | bytes accessed | tf_op | source)
XLA Modules:
  0.0 98.3 jit_solution(1760102128707393439)
XLA Ops:
  0.6 0.8 pad_maximum_fusion
  1.5 3.8 %collective-permute-start = (bf16[2,128,128]{2,1,0:T(8,128)(2,1)S(1)}, bf16[2,128,128]{2,1,0:T(8,128)(2,1)S(1)}, u32[]{:S(2)}, u32[]{:S(2)}) collective-permute-start(bf16[2,128,128]{2,1,0:T(8,128)(2,1)S(1)} %pad_maximum_fusion), channel_id=1, source_target_pairs={{0,8},{8,16},{16,24},{24,32},{32,40},{40,48},{48,56},{56,64},{64,7... | collective-permute-start | bytes 196616 | tf_op jit(solution)/shard_map/ppermute | solution.py:17
  5.4 0.7 copy.28
  6.3 1.3 %copy.26 = bf16[128,2048]{0,1:T(8,128)(2,1)S(1)} copy(bf16[128,2048]{1,0:T(8,128)(2,1)} %param.7) | data formatting | bytes 1048576 | tf_op args[0]
  8.0 7.3 %collective-permute-done = bf16[2,128,128]{2,1,0:T(8,128)(2,1)S(1)} collective-permute-done((bf16[2,128,128]{2,1,0:T(8,128)(2,1)S(1)}, bf16[2,128,128]{2,1,0:T(8,128)(2,1)S(1)}, u32[]{:S(2)}, u32[]{:S(2)}) %collective-permute-start) | collective-permute-done | bytes 65568 | tf_op jit(solution)/shard_map/ppermute | solution.py:17
  15.3 1.9 %collective-permute-start.1 = (bf16[2,128,128]{2,1,0:T(8,128)(2,1)S(1)}, bf16[2,128,128]{2,1,0:T(8,128)(2,1)S(1)}, u32[]{:S(2)}, u32[]{:S(2)}) collective-permute-start(bf16[2,128,128]{2,1,0:T(8,128)(2,1)S(1)} %collective-permute-done), channel_id=1, source_target_pairs={{0,8},{8,16},{16,24},{24,32},{32,40},{40,48},{48,56},{56,64},{64,7... | collective-permute-start | bytes 196616 | tf_op jit(solution)/shard_map/ppermute | solution.py:17
  17.2 6.3 %collective-permute-done.1 = bf16[2,128,128]{2,1,0:T(8,128)(2,1)S(1)} collective-permute-done((bf16[2,128,128]{2,1,0:T(8,128)(2,1)S(1)}, bf16[2,128,128]{2,1,0:T(8,128)(2,1)S(1)}, u32[]{:S(2)}, u32[]{:S(2)}) %collective-permute-start.1) | collective-permute-done | bytes 65568 | tf_op jit(solution)/shard_map/ppermute | solution.py:17
  23.5 1.9 %collective-permute-start.2 = (bf16[2,128,128]{2,1,0:T(8,128)(2,1)S(1)}, bf16[2,128,128]{2,1,0:T(8,128)(2,1)S(1)}, u32[]{:S(2)}, u32[]{:S(2)}) collective-permute-start(bf16[2,128,128]{2,1,0:T(8,128)(2,1)S(1)} %collective-permute-done.1), channel_id=1, source_target_pairs={{0,8},{8,16},{16,24},{24,32},{32,40},{40,48},{48,56},{56,64},{64,7... | collective-permute-start | bytes 196616 | tf_op jit(solution)/shard_map/ppermute | solution.py:17
  25.6 6.2 %collective-permute-done.2 = bf16[2,128,128]{2,1,0:T(8,128)(2,1)S(1)} collective-permute-done((bf16[2,128,128]{2,1,0:T(8,128)(2,1)S(1)}, bf16[2,128,128]{2,1,0:T(8,128)(2,1)S(1)}, u32[]{:S(2)}, u32[]{:S(2)}) %collective-permute-start.2) | collective-permute-done | bytes 65568 | tf_op jit(solution)/shard_map/ppermute | solution.py:17
  31.8 1.9 %collective-permute-start.3 = (bf16[2,128,128]{2,1,0:T(8,128)(2,1)S(1)}, bf16[2,128,128]{2,1,0:T(8,128)(2,1)S(1)}, u32[]{:S(2)}, u32[]{:S(2)}) collective-permute-start(bf16[2,128,128]{2,1,0:T(8,128)(2,1)S(1)} %collective-permute-done.2), channel_id=1, source_target_pairs={{0,8},{8,16},{16,24},{24,32},{32,40},{40,48},{48,56},{56,64},{64,7... | collective-permute-start | bytes 196616 | tf_op jit(solution)/shard_map/ppermute | solution.py:17
  33.7 6.3 %collective-permute-done.3 = bf16[2,128,128]{2,1,0:T(8,128)(2,1)S(1)} collective-permute-done((bf16[2,128,128]{2,1,0:T(8,128)(2,1)S(1)}, bf16[2,128,128]{2,1,0:T(8,128)(2,1)S(1)}, u32[]{:S(2)}, u32[]{:S(2)}) %collective-permute-start.3) | collective-permute-done | bytes 65568 | tf_op jit(solution)/shard_map/ppermute | solution.py:17
  40.2 24.4 %while.15 = (s32[]{:T(128)}, f32[640,1,128]{0,2,1:T(8,128)S(1)}, f32[640,1,128]{0,2,1:T(8,128)S(1)}, bf16[4,128,1,4,128]{4,1,3,2,0:T(8,128)(2,1)}, bf16[4,128,1,...) while((s32[]{:T(128)}, f32[640,1,128]{0,2,1:T(8,128)S(1)}, ...), condition=%wide.region_6.7_spmd.clone, body=%wide.region_3.6_spmd.clone.sunk | while | flops 510082048 | bytes 16575120 | solution.py:89
  41.7 0.6 log_add_fusion.2
  42.4 1.2 %fusion.70 = f32[640,1,128]{0,2,1:T(8,128)S(1)} fusion(f32[640,1,128]{0,2,1:T(8,128)S(1)} %get-tuple-element.262, pred[]{:T(512)S(6)} %compare.3, bf16[1,128,1,4,128]{1,4,3,0,2:T(8,128)(2,1)S(1)} %constant_dynamic-slice_fusion.2, f32[1,4,128,640]{3,2,1,0:T(8,128)S(1)} %get-tuple-element.243, f32[4,128]{1,0:T(4,128)} %log_add_fusion.2, ...), kind=kOutput, calls=%fused_computation.12.clone.1 | convolution fusion | flops 85032960 | bytes 2181121 | tf_op jit(solution)/shard_map/while/body/eval_jaxpr/ghqk,qghd->kgd/dot_general | solution.py:55
  44.9 1.0 %fusion.71 = bf16[4,128,1,4,128]{4,1,3,2,0:T(8,128)(2,1)} fusion(bf16[4,128,1,4,128]{4,1,3,2,0:T(8,128)(2,1)} %get-tuple-element.263, s32[]{:T(128)} %get-tuple-element.260, bf16[4,128,640]{2,1,0:T(8,128)(2,1)S(1)} %fusion.68, bf16[640,1,128]{2,0,1:T(8,128)(2,1)S(1)} %get-tuple-element.280), kind=kOutput, calls=%fused_computation.24.clone.1 | convolution fusion | flops 84017152 | bytes 950784 | tf_op jit(solution)/shard_map/while/body/eval_jaxpr/ghqk,kgd->qghd/dot_general | solution.py:50
  47.8 0.6 log_add_fusion.2
  48.5 1.2 %fusion.70 = f32[640,1,128]{0,2,1:T(8,128)S(1)} fusion(f32[640,1,128]{0,2,1:T(8,128)S(1)} %get-tuple-element.262, pred[]{:T(512)S(6)} %compare.3, bf16[1,128,1,4,128]{1,4,3,0,2:T(8,128)(2,1)S(1)} %constant_dynamic-slice_fusion.2, f32[1,4,128,640]{3,2,1,0:T(8,128)S(1)} %get-tuple-element.243, f32[4,128]{1,0:T(4,128)} %log_add_fusion.2, ...), kind=kOutput, calls=%fused_computation.12.clone.1 | convolution fusion | flops 85032960 | bytes 2181121 | tf_op jit(solution)/shard_map/while/body/eval_jaxpr/ghqk,qghd->kgd/dot_general | solution.py:55
  51.0 1.0 %fusion.71 = bf16[4,128,1,4,128]{4,1,3,2,0:T(8,128)(2,1)} fusion(bf16[4,128,1,4,128]{4,1,3,2,0:T(8,128)(2,1)} %get-tuple-element.263, s32[]{:T(128)} %get-tuple-element.260, bf16[4,128,640]{2,1,0:T(8,128)(2,1)S(1)} %fusion.68, bf16[640,1,128]{2,0,1:T(8,128)(2,1)S(1)} %get-tuple-element.280), kind=kOutput, calls=%fused_computation.24.clone.1 | convolution fusion | flops 84017152 | bytes 950784 | tf_op jit(solution)/shard_map/while/body/eval_jaxpr/ghqk,kgd->qghd/dot_general | solution.py:50
  54.6 1.2 %fusion.70 = f32[640,1,128]{0,2,1:T(8,128)S(1)} fusion(f32[640,1,128]{0,2,1:T(8,128)S(1)} %get-tuple-element.262, pred[]{:T(512)S(6)} %compare.3, bf16[1,128,1,4,128]{1,4,3,0,2:T(8,128)(2,1)S(1)} %constant_dynamic-slice_fusion.2, f32[1,4,128,640]{3,2,1,0:T(8,128)S(1)} %get-tuple-element.243, f32[4,128]{1,0:T(4,128)} %log_add_fusion.2, ...), kind=kOutput, calls=%fused_computation.12.clone.1 | convolution fusion | flops 85032960 | bytes 2181121 | tf_op jit(solution)/shard_map/while/body/eval_jaxpr/ghqk,qghd->kgd/dot_general | solution.py:55
  57.1 1.0 %fusion.71 = bf16[4,128,1,4,128]{4,1,3,2,0:T(8,128)(2,1)} fusion(bf16[4,128,1,4,128]{4,1,3,2,0:T(8,128)(2,1)} %get-tuple-element.263, s32[]{:T(128)} %get-tuple-element.260, bf16[4,128,640]{2,1,0:T(8,128)(2,1)S(1)} %fusion.68, bf16[640,1,128]{2,0,1:T(8,128)(2,1)S(1)} %get-tuple-element.280), kind=kOutput, calls=%fused_computation.24.clone.1 | convolution fusion | flops 84017152 | bytes 950784 | tf_op jit(solution)/shard_map/while/body/eval_jaxpr/ghqk,kgd->qghd/dot_general | solution.py:50
  60.7 1.2 %fusion.70 = f32[640,1,128]{0,2,1:T(8,128)S(1)} fusion(f32[640,1,128]{0,2,1:T(8,128)S(1)} %get-tuple-element.262, pred[]{:T(512)S(6)} %compare.3, bf16[1,128,1,4,128]{1,4,3,0,2:T(8,128)(2,1)S(1)} %constant_dynamic-slice_fusion.2, f32[1,4,128,640]{3,2,1,0:T(8,128)S(1)} %get-tuple-element.243, f32[4,128]{1,0:T(4,128)} %log_add_fusion.2, ...), kind=kOutput, calls=%fused_computation.12.clone.1 | convolution fusion | flops 85032960 | bytes 2181121 | tf_op jit(solution)/shard_map/while/body/eval_jaxpr/ghqk,qghd->kgd/dot_general | solution.py:55
  63.2 1.0 %fusion.71 = bf16[4,128,1,4,128]{4,1,3,2,0:T(8,128)(2,1)} fusion(bf16[4,128,1,4,128]{4,1,3,2,0:T(8,128)(2,1)} %get-tuple-element.263, s32[]{:T(128)} %get-tuple-element.260, bf16[4,128,640]{2,1,0:T(8,128)(2,1)S(1)} %fusion.68, bf16[640,1,128]{2,0,1:T(8,128)(2,1)S(1)} %get-tuple-element.280), kind=kOutput, calls=%fused_computation.24.clone.1 | convolution fusion | flops 84017152 | bytes 950784 | tf_op jit(solution)/shard_map/while/body/eval_jaxpr/ghqk,kgd->qghd/dot_general | solution.py:50
  65.0 2.1 %collective-permute-start.4 = (f32[2,128,128]{2,1,0:T(8,128)S(1)}, f32[2,128,128]{2,1,0:T(8,128)S(1)}, u32[]{:S(2)}, u32[]{:S(2)}) collective-permute-start(f32[2,128,128]{2,1,0:T(8,128)S(1)} %slice.40), channel_id=1, source_target_pairs={{8,0},{16,8},{24,16},{32,24},{40,32},{48,40},{56,48},{64,56},{72,6... | collective-permute-start | bytes 393224 | tf_op jit(solution)/shard_map/ppermute | solution.py:17
  67.1 6.1 %collective-permute-done.4 = f32[2,128,128]{2,1,0:T(8,128)S(1)} collective-permute-done((f32[2,128,128]{2,1,0:T(8,128)S(1)}, f32[2,128,128]{2,1,0:T(8,128)S(1)}, u32[]{:S(2)}, u32[]{:S(2)}) %collective-permute-start.4) | collective-permute-done | bytes 131104 | tf_op jit(solution)/shard_map/ppermute | solution.py:17
  73.1 2.9 %collective-permute-start.5 = (f32[2,128,128]{2,1,0:T(8,128)S(1)}, f32[2,128,128]{2,1,0:T(8,128)S(1)}, u32[]{:S(2)}, u32[]{:S(2)}) collective-permute-start(f32[2,128,128]{2,1,0:T(8,128)S(1)} %slice_add_fusion.3), channel_id=1, source_target_pairs={{8,0},{16,8},{24,16},{32,24},{40,32},{48,40},{56,48},{64,56},{72,6... | collective-permute-start | bytes 393224 | tf_op jit(solution)/shard_map/ppermute | solution.py:17
  76.1 4.5 %collective-permute-done.5 = f32[2,128,128]{2,1,0:T(8,128)S(1)} collective-permute-done((f32[2,128,128]{2,1,0:T(8,128)S(1)}, f32[2,128,128]{2,1,0:T(8,128)S(1)}, u32[]{:S(2)}, u32[]{:S(2)}) %collective-permute-start.5) | collective-permute-done | bytes 131104 | tf_op jit(solution)/shard_map/ppermute | solution.py:17
  80.6 4.5 %collective-permute-start.6 = (f32[2,128,128]{2,1,0:T(8,128)S(1)}, f32[2,128,128]{2,1,0:T(8,128)S(1)}, u32[]{:S(2)}, u32[]{:S(2)}) collective-permute-start(f32[2,128,128]{2,1,0:T(8,128)S(1)} %slice_add_fusion.2), channel_id=1, source_target_pairs={{8,0},{16,8},{24,16},{32,24},{40,32},{48,40},{56,48},{64,56},{72,6... | collective-permute-start | bytes 393224 | tf_op jit(solution)/shard_map/ppermute | solution.py:17
  85.0 3.6 %collective-permute-done.6 = f32[2,128,128]{2,1,0:T(8,128)S(1)} collective-permute-done((f32[2,128,128]{2,1,0:T(8,128)S(1)}, f32[2,128,128]{2,1,0:T(8,128)S(1)}, u32[]{:S(2)}, u32[]{:S(2)}) %collective-permute-start.6) | collective-permute-done | bytes 131104 | tf_op jit(solution)/shard_map/ppermute | solution.py:17
  88.7 6.5 %collective-permute-start.7 = (f32[2,128,128]{2,1,0:T(8,128)S(1)}, f32[2,128,128]{2,1,0:T(8,128)S(1)}, u32[]{:S(2)}, u32[]{:S(2)}) collective-permute-start(f32[2,128,128]{2,1,0:T(8,128)S(1)} %slice_add_fusion.1), channel_id=1, source_target_pairs={{8,0},{16,8},{24,16},{32,24},{40,32},{48,40},{56,48},{64,56},{72,6... | collective-permute-start | bytes 393224 | tf_op jit(solution)/shard_map/ppermute | solution.py:17
  95.6 1.2 %reshape.251 = bf16[128,2048]{1,0:T(8,128)(2,1)} reshape(bf16[128,1,4,4,128]{4,3,2,0,1:T(4,128)(2,1)S(1)} %copy.31) | data formatting | bytes 1048576 | tf_op jit(solution)/shard_map/reshape | solution.py:90
  96.8 0.9 collective-permute-done.7
  97.7 0.6 slice_bitcast_fusion.2
  (172 shorter events, 15.0 us)
Async XLA Ops:
  0.6 7.0 %copy-start.2 = (bf16[128,2048]{1,0:T(8,128)(2,1)S(1)}, bf16[128,2048]{1,0:T(8,128)(2,1)}, u32[]{:S(2)}) copy-start(bf16[128,2048]{1,0:T(8,128)(2,1)} %param.10) | copy-start | bytes 1572868
  1.5 13.8 %collective-permute-start = (bf16[2,128,128]{2,1,0:T(8,128)(2,1)S(1)}, bf16[2,128,128]{2,1,0:T(8,128)(2,1)S(1)}, u32[]{:S(2)}, u32[]{:S(2)}) collective-permute-start(bf16[2,128,128]{2,1,0:T(8,128)(2,1)S(1)} %pad_maximum_fusion), channel_id=1, source_target_pairs={{0,8},{8,16},{16,24},{24,32},{32,40},{40,48},{48,56},{56,64},{64,7... | collective-permute-start | bytes 196616 | tf_op jit(solution)/shard_map/ppermute | solution.py:17
  6.3 33.9 %copy-start.9 = (bf16[128,128]{1,0:T(8,128)(2,1)S(1)}, bf16[128,128]{1,0:T(8,128)(2,1)}, u32[]{:S(2)}) copy-start(bf16[128,128]{1,0:T(8,128)(2,1)} %param.9) | copy-start | bytes 98308
  6.3 33.9 %copy-start.10 = (bf16[128,128]{1,0:T(8,128)(2,1)S(1)}, bf16[128,128]{1,0:T(8,128)(2,1)}, u32[]{:S(2)}) copy-start(bf16[128,128]{1,0:T(8,128)(2,1)} %param.8) | copy-start | bytes 98308
  15.3 8.3 %collective-permute-start.1 = (bf16[2,128,128]{2,1,0:T(8,128)(2,1)S(1)}, bf16[2,128,128]{2,1,0:T(8,128)(2,1)S(1)}, u32[]{:S(2)}, u32[]{:S(2)}) collective-permute-start(bf16[2,128,128]{2,1,0:T(8,128)(2,1)S(1)} %collective-permute-done), channel_id=1, source_target_pairs={{0,8},{8,16},{16,24},{24,32},{32,40},{40,48},{48,56},{56,64},{64,7... | collective-permute-start | bytes 196616 | tf_op jit(solution)/shard_map/ppermute | solution.py:17
  23.5 8.3 %collective-permute-start.2 = (bf16[2,128,128]{2,1,0:T(8,128)(2,1)S(1)}, bf16[2,128,128]{2,1,0:T(8,128)(2,1)S(1)}, u32[]{:S(2)}, u32[]{:S(2)}) collective-permute-start(bf16[2,128,128]{2,1,0:T(8,128)(2,1)S(1)} %collective-permute-done.1), channel_id=1, source_target_pairs={{0,8},{8,16},{16,24},{24,32},{32,40},{40,48},{48,56},{56,64},{64,7... | collective-permute-start | bytes 196616 | tf_op jit(solution)/shard_map/ppermute | solution.py:17
  31.8 8.3 %collective-permute-start.3 = (bf16[2,128,128]{2,1,0:T(8,128)(2,1)S(1)}, bf16[2,128,128]{2,1,0:T(8,128)(2,1)S(1)}, u32[]{:S(2)}, u32[]{:S(2)}) collective-permute-start(bf16[2,128,128]{2,1,0:T(8,128)(2,1)S(1)} %collective-permute-done.2), channel_id=1, source_target_pairs={{0,8},{8,16},{16,24},{24,32},{32,40},{40,48},{48,56},{56,64},{64,7... | collective-permute-start | bytes 196616 | tf_op jit(solution)/shard_map/ppermute | solution.py:17
  40.3 2.1 %copy-start = (bf16[4,128,1,4,128]{1,4,3,0,2:T(8,128)(2,1)}, bf16[4,128,1,4,128]{1,4,3,0,2:T(8,128)(2,1)S(1)}, u32[]{:S(2)}) copy-start(bf16[4,128,1,4,128]{1,4,3,0,2:T(8,128)(2,1)S(1)} %get-tuple-element.281) | copy-start | bytes 1572868 | tf_op jit(solution)/shard_map/while
  42.4 1.4 %copy-start.4 = (f32[4,128]{1,0:T(4,128)S(1)}, f32[4,128]{1,0:T(4,128)}, u32[]{:S(2)}) copy-start(f32[4,128]{1,0:T(4,128)} %log_add_fusion.2) | copy-start | bytes 6148 | tf_op jit(solution)/shard_map/while
  44.8 1.4 %copy-start.1 = (bf16[4,128,1,4,128]{1,4,3,0,2:T(8,128)(2,1)S(1)}, bf16[4,128,1,4,128]{1,4,3,0,2:T(8,128)(2,1)}, u32[]{:S(2)}) copy-start(bf16[4,128,1,4,128]{1,4,3,0,2:T(8,128)(2,1)} %copy-done) | copy-start | bytes 1572868 | tf_op jit(solution)/shard_map/while
  44.9 1.4 %copy-start.6 = (s32[640]{0:T(1024)S(1)}, s32[640]{0:T(1024)}, u32[]{:S(2)}) copy-start(s32[640]{0:T(1024)} %copy-done.5) | copy-start | bytes 7684 | tf_op jit(solution)/shard_map/while
  44.9 1.4 %copy-start.8 = (s32[640]{0:T(1024)S(1)}, s32[640]{0:T(1024)}, u32[]{:S(2)}) copy-start(s32[640]{0:T(1024)} %copy-done.7) | copy-start | bytes 7684 | tf_op jit(solution)/shard_map/while
  46.4 2.1 %copy-start = (bf16[4,128,1,4,128]{1,4,3,0,2:T(8,128)(2,1)}, bf16[4,128,1,4,128]{1,4,3,0,2:T(8,128)(2,1)S(1)}, u32[]{:S(2)}) copy-start(bf16[4,128,1,4,128]{1,4,3,0,2:T(8,128)(2,1)S(1)} %get-tuple-element.281) | copy-start | bytes 1572868 | tf_op jit(solution)/shard_map/while
  48.5 1.4 %copy-start.4 = (f32[4,128]{1,0:T(4,128)S(1)}, f32[4,128]{1,0:T(4,128)}, u32[]{:S(2)}) copy-start(f32[4,128]{1,0:T(4,128)} %log_add_fusion.2) | copy-start | bytes 6148 | tf_op jit(solution)/shard_map/while
  50.9 1.4 %copy-start.1 = (bf16[4,128,1,4,128]{1,4,3,0,2:T(8,128)(2,1)S(1)}, bf16[4,128,1,4,128]{1,4,3,0,2:T(8,128)(2,1)}, u32[]{:S(2)}) copy-start(bf16[4,128,1,4,128]{1,4,3,0,2:T(8,128)(2,1)} %copy-done) | copy-start | bytes 1572868 | tf_op jit(solution)/shard_map/while
  51.0 1.4 %copy-start.6 = (s32[640]{0:T(1024)S(1)}, s32[640]{0:T(1024)}, u32[]{:S(2)}) copy-start(s32[640]{0:T(1024)} %copy-done.5) | copy-start | bytes 7684 | tf_op jit(solution)/shard_map/while
  51.0 1.4 %copy-start.8 = (s32[640]{0:T(1024)S(1)}, s32[640]{0:T(1024)}, u32[]{:S(2)}) copy-start(s32[640]{0:T(1024)} %copy-done.7) | copy-start | bytes 7684 | tf_op jit(solution)/shard_map/while
  52.5 2.1 %copy-start = (bf16[4,128,1,4,128]{1,4,3,0,2:T(8,128)(2,1)}, bf16[4,128,1,4,128]{1,4,3,0,2:T(8,128)(2,1)S(1)}, u32[]{:S(2)}) copy-start(bf16[4,128,1,4,128]{1,4,3,0,2:T(8,128)(2,1)S(1)} %get-tuple-element.281) | copy-start | bytes 1572868 | tf_op jit(solution)/shard_map/while
  54.5 1.4 %copy-start.4 = (f32[4,128]{1,0:T(4,128)S(1)}, f32[4,128]{1,0:T(4,128)}, u32[]{:S(2)}) copy-start(f32[4,128]{1,0:T(4,128)} %log_add_fusion.2) | copy-start | bytes 6148 | tf_op jit(solution)/shard_map/while
  57.0 1.4 %copy-start.1 = (bf16[4,128,1,4,128]{1,4,3,0,2:T(8,128)(2,1)S(1)}, bf16[4,128,1,4,128]{1,4,3,0,2:T(8,128)(2,1)}, u32[]{:S(2)}) copy-start(bf16[4,128,1,4,128]{1,4,3,0,2:T(8,128)(2,1)} %copy-done) | copy-start | bytes 1572868 | tf_op jit(solution)/shard_map/while
  57.1 1.4 %copy-start.6 = (s32[640]{0:T(1024)S(1)}, s32[640]{0:T(1024)}, u32[]{:S(2)}) copy-start(s32[640]{0:T(1024)} %copy-done.5) | copy-start | bytes 7684 | tf_op jit(solution)/shard_map/while
  57.1 1.4 %copy-start.8 = (s32[640]{0:T(1024)S(1)}, s32[640]{0:T(1024)}, u32[]{:S(2)}) copy-start(s32[640]{0:T(1024)} %copy-done.7) | copy-start | bytes 7684 | tf_op jit(solution)/shard_map/while
  58.6 2.1 %copy-start = (bf16[4,128,1,4,128]{1,4,3,0,2:T(8,128)(2,1)}, bf16[4,128,1,4,128]{1,4,3,0,2:T(8,128)(2,1)S(1)}, u32[]{:S(2)}) copy-start(bf16[4,128,1,4,128]{1,4,3,0,2:T(8,128)(2,1)S(1)} %get-tuple-element.281) | copy-start | bytes 1572868 | tf_op jit(solution)/shard_map/while
  60.6 1.4 %copy-start.4 = (f32[4,128]{1,0:T(4,128)S(1)}, f32[4,128]{1,0:T(4,128)}, u32[]{:S(2)}) copy-start(f32[4,128]{1,0:T(4,128)} %log_add_fusion.2) | copy-start | bytes 6148 | tf_op jit(solution)/shard_map/while
  63.1 1.4 %copy-start.1 = (bf16[4,128,1,4,128]{1,4,3,0,2:T(8,128)(2,1)S(1)}, bf16[4,128,1,4,128]{1,4,3,0,2:T(8,128)(2,1)}, u32[]{:S(2)}) copy-start(bf16[4,128,1,4,128]{1,4,3,0,2:T(8,128)(2,1)} %copy-done) | copy-start | bytes 1572868 | tf_op jit(solution)/shard_map/while
  63.1 1.4 %copy-start.6 = (s32[640]{0:T(1024)S(1)}, s32[640]{0:T(1024)}, u32[]{:S(2)}) copy-start(s32[640]{0:T(1024)} %copy-done.5) | copy-start | bytes 7684 | tf_op jit(solution)/shard_map/while
  63.2 1.4 %copy-start.8 = (s32[640]{0:T(1024)S(1)}, s32[640]{0:T(1024)}, u32[]{:S(2)}) copy-start(s32[640]{0:T(1024)} %copy-done.7) | copy-start | bytes 7684 | tf_op jit(solution)/shard_map/while
  64.9 30.2 %copy-start.3 = (bf16[4,128,1,4,128]{4,1,3,2,0:T(8,128)(2,1)S(1)}, bf16[4,128,1,4,128]{4,1,3,2,0:T(8,128)(2,1)}, u32[]{:S(2)}) copy-start(bf16[4,128,1,4,128]{4,1,3,2,0:T(8,128)(2,1)} %get-tuple-element.52) | copy-start | bytes 1572868
  65.0 8.1 %collective-permute-start.4 = (f32[2,128,128]{2,1,0:T(8,128)S(1)}, f32[2,128,128]{2,1,0:T(8,128)S(1)}, u32[]{:S(2)}, u32[]{:S(2)}) collective-permute-start(f32[2,128,128]{2,1,0:T(8,128)S(1)} %slice.40), channel_id=1, source_target_pairs={{8,0},{16,8},{24,16},{32,24},{40,32},{48,40},{56,48},{64,56},{72,6... | collective-permute-start | bytes 393224 | tf_op jit(solution)/shard_map/ppermute | solution.py:17
  73.1 7.4 %collective-permute-start.5 = (f32[2,128,128]{2,1,0:T(8,128)S(1)}, f32[2,128,128]{2,1,0:T(8,128)S(1)}, u32[]{:S(2)}, u32[]{:S(2)}) collective-permute-start(f32[2,128,128]{2,1,0:T(8,128)S(1)} %slice_add_fusion.3), channel_id=1, source_target_pairs={{8,0},{16,8},{24,16},{32,24},{40,32},{48,40},{56,48},{64,56},{72,6... | collective-permute-start | bytes 393224 | tf_op jit(solution)/shard_map/ppermute | solution.py:17
  80.6 8.1 %collective-permute-start.6 = (f32[2,128,128]{2,1,0:T(8,128)S(1)}, f32[2,128,128]{2,1,0:T(8,128)S(1)}, u32[]{:S(2)}, u32[]{:S(2)}) collective-permute-start(f32[2,128,128]{2,1,0:T(8,128)S(1)} %slice_add_fusion.2), channel_id=1, source_target_pairs={{8,0},{16,8},{24,16},{32,24},{40,32},{48,40},{56,48},{64,56},{72,6... | collective-permute-start | bytes 393224 | tf_op jit(solution)/shard_map/ppermute | solution.py:17
  88.7 9.0 %collective-permute-start.7 = (f32[2,128,128]{2,1,0:T(8,128)S(1)}, f32[2,128,128]{2,1,0:T(8,128)S(1)}, u32[]{:S(2)}, u32[]{:S(2)}) collective-permute-start(f32[2,128,128]{2,1,0:T(8,128)S(1)} %slice_add_fusion.1), channel_id=1, source_target_pairs={{8,0},{16,8},{24,16},{32,24},{40,32},{48,40},{56,48},{64,56},{72,6... | collective-permute-start | bytes 393224 | tf_op jit(solution)/shard_map/ppermute | solution.py:17
  (32 other events, 28.3 us)
where the time goes:
time: 98.8 us; the launch traced here: 98.3 us
  waiting for transfers between devices  41.2 us (42%)
  starting transfers between devices  25.5 us (26%)
  matrix products  16.5 us (17%)
  local copies, waits for them, and re-layouts  7.3 us (7%)
  other arithmetic  5.99 us (6%)
    ppermute x8, waiting for transfers between devices, passed_along(): return lax.ppermute(array, axis, pairs)  41.2 us
    ppermute x8, starting transfers between devices, passed_along(): return lax.ppermute(array, axis, pairs)  25.5 us
    dot_general x4, matrix products, attend(): jnp.einsum('ghqk,qghd->kgd', probs_b, grad_blk, preferred_element_type=jn...  4.94 us
    dot_general x4, matrix products, attend(): jnp.einsum('ghqk,kgd->qghd', dscore, key_win, preferred_element_type=jnp....  4 us
    add x4, other arithmetic, attend(): lse = peak + jnp.log(total)  2.37 us
    dot_general x4, matrix products, attend(): jnp.einsum('qghd,kgd->ghqk', grad_blk, value_win, preferred_element_type=...  2.22 us
    dot_general x4, matrix products, attend(): jnp.einsum('ghqk,kgd->qghd', probs_b, value_win, preferred_element_type=j...  2.1 us
    dot_general x4, matrix products, attend(): jnp.einsum('qghd,kgd->ghqk', query_blk, key_win, preferred_element_type=j...  2.03 us
  transfers between devices with their start and end apart: 8, of which 8 were waited for; matrix products, arithmetic and copies ran while one was open for 4% of the time, Pallas kernels for 0%

commit v1 on v0

v1 whole, which is shorter than its diff:
```python
import math

import jax
import jax.numpy as jnp
from jax import lax
from jax.experimental import pallas as pl
from jax.experimental.pallas import tpu as pltpu
from jax.sharding import PartitionSpec as P

HEADS = 128
KV_HEADS = 8
HEAD_DIM = 128
REACH = 4
TOK = 128
GROUP = HEADS // KV_HEADS
PAIR = 2
WIDE = PAIR * TOK
DOCS = 32
F32 = jnp.float32
BF16 = jnp.bfloat16
NT = (((1,), (1,)), ((), ()))
NN = (((1,), (0,)), ((), ()))


def dot(a, b, dims):
    return lax.dot_general(a, b, dims, preferred_element_type=F32)


def doc_starts(lengths_ref, row):
    total = jnp.int32(0)
    starts = jnp.zeros_like(row)
    for doc in range(DOCS):
        total = total + lengths_ref[doc]
        starts = jnp.where(total <= row, total, starts)
    return starts


def attend_kernel(
    index_ref,
    lengths_ref,
    query_ref,
    grad_ref,
    own_ref,
    one_ref,
    two_ref,
    three_ref,
    four_ref,
    grad_query_ref,
    own_out_ref,
    one_out_ref,
    two_out_ref,
    three_out_ref,
    four_out_ref,
    key_ref,
    key_t_ref,
    value_ref,
    bias_ref,
    key_acc_ref,
    value_acc_ref,
):
    scale = 1.0 / math.sqrt(HEAD_DIM)
    window = (three_ref, two_ref, one_ref, own_ref, four_ref)
    for at, block in enumerate(window):
        rows = slice(at * TOK, (at + 1) * TOK)
        key_ref[rows, :] = block[:, :HEAD_DIM]
        value_ref[rows, :] = block[:, HEAD_DIM:]
    key_t_ref[...] = key_ref[...].T

    first = index_ref[0] * TOK
    query_pos = first + lax.broadcasted_iota(jnp.int32, (1, TOK), 1)
    starts = doc_starts(lengths_ref, query_pos)
    lane = lax.broadcasted_iota(jnp.int32, (TOK, TOK), 1)
    row = lax.broadcasted_iota(jnp.int32, (TOK, TOK), 0)
    own_side = row <= lane
    for at, back in enumerate((3, 2, 1, 0)):
        key_pos = first - back * TOK + row
        if back == 0:
            key_pos = jnp.where(own_side, key_pos, key_pos - REACH * TOK)
        bias_ref[at * TOK : (at + 1) * TOK, :] = jnp.where(key_pos >= starts, 0.0, -1e30)
    own_wide = jnp.concatenate([own_side] * PAIR, axis=1)
    split = 3 * TOK

    key_acc_ref[...] = jnp.zeros_like(key_acc_ref)
    value_acc_ref[...] = jnp.zeros_like(value_acc_ref)

    def merged(scores):
        own = jnp.where(own_wide, scores[split : split + TOK], scores[split + TOK :])
        return jnp.concatenate([scores[:split], own], axis=0)

    def parted(blocks):
        own = blocks[split:]
        zero = jnp.zeros_like(own)
        return jnp.concatenate(
            [blocks[:split], jnp.where(own_wide, own, zero), jnp.where(own_wide, zero, own)], axis=0
        )

    def turn(step):
        heads = [pl.ds(pl.multiple_of((step * PAIR + h) * HEAD_DIM, HEAD_DIM), HEAD_DIM) for h in range(PAIR)]
        query = jnp.concatenate([query_ref[:, head] for head in heads], axis=0)
        grad = jnp.concatenate([grad_ref[:, head] for head in heads], axis=0)
        bias = jnp.concatenate([bias_ref[...]] * PAIR, axis=1)
        scores = merged(dot(key_ref[...], query, NT)) * (scale * math.log2(math.e)) + bias
        dprobs = merged(dot(value_ref[...], grad, NT))
        peak = jnp.max(scores, axis=0, keepdims=True)
        weights = jnp.exp2(scores - peak)
        inverse = 1.0 / jnp.sum(weights, axis=0, keepdims=True)
        delta = jnp.sum(weights * dprobs, axis=0, keepdims=True) * inverse
        probs = weights * inverse
        dscore = parted(probs * (dprobs - delta)).astype(BF16)
        probs = parted(probs).astype(BF16)
        value_acc_ref[...] += dot(probs, grad, NN)
        key_acc_ref[...] += dot(dscore, query, NN)
        grad_query = (dot(key_t_ref[...], dscore, NN) * scale).T.astype(BF16)
        for h, head in enumerate(heads):
            grad_query_ref[:, head] = grad_query[h * TOK : (h + 1) * TOK]

    for step in range(GROUP // PAIR):
        turn(step)

    outs = (three_out_ref, two_out_ref, one_out_ref, own_out_ref, four_out_ref)
    for at, out in enumerate(outs):
        rows = slice(at * TOK, (at + 1) * TOK)
        out[:, :HEAD_DIM] = (key_acc_ref[rows, :] * scale).astype(out.dtype)
        out[:, HEAD_DIM:] = value_acc_ref[rows, :].astype(out.dtype)


def attend(index, lengths, queries, grad_out, blocks):
    whole = pl.BlockSpec(memory_space=pltpu.VMEM)
    scalars = pl.BlockSpec(memory_space=pltpu.SMEM)
    both = (TOK, 2 * HEAD_DIM)
    width = (REACH + 1) * TOK
    return pl.pallas_call(
        attend_kernel,
        out_shape=(
            jax.ShapeDtypeStruct(queries.shape, BF16),
            jax.ShapeDtypeStruct(both, F32),
            *(jax.ShapeDtypeStruct(both, BF16) for _ in range(REACH)),
        ),
        in_specs=[scalars] * 2 + [whole] * (3 + REACH),
        out_specs=[whole] * (2 + REACH),
        scratch_shapes=[
            pltpu.VMEM((width, HEAD_DIM), BF16),
            pltpu.VMEM((HEAD_DIM, width), BF16),
            pltpu.VMEM((width, HEAD_DIM), BF16),
            pltpu.VMEM((REACH * TOK, TOK), F32),
            pltpu.VMEM((width, HEAD_DIM), F32),
            pltpu.VMEM((width, HEAD_DIM), F32),
        ],
        compiler_params=pltpu.CompilerParams(vmem_limit_bytes=32 * 1024 * 1024),
        cost_estimate=pl.CostEstimate(flops=2 * 10**9, bytes_accessed=2 * 10**6, transcendentals=10**6),
        name="attend",
    )(index, lengths, queries, grad_out, *blocks)


def passed_along(array, by):
    devices = lax.axis_size("ctx")
    pairs = [(i, i + by) for i in range(devices) if 0 <= i + by < devices]
    return lax.ppermute(array, "ctx", pairs)


def local(queries, keys, values, grad_out, doc_lengths):
    index = lax.axis_index("ctx").astype(jnp.int32).reshape(1)
    own = jnp.concatenate([keys, values], axis=1)
    blocks = [own] + [passed_along(own, by) for by in range(1, REACH + 1)]
    grad_q, mine, *shares = attend(index, doc_lengths, queries, grad_out, blocks)
    total = mine
    for by, share in enumerate(shares, 1):
        total = total + passed_along(share, -by).astype(F32)
    total = total.astype(BF16)
    return (grad_q, total[:, :HEAD_DIM], total[:, HEAD_DIM:])


def solution(mesh):
    placed = (P("ctx", "tp"), P("ctx", "tp"), P("ctx", "tp"), P("ctx", "tp"), P())
    return jax.shard_map(
        local,
        mesh=mesh,
        in_specs=placed,
        out_specs=(P("ctx", "tp"), P("ctx", "tp"), P("ctx", "tp")),
        check_vma=False,
    )
```

time: 98.8 us -> 63.6 us (0.64)
  waiting for transfers between devices: 41.2 us -> 12.3 us
  matrix products: 16.5 us -> 0 us
  starting transfers between devices: 25.5 us -> 39.8 us
  Pallas kernels: 0 us -> 6.8 us
  other arithmetic: 5.99 us -> 0.05 us
  local copies, waits for them, and re-layouts: 7.3 us -> 3.51 us
    ppermute x8, waiting for transfers between devices: 41.2 us -> 12.3 us  [passed_along(): return lax.ppermute(array, 'ctx', pairs)]
    dot_general x24 -> x0, matrix products: 16.5 us -> none  [the longest x4 4.94 us: attend(): jnp.einsum('ghqk,qghd->kgd', probs_b, grad_blk, preferred_element_type=jn...]
    ppermute x8, starting transfers between devices: 25.5 us -> 39.8 us  [passed_along(): return lax.ppermute(array, 'ctx', pairs)]
    pallas_call x0 -> x1, Pallas kernels: none -> 6.8 us  [attend(): pl.pallas_call(attend_kernel, out_shape=(jax.ShapeDtypeStruct(queries.sha...]
    add x9 -> x0, other arithmetic: 2.44 us -> none  [the longest x4 2.37 us: attend(): lse = peak + jnp.log(total)]
    while x106 -> x0, local copies, waits for them, and re-layouts: 2.09 us -> none
    reduce_sum x6 -> x0, other arithmetic: 1.83 us -> none  [the longest x4 1.65 us: attend(): jnp.sum(jnp.where(mask, jnp.exp(scores - peak), 0.0), axis=-1, keepdims=T...]
    unnamed x14 -> x9, local copies, waits for them, and re-layouts: 1.66 us -> 2.86 us
  transfers between devices with their start and end apart: 8 -> 8, of which waited for: 8 -> 3; matrix products, arithmetic and copies ran while one was open for 4% -> 0% of each run, Pallas kernels for 0% -> 0%
where the time goes in v1:
time: 63.6 us; the launch traced here: 63.2 us
  starting transfers between devices  39.8 us (63%)
  waiting for transfers between devices  12.3 us (19%)
  Pallas kernels  6.8 us (11%)
  local copies, waits for them, and re-layouts  3.51 us (6%)
  between operations  0.77 us (1%)
    ppermute x8, starting transfers between devices, passed_along(): return lax.ppermute(array, 'ctx', pairs)  39.8 us
    ppermute x8, waiting for transfers between devices, passed_along(): return lax.ppermute(array, 'ctx', pairs)  12.3 us
    pallas_call x1, Pallas kernels, attend(): pl.pallas_call(attend_kernel, out_shape=(jax.ShapeDtypeStruct(queries.sha...  6.8 us
    unnamed x9, local copies, waits for them, and re-layouts  2.86 us
  transfers between devices with their start and end apart: 8, of which 3 were waited for; matrix products, arithmetic and copies ran while one was open for 0% of the time, Pallas kernels for 0%

profile of v1, /device:TPU:24, one launch (start us, length us, event | category | flops | bytes accessed | tf_op | source)
XLA Modules:
  0.0 63.2 jit_solution(4242942324087139588)
XLA Ops:
  0.6 0.0 copy-start.3
  0.6 0.8 %constant_dynamic-update-slice_fusion.1 = bf16[128,256]{1,0:T(8,128)(2,1)S(1)} fusion(bf16[128,128]{1,0:T(8,128)(2,1)} %param.6), kind=kLoop, calls=%fused_computation.2 | loop fusion | bytes 65536
  1.4 0.0 copy-done.3
  1.4 9.1 %collective-permute-start.3 = (bf16[128,256]{1,0:T(8,128)(2,1)S(1)}, bf16[128,256]{1,0:T(8,128)(2,1)S(1)}, u32[]{:S(2)}, u32[]{:S(2)}) collective-permute-start(bf16[128,256]{1,0:T(8,128)(2,1)S(1)} %constant_dynamic-update-slice_fusion.own_ref), channel_id=1, source_target_pairs={{0,32},{8,40},{16,48},{24,56},{32,64},{40,72},{48,80},{56,88},{64,... | collective-permute-start | bytes 196616 | tf_op jit(solution)/shard_map/ppermute | solution.py:158
  10.5 6.5 %collective-permute-start.2 = (bf16[128,256]{1,0:T(8,128)(2,1)S(1)}, bf16[128,256]{1,0:T(8,128)(2,1)S(1)}, u32[]{:S(2)}, u32[]{:S(2)}) collective-permute-start(bf16[128,256]{1,0:T(8,128)(2,1)S(1)} %constant_dynamic-update-slice_fusion.own_ref), channel_id=1, source_target_pairs={{0,24},{8,32},{16,40},{24,48},{32,56},{40,64},{48,72},{56,80},{64,... | collective-permute-start | bytes 196616 | tf_op jit(solution)/shard_map/ppermute | solution.py:158
  17.1 5.5 %collective-permute-start.1 = (bf16[128,256]{1,0:T(8,128)(2,1)S(1)}, bf16[128,256]{1,0:T(8,128)(2,1)S(1)}, u32[]{:S(2)}, u32[]{:S(2)}) collective-permute-start(bf16[128,256]{1,0:T(8,128)(2,1)S(1)} %constant_dynamic-update-slice_fusion.own_ref), channel_id=1, source_target_pairs={{0,16},{8,24},{16,32},{24,40},{32,48},{40,56},{48,64},{56,72},{64,... | collective-permute-start | bytes 196616 | tf_op jit(solution)/shard_map/ppermute | solution.py:158
  22.6 2.9 %collective-permute-start = (bf16[128,256]{1,0:T(8,128)(2,1)S(1)}, bf16[128,256]{1,0:T(8,128)(2,1)S(1)}, u32[]{:S(2)}, u32[]{:S(2)}) collective-permute-start(bf16[128,256]{1,0:T(8,128)(2,1)S(1)} %constant_dynamic-update-slice_fusion.own_ref), channel_id=1, source_target_pairs={{0,8},{8,16},{16,24},{24,32},{32,40},{40,48},{48,56},{56,64},{64,7... | collective-permute-start | bytes 196616 | tf_op jit(solution)/shard_map/ppermute | solution.py:158
  25.5 0.0 copy-start.2
  25.5 0.0 collective-permute-done.3.four_ref
  25.5 0.0 collective-permute-done.2.three_ref
  25.6 1.3 %collective-permute-done.1.two_ref = bf16[128,256]{1,0:T(8,128)(2,1)S(1)} collective-permute-done((bf16[128,256]{1,0:T(8,128)(2,1)S(1)}, bf16[128,256]{1,0:T(8,128)(2,1)S(1)}, u32[]{:S(2)}, u32[]{:S(2)}) %collective-permute-start.1) | collective-permute-done | bytes 65568 | tf_op jit(solution)/shard_map/ppermute | solution.py:158
  26.9 4.0 %collective-permute-done.one_ref = bf16[128,256]{1,0:T(8,128)(2,1)S(1)} collective-permute-done((bf16[128,256]{1,0:T(8,128)(2,1)S(1)}, bf16[128,256]{1,0:T(8,128)(2,1)S(1)}, u32[]{:S(2)}, u32[]{:S(2)}) %collective-permute-start) | collective-permute-done | bytes 65568 | tf_op jit(solution)/shard_map/ppermute | solution.py:158
  30.8 0.0 copy-done.2
  30.9 0.0 copy-start
  30.9 1.0 %copy-done = bf16[128,2048]{1,0:T(8,128)(2,1)S(1)} copy-done((bf16[128,2048]{1,0:T(8,128)(2,1)S(1)}, bf16[128,2048]{1,0:T(8,128)(2,1)}, u32[]{:S(2)}) %copy-start) | copy-done | bytes 524312
  31.9 0.0 copy-start.1
  31.9 1.0 %copy-done.1 = bf16[128,2048]{1,0:T(8,128)(2,1)S(1)} copy-done((bf16[128,2048]{1,0:T(8,128)(2,1)S(1)}, bf16[128,2048]{1,0:T(8,128)(2,1)}, u32[]{:S(2)}) %copy-start.1) | copy-done | bytes 524312
  32.9 6.8 %attend.1 = (bf16[128,2048]{1,0:T(8,128)(2,1)}, f32[128,256]{1,0:T(8,128)S(1)}, bf16[128,256]{1,0:T(8,128)(2,1)S(1)}, bf16[128,256]{1,0:T(8,128)(2,1)S(1)}, bf16...) custom-call(s32[1]{0:T(128)} %bitcast.index_ref, s32[32]{0:T(128)S(1)} %copy-done.2, ...), custom_call_target="tpu_custom_call" | custom-call | flops 2000000000 | bytes 2000000 | tf_op jit(solution)/shard_map/attend/pallas_call | solution.py:132
  39.7 2.9 %collective-permute-start.4 = (bf16[128,256]{1,0:T(8,128)(2,1)S(1)}, bf16[128,256]{1,0:T(8,128)(2,1)S(1)}, u32[]{:S(2)}, u32[]{:S(2)}) collective-permute-start(bf16[128,256]{1,0:T(8,128)(2,1)S(1)} %get-tuple-element.11), channel_id=1, source_target_pairs={{8,0},{16,8},{24,16},{32,24},{40,32},{48,40},{56,48},{64,56},{72,6... | collective-permute-start | bytes 196616 | tf_op jit(solution)/shard_map/ppermute | solution.py:158
  42.6 3.1 %collective-permute-start.5 = (bf16[128,256]{1,0:T(8,128)(2,1)S(1)}, bf16[128,256]{1,0:T(8,128)(2,1)S(1)}, u32[]{:S(2)}, u32[]{:S(2)}) collective-permute-start(bf16[128,256]{1,0:T(8,128)(2,1)S(1)} %get-tuple-element.12), channel_id=1, source_target_pairs={{16,0},{24,8},{32,16},{40,24},{48,32},{56,40},{64,48},{72,56},{80,... | collective-permute-start | bytes 196616 | tf_op jit(solution)/shard_map/ppermute | solution.py:158
  45.7 4.4 %collective-permute-start.6 = (bf16[128,256]{1,0:T(8,128)(2,1)S(1)}, bf16[128,256]{1,0:T(8,128)(2,1)S(1)}, u32[]{:S(2)}, u32[]{:S(2)}) collective-permute-start(bf16[128,256]{1,0:T(8,128)(2,1)S(1)} %get-tuple-element.13), channel_id=1, source_target_pairs={{24,0},{32,8},{40,16},{48,24},{56,32},{64,40},{72,48},{80,56},{88,... | collective-permute-start | bytes 196616 | tf_op jit(solution)/shard_map/ppermute | solution.py:158
  50.1 5.4 %collective-permute-start.7 = (bf16[128,256]{1,0:T(8,128)(2,1)S(1)}, bf16[128,256]{1,0:T(8,128)(2,1)S(1)}, u32[]{:S(2)}, u32[]{:S(2)}) collective-permute-start(bf16[128,256]{1,0:T(8,128)(2,1)S(1)} %get-tuple-element.14), channel_id=1, source_target_pairs={{32,0},{40,8},{48,16},{56,24},{64,32},{72,40},{80,48},{88,56},{96,... | collective-permute-start | bytes 196616 | tf_op jit(solution)/shard_map/ppermute | solution.py:158
  55.5 0.0 collective-permute-done.4
  55.5 0.0 collective-permute-done.5
  55.5 0.0 collective-permute-done.6
  55.5 7.0 %collective-permute-done.7 = bf16[128,256]{1,0:T(8,128)(2,1)S(1)} collective-permute-done((bf16[128,256]{1,0:T(8,128)(2,1)S(1)}, bf16[128,256]{1,0:T(8,128)(2,1)S(1)}, u32[]{:S(2)}, u32[]{:S(2)}) %collective-permute-start.7) | collective-permute-done | bytes 65568 | tf_op jit(solution)/shard_map/ppermute | solution.py:158
  62.5 0.6 fusion
  (2 shorter events, 0.1 us)
Async XLA Ops:
  0.6 0.8 %copy-start.3 = (bf16[128,128]{1,0:T(8,128)(2,1)S(1)}, bf16[128,128]{1,0:T(8,128)(2,1)}, u32[]{:S(2)}) copy-start(bf16[128,128]{1,0:T(8,128)(2,1)} %param.7) | copy-start | bytes 98308
  1.4 24.1 %collective-permute-start.3 = (bf16[128,256]{1,0:T(8,128)(2,1)S(1)}, bf16[128,256]{1,0:T(8,128)(2,1)S(1)}, u32[]{:S(2)}, u32[]{:S(2)}) collective-permute-start(bf16[128,256]{1,0:T(8,128)(2,1)S(1)} %constant_dynamic-update-slice_fusion.own_ref), channel_id=1, source_target_pairs={{0,32},{8,40},{16,48},{24,56},{32,64},{40,72},{48,80},{56,88},{64,... | collective-permute-start | bytes 196616 | tf_op jit(solution)/shard_map/ppermute | solution.py:158
  10.5 15.0 %collective-permute-start.2 = (bf16[128,256]{1,0:T(8,128)(2,1)S(1)}, bf16[128,256]{1,0:T(8,128)(2,1)S(1)}, u32[]{:S(2)}, u32[]{:S(2)}) collective-permute-start(bf16[128,256]{1,0:T(8,128)(2,1)S(1)} %constant_dynamic-update-slice_fusion.own_ref), channel_id=1, source_target_pairs={{0,24},{8,32},{16,40},{24,48},{32,56},{40,64},{48,72},{56,80},{64,... | collective-permute-start | bytes 196616 | tf_op jit(solution)/shard_map/ppermute | solution.py:158
  17.1 9.8 %collective-permute-start.1 = (bf16[128,256]{1,0:T(8,128)(2,1)S(1)}, bf16[128,256]{1,0:T(8,128)(2,1)S(1)}, u32[]{:S(2)}, u32[]{:S(2)}) collective-permute-start(bf16[128,256]{1,0:T(8,128)(2,1)S(1)} %constant_dynamic-update-slice_fusion.own_ref), channel_id=1, source_target_pairs={{0,16},{8,24},{16,32},{24,40},{32,48},{40,56},{48,64},{56,72},{64,... | collective-permute-start | bytes 196616 | tf_op jit(solution)/shard_map/ppermute | solution.py:158
  22.6 8.3 %collective-permute-start = (bf16[128,256]{1,0:T(8,128)(2,1)S(1)}, bf16[128,256]{1,0:T(8,128)(2,1)S(1)}, u32[]{:S(2)}, u32[]{:S(2)}) collective-permute-start(bf16[128,256]{1,0:T(8,128)(2,1)S(1)} %constant_dynamic-update-slice_fusion.own_ref), channel_id=1, source_target_pairs={{0,8},{8,16},{16,24},{24,32},{32,40},{40,48},{48,56},{56,64},{64,7... | collective-permute-start | bytes 196616 | tf_op jit(solution)/shard_map/ppermute | solution.py:158
  25.5 5.3 %copy-start.2 = (s32[32]{0:T(128)S(1)}, s32[32]{0:T(128)}, u32[]{:S(2)}) copy-start(s32[32]{0:T(128)} %lengths_ref.1) | copy-start | bytes 388
  30.9 1.0 %copy-start = (bf16[128,2048]{1,0:T(8,128)(2,1)S(1)}, bf16[128,2048]{1,0:T(8,128)(2,1)}, u32[]{:S(2)}) copy-start(bf16[128,2048]{1,0:T(8,128)(2,1)} %query_ref.1) | copy-start | bytes 1572868
  31.9 1.0 %copy-start.1 = (bf16[128,2048]{1,0:T(8,128)(2,1)S(1)}, bf16[128,2048]{1,0:T(8,128)(2,1)}, u32[]{:S(2)}) copy-start(bf16[128,2048]{1,0:T(8,128)(2,1)} %grad_ref.1) | copy-start | bytes 1572868
  39.7 15.8 %collective-permute-start.4 = (bf16[128,256]{1,0:T(8,128)(2,1)S(1)}, bf16[128,256]{1,0:T(8,128)(2,1)S(1)}, u32[]{:S(2)}, u32[]{:S(2)}) collective-permute-start(bf16[128,256]{1,0:T(8,128)(2,1)S(1)} %get-tuple-element.11), channel_id=1, source_target_pairs={{8,0},{16,8},{24,16},{32,24},{40,32},{48,40},{56,48},{64,56},{72,6... | collective-permute-start | bytes 196616 | tf_op jit(solution)/shard_map/ppermute | solution.py:158
  42.6 12.9 %collective-permute-start.5 = (bf16[128,256]{1,0:T(8,128)(2,1)S(1)}, bf16[128,256]{1,0:T(8,128)(2,1)S(1)}, u32[]{:S(2)}, u32[]{:S(2)}) collective-permute-start(bf16[128,256]{1,0:T(8,128)(2,1)S(1)} %get-tuple-element.12), channel_id=1, source_target_pairs={{16,0},{24,8},{32,16},{40,24},{48,32},{56,40},{64,48},{72,56},{80,... | collective-permute-start | bytes 196616 | tf_op jit(solution)/shard_map/ppermute | solution.py:158
  45.7 9.8 %collective-permute-start.6 = (bf16[128,256]{1,0:T(8,128)(2,1)S(1)}, bf16[128,256]{1,0:T(8,128)(2,1)S(1)}, u32[]{:S(2)}, u32[]{:S(2)}) collective-permute-start(bf16[128,256]{1,0:T(8,128)(2,1)S(1)} %get-tuple-element.13), channel_id=1, source_target_pairs={{24,0},{32,8},{40,16},{48,24},{56,32},{64,40},{72,48},{80,56},{88,... | collective-permute-start | bytes 196616 | tf_op jit(solution)/shard_map/ppermute | solution.py:158
  50.1 12.4 %collective-permute-start.7 = (bf16[128,256]{1,0:T(8,128)(2,1)S(1)}, bf16[128,256]{1,0:T(8,128)(2,1)S(1)}, u32[]{:S(2)}, u32[]{:S(2)}) collective-permute-start(bf16[128,256]{1,0:T(8,128)(2,1)S(1)} %get-tuple-element.14), channel_id=1, source_target_pairs={{32,0},{40,8},{48,16},{56,24},{64,32},{72,40},{80,48},{88,56},{96,... | collective-permute-start | bytes 196616 | tf_op jit(solution)/shard_map/ppermute | solution.py:158

commit v2 on v0

v2 whole, which is shorter than its diff:
```python
import math

import jax
import jax.numpy as jnp
from jax import lax
from jax.experimental import pallas as pl
from jax.experimental.pallas import tpu as pltpu
from jax.sharding import PartitionSpec as P

HEADS = 128
KV_HEADS = 8
HEAD_DIM = 128
REACH = 4
TOK = 128
GROUP = HEADS // KV_HEADS
ROWS = GROUP * TOK
PAIR = 2
WIDE = PAIR * TOK
STEPS = GROUP // PAIR
DOCS = 32
NEAR = (1, 3)
HOP = 1
SCALE = 1.0 / math.sqrt(HEAD_DIM)
SCALE_LOG2E = SCALE * math.log2(math.e)
MASKED = -1e30
F32 = jnp.float32
BF16 = jnp.bfloat16
NT = (((1,), (1,)), ((), ()))
NN = (((1,), (0,)), ((), ()))


def dot(a, b, dims):
    return lax.dot_general(a, b, dims, preferred_element_type=F32)


def key_of(block):
    return block[:TOK]


def value_of(block):
    return block[TOK:]


def columns(step):
    return slice(step * WIDE, (step + 1) * WIDE)


def doc_starts(lengths_ref, row):
    total = jnp.int32(0)
    starts = jnp.zeros_like(row)
    for doc in range(DOCS):
        total = total + lengths_ref[doc]
        starts = jnp.where(total <= row, total, starts)
    return starts


def positions(index_ref, lengths_ref):
    first = index_ref[0] * TOK
    query_pos = first + lax.broadcasted_iota(jnp.int32, (1, TOK), 1)
    starts = doc_starts(lengths_ref, query_pos)
    key_pos = first + lax.broadcasted_iota(jnp.int32, (TOK, TOK), 0)
    return key_pos, starts


def bias_of(key_pos, starts):
    bias = jnp.where(key_pos >= starts, 0.0, MASKED)
    return jnp.concatenate([bias] * PAIR, axis=1)


def own_side():
    lane = lax.broadcasted_iota(jnp.int32, (TOK, WIDE), 1)
    row = lax.broadcasted_iota(jnp.int32, (TOK, WIDE), 0)
    return row <= lax.rem(lane, TOK)


def top(x):
    return jnp.max(x, axis=0, keepdims=True)


def total(x):
    return jnp.sum(x, axis=0, keepdims=True)


def load_kernel(
    index_ref,
    lengths_ref,
    query_hbm,
    grad_hbm,
    own_ref,
    query_ref,
    grad_ref,
    score_ref,
    dprob_ref,
    near_bias_ref,
    far_bias_ref,
    query_sems,
    grad_sems,
):
    def copies(head):
        there, here = pl.ds(head * HEAD_DIM, HEAD_DIM), pl.ds(head * TOK, TOK)
        return (
            pltpu.make_async_copy(query_hbm.at[:, there], query_ref.at[here, :], query_sems.at[head]),
            pltpu.make_async_copy(grad_hbm.at[:, there], grad_ref.at[here, :], grad_sems.at[head]),
        )

    for head in range(GROUP):
        for copy in copies(head):
            copy.start()
    key_pos, starts = positions(index_ref, lengths_ref)
    for at, back in enumerate(NEAR):
        near_bias_ref[at * TOK : (at + 1) * TOK, :] = bias_of(key_pos - back * TOK, starts)
    far_bias_ref[:TOK, :] = bias_of(key_pos - (NEAR[0] + HOP) * TOK, starts)
    far_bias_ref[TOK:, :] = jnp.where(own_side(), bias_of(key_pos, starts), bias_of(key_pos - REACH * TOK, starts))
    for step in range(STEPS):
        for head in range(step * PAIR, (step + 1) * PAIR):
            for copy in copies(head):
                copy.wait()
        at = columns(step)
        score_ref[:, at] = dot(key_of(own_ref), query_ref[at, :], NT)
        dprob_ref[:, at] = dot(value_of(own_ref), grad_ref[at, :], NT)


def near_kernel(bias_ref, query_ref, grad_ref, near_a_ref, near_b_ref, weight_ref, dprob_ref, stat_ref):
    keys = jnp.concatenate([key_of(near_a_ref), key_of(near_b_ref)], axis=0)
    values = jnp.concatenate([value_of(near_a_ref), value_of(near_b_ref)], axis=0)
    for step in range(STEPS):
        at = columns(step)
        scores = dot(keys, query_ref[at, :], NT) * SCALE_LOG2E + bias_ref[...]
        dprobs = dot(values, grad_ref[at, :], NT)
        peak = top(scores)
        weights = jnp.exp2(scores - peak)
        weight_ref[:, at] = weights
        dprob_ref[:, at] = dprobs
        stat_ref[0:1, at] = peak
        stat_ref[1:2, at] = total(weights)
        stat_ref[2:3, at] = total(weights * dprobs)


def far_kernel(
    bias_ref,
    query_ref,
    grad_ref,
    score_ref,
    dprob_ref,
    near_stat_ref,
    far_a_ref,
    far_b_ref,
    sums_ref,
    far_dscore_ref,
    own_prob_ref,
    own_dscore_ref,
    stat_ref,
    far_prob_ref,
):
    own = own_side()
    keys = jnp.concatenate([key_of(far_a_ref), key_of(far_b_ref)], axis=0)
    values = jnp.concatenate([value_of(far_a_ref), value_of(far_b_ref)], axis=0)

    def joined(fresh, mine):
        return jnp.concatenate([fresh[:TOK], jnp.where(own, mine, fresh[TOK:])], axis=0)

    for step in range(STEPS):
        at = columns(step)
        scores = joined(dot(keys, query_ref[at, :], NT), score_ref[:, at]) * SCALE_LOG2E + bias_ref[...]
        dprobs = joined(dot(values, grad_ref[at, :], NT), dprob_ref[:, at])
        near_peak = near_stat_ref[0:1, at]
        peak = jnp.maximum(top(scores), near_peak)
        weights = jnp.exp2(scores - peak)
        near_factor = jnp.exp2(near_peak - peak)
        inverse = 1.0 / (total(weights) + near_stat_ref[1:2, at] * near_factor)
        delta = (total(weights * dprobs) + near_stat_ref[2:3, at] * near_factor) * inverse
        stat_ref[0:1, at] = near_factor * inverse
        stat_ref[1:2, at] = delta
        probs = weights * inverse
        dscores = probs * (dprobs - delta)
        far_prob_ref[:TOK, at] = probs[:TOK].astype(BF16)
        far_dscore_ref[:TOK, at] = dscores[:TOK].astype(BF16)
        far_prob_ref[TOK:, at] = jnp.where(own, 0.0, probs[TOK:]).astype(BF16)
        far_dscore_ref[TOK:, at] = jnp.where(own, 0.0, dscores[TOK:]).astype(BF16)
        own_prob_ref[:, at] = jnp.where(own, probs[TOK:], 0.0).astype(BF16)
        own_dscore_ref[:, at] = jnp.where(own, dscores[TOK:], 0.0).astype(BF16)
    keys = (dot(far_dscore_ref[...], query_ref[...], NN) * SCALE).astype(BF16)
    values = dot(far_prob_ref[...], grad_ref[...], NN).astype(BF16)
    for at in range(len(NEAR)):
        rows = slice(at * TOK, (at + 1) * TOK)
        sums_ref[2 * at * TOK : (2 * at + 1) * TOK] = keys[rows]
        sums_ref[(2 * at + 1) * TOK : (2 * at + 2) * TOK] = values[rows]


def rest_kernel(
    query_ref,
    grad_ref,
    weight_ref,
    dprob_ref,
    stat_ref,
    far_dscore_ref,
    own_prob_ref,
    own_dscore_ref,
    own_ref,
    near_a_ref,
    far_a_ref,
    near_b_ref,
    far_b_ref,
    grad_query_hbm,
    own_sums_ref,
    near_a_sums_ref,
    near_b_sums_ref,
    near_prob_ref,
    near_dscore_ref,
    grad_query_ref,
    out_sems,
):
    far_keys = jnp.concatenate([key_of(far_a_ref), key_of(far_b_ref)], axis=0).T
    near_keys = jnp.concatenate([key_of(near_a_ref), key_of(near_b_ref)], axis=0).T
    own_keys = key_of(own_ref).T

    def out_copy(step):
        at = pl.ds(step * WIDE, WIDE)
        return pltpu.make_async_copy(grad_query_ref.at[:, at], grad_query_hbm.at[:, at], out_sems.at[step])

    for step in range(STEPS):
        at = columns(step)
        probs = weight_ref[:, at] * stat_ref[0:1, at]
        dscores = (probs * (dprob_ref[:, at] - stat_ref[1:2, at])).astype(BF16)
        near_prob_ref[:, at] = probs.astype(BF16)
        near_dscore_ref[:, at] = dscores
        grad_query = dot(far_keys, far_dscore_ref[:, at], NN) + dot(near_keys, dscores, NN)
        grad_query = ((grad_query + dot(own_keys, own_dscore_ref[:, at], NN)) * SCALE).T.astype(BF16)
        for h in range(PAIR):
            head = slice((step * PAIR + h) * HEAD_DIM, (step * PAIR + h + 1) * HEAD_DIM)
            grad_query_ref[:, head] = grad_query[h * TOK : (h + 1) * TOK]
        out_copy(step).start()
    near_keys = dot(near_dscore_ref[...], query_ref[...], NN) * SCALE
    near_values = dot(near_prob_ref[...], grad_ref[...], NN)
    for at, sums_ref in enumerate((near_a_sums_ref, near_b_sums_ref)):
        rows = slice(at * TOK, (at + 1) * TOK)
        sums_ref[:TOK] = near_keys[rows]
        sums_ref[TOK:] = near_values[rows]
    own_sums_ref[:TOK] = dot(own_dscore_ref[...], query_ref[...], NN) * SCALE
    own_sums_ref[TOK:] = dot(own_prob_ref[...], grad_ref[...], NN)
    for step in range(STEPS):
        out_copy(step).wait()


WHOLE = pl.BlockSpec(memory_space=pltpu.VMEM)
SCALARS = pl.BlockSpec(memory_space=pltpu.SMEM)
FAR = pl.BlockSpec(memory_space=pl.ANY)


def call(kernel, name, flops, in_specs, outs, scratch, *args, traffic=10**6):
    return pl.pallas_call(
        kernel,
        out_shape=[jax.ShapeDtypeStruct(shape, dtype) for shape, dtype, _ in outs],
        in_specs=in_specs,
        out_specs=[spec for _, _, spec in outs],
        scratch_shapes=scratch,
        compiler_params=pltpu.CompilerParams(vmem_limit_bytes=16 * 1024 * 1024),
        cost_estimate=pl.CostEstimate(flops=flops, bytes_accessed=traffic, transcendentals=10**5),
        name=name,
    )(*args)


def load(index, lengths, queries, grad_out, own):
    return call(
        load_kernel,
        "load",
        2 * 10**8,
        [SCALARS] * 2 + [FAR, FAR, WHOLE],
        [((ROWS, HEAD_DIM), BF16, WHOLE)] * 2
        + [((TOK, ROWS), F32, WHOLE)] * 2
        + [((2 * TOK, WIDE), F32, WHOLE)] * 2,
        [pltpu.SemaphoreType.DMA((GROUP,))] * 2,
        index,
        lengths,
        queries,
        grad_out,
        own,
        traffic=0,
    )


def near_part(bias, query, grad, near_a, near_b):
    return call(
        near_kernel,
        "near_part",
        4 * 10**8,
        [WHOLE] * 5,
        [((2 * TOK, ROWS), F32, WHOLE)] * 2 + [((8, ROWS), F32, WHOLE)],
        [],
        bias,
        query,
        grad,
        near_a,
        near_b,
    )


def far_part(bias, query, grad, score, dprob, near_stat, far_a, far_b):
    return call(
        far_kernel,
        "far_part",
        6 * 10**8,
        [WHOLE] * 8,
        [
            ((4 * TOK, HEAD_DIM), BF16, WHOLE),
            ((2 * TOK, ROWS), BF16, WHOLE),
            ((TOK, ROWS), BF16, WHOLE),
            ((TOK, ROWS), BF16, WHOLE),
            ((8, ROWS), F32, WHOLE),
        ],
        [pltpu.VMEM((2 * TOK, ROWS), BF16)],
        bias,
        query,
        grad,
        score,
        dprob,
        near_stat,
        far_a,
        far_b,
    )


def rest_part(query, grad, weight, dprob, stat, far_dscore, own_prob, own_dscore, *blocks):
    return call(
        rest_kernel,
        "rest_part",
        8 * 10**8,
        [WHOLE] * 13,
        [
            ((TOK, GROUP * HEAD_DIM), BF16, FAR),
            *[((2 * TOK, HEAD_DIM), F32, WHOLE)] * 3,
        ],
        [
            pltpu.VMEM((2 * TOK, ROWS), BF16),
            pltpu.VMEM((2 * TOK, ROWS), BF16),
            pltpu.VMEM((TOK, GROUP * HEAD_DIM), BF16),
            pltpu.SemaphoreType.DMA((STEPS,)),
        ],
        query,
        grad,
        weight,
        dprob,
        stat,
        far_dscore,
        own_prob,
        own_dscore,
        *blocks,
    )


def passed_along(array, by):
    devices = lax.axis_size("ctx")
    pairs = [(i, i + by) for i in range(devices) if 0 <= i + by < devices]
    return lax.ppermute(array, "ctx", pairs)


def local(queries, keys, values, grad_out, doc_lengths):
    index = lax.axis_index("ctx").astype(jnp.int32).reshape(1)
    low = jnp.array(-jnp.inf, BF16)
    own = lax.max(
        lax.pad(keys, low, ((0, TOK, 0), (0, 0, 0))), lax.pad(values, low, ((TOK, 0, 0), (0, 0, 0)))
    )
    near_b = passed_along(own, NEAR[1])
    near_a = passed_along(own, NEAR[0])
    query, grad, own_score, own_dprob, near_bias, far_bias = load(index, doc_lengths, queries, grad_out, own)
    near_b, near_a, far_bias = lax.optimization_barrier((near_b, near_a, far_bias))
    far = passed_along(jnp.concatenate([near_a, near_b], axis=0), HOP)
    near_weight, near_dprob, near_stat = near_part(near_bias, query, grad, near_a, near_b)
    far_a, far_b = far[: 2 * TOK], far[2 * TOK :]
    far_sums, far_dscore, own_prob, own_dscore, stat = far_part(
        far_bias, query, grad, own_score, own_dprob, near_stat, far_a, far_b
    )
    far_sums = passed_along(far_sums, -HOP)
    grad_q, own_sums, near_a_sums, near_b_sums = rest_part(
        query, grad, near_weight, near_dprob, stat, far_dscore, own_prob, own_dscore, own, near_a, far_a, near_b, far_b
    )
    near_b_sums = (near_b_sums + far_sums[2 * TOK :].astype(F32)).astype(BF16)
    near_a_sums = (near_a_sums + far_sums[: 2 * TOK].astype(F32)).astype(BF16)
    near_b_sums = passed_along(near_b_sums, -NEAR[1])
    near_a_sums = passed_along(near_a_sums, -NEAR[0])
    sums = (own_sums + near_b_sums.astype(F32) + near_a_sums.astype(F32)).astype(BF16)
    return (grad_q, key_of(sums), value_of(sums))


def solution(mesh):
    placed = (P("ctx", "tp"), P("ctx", "tp"), P("ctx", "tp"), P("ctx", "tp"), P())
    return jax.shard_map(
        local,
        mesh=mesh,
        in_specs=placed,
        out_specs=(P("ctx", "tp"), P("ctx", "tp"), P("ctx", "tp")),
        check_vma=False,
    )
```

time: 98.8 us -> 50.9 us (0.52)
  waiting for transfers between devices: 41.2 us -> 11.9 us
  matrix products: 16.5 us -> 0 us
  Pallas kernels: 0 us -> 8.38 us
  other arithmetic: 5.99 us -> 0.85 us
  local copies, waits for them, and re-layouts: 7.3 us -> 3.37 us
    ppermute x8 -> x6, waiting for transfers between devices: 41.2 us -> 11.9 us  [passed_along(): return lax.ppermute(array, 'ctx', pairs)]
    dot_general x24 -> x0, matrix products: 16.5 us -> none  [the longest x4 4.94 us: attend(): jnp.einsum('ghqk,qghd->kgd', probs_b, grad_blk, preferred_element_type=jn...]
    pallas_call x0 -> x4, Pallas kernels: none -> 8.38 us  [call(): pl.pallas_call(kernel, out_shape=[jax.ShapeDtypeStruct(shape, dtype) for...]
    add x9 -> x0, other arithmetic: 2.44 us -> none  [the longest x4 2.37 us: attend(): lse = peak + jnp.log(total)]
    while x106 -> x0, local copies, waits for them, and re-layouts: 2.09 us -> none
    reduce_sum x6 -> x0, other arithmetic: 1.83 us -> none  [the longest x4 1.65 us: attend(): jnp.sum(jnp.where(mask, jnp.exp(scores - peak), 0.0), axis=-1, keepdims=T...]
    reshape x1 -> x0, local copies, waits for them, and re-layouts: 1.18 us -> none  [local(): jnp.moveaxis(grad_queries, 0, 2).reshape(tok, kv_local * group * HEAD_DIM)]
    unnamed x14 -> x6, local copies, waits for them, and re-layouts: 1.66 us -> 2.73 us
  transfers between devices with their start and end apart: 8 -> 6, of which waited for: 8 -> 4; matrix products, arithmetic and copies ran while one was open for 4% -> 0% of each run, Pallas kernels for 0% -> 12%
where the time goes in v2:
time: 50.9 us; the launch traced here: 50.4 us
  starting transfers between devices  25.2 us (50%)
  waiting for transfers between devices  11.9 us (23%)
  Pallas kernels  8.38 us (16%)
  local copies, waits for them, and re-layouts  3.37 us (7%)
  other arithmetic  0.85 us (2%)
  between operations  0.76 us (1%)
    ppermute x6, starting transfers between devices, passed_along(): return lax.ppermute(array, 'ctx', pairs)  25.2 us
    ppermute x6, waiting for transfers between devices, passed_along(): return lax.ppermute(array, 'ctx', pairs)  11.9 us
    pallas_call x4, Pallas kernels, call(): pl.pallas_call(kernel, out_shape=[jax.ShapeDtypeStruct(shape, dtype) for...  8.38 us
    unnamed x6, local copies, waits for them, and re-layouts  2.73 us
  transfers between devices with their start and end apart: 6, of which 4 were waited for; matrix products, arithmetic and copies ran while one was open for 0% of the time, Pallas kernels for 12%

profile of v2, /device:TPU:24, one launch (start us, length us, event | category | flops | bytes accessed | tf_op | source)
XLA Modules:
  0.0 50.4 jit_solution(1419906255720037135)
XLA Ops:
  0.6 0.8 %pad_maximum_fusion.1.own_ref = bf16[256,128]{1,0:T(8,128)(2,1)S(1)} fusion(bf16[128,128]{1,0:T(8,128)(2,1)} %param.7, bf16[128,128]{1,0:T(8,128)(2,1)} %param.6), kind=kLoop, calls=%fused_computation.4 | loop fusion | flops 131072 | bytes 131072 | tf_op jit(solution)/shard_map/max | solution.py:360
  1.4 6.5 %collective-permute-start = (bf16[256,128]{1,0:T(8,128)(2,1)S(1)}, bf16[256,128]{1,0:T(8,128)(2,1)S(1)}, u32[]{:S(2)}, u32[]{:S(2)}) collective-permute-start(bf16[256,128]{1,0:T(8,128)(2,1)S(1)} %pad_maximum_fusion.1.own_ref), channel_id=1, source_target_pairs={{0,24},{8,32},{16,40},{24,48},{32,56},{40,64},{48,72},{56,80},{64,... | collective-permute-start | bytes 196616 | tf_op jit(solution)/shard_map/ppermute | solution.py:354
  7.9 5.0 %collective-permute-start.1 = (bf16[256,128]{1,0:T(8,128)(2,1)S(1)}, bf16[256,128]{1,0:T(8,128)(2,1)S(1)}, u32[]{:S(2)}, u32[]{:S(2)}) collective-permute-start(bf16[256,128]{1,0:T(8,128)(2,1)S(1)} %pad_maximum_fusion.1.own_ref), channel_id=1, source_target_pairs={{0,8},{8,16},{16,24},{24,32},{32,40},{40,48},{48,56},{56,64},{64,7... | collective-permute-start | bytes 196616 | tf_op jit(solution)/shard_map/ppermute | solution.py:354
  13.0 0.0 copy-start
  13.0 1.0 %copy-done = bf16[128,2048]{1,0:T(8,128)(2,1)S(1)} copy-done((bf16[128,2048]{1,0:T(8,128)(2,1)S(1)}, bf16[128,2048]{1,0:T(8,128)(2,1)}, u32[]{:S(2)}) %copy-start) | copy-done | bytes 524312
  14.0 0.0 copy-start.1
  14.0 1.0 %copy-done.1 = bf16[128,2048]{1,0:T(8,128)(2,1)S(1)} copy-done((bf16[128,2048]{1,0:T(8,128)(2,1)S(1)}, bf16[128,2048]{1,0:T(8,128)(2,1)}, u32[]{:S(2)}) %copy-start.1) | copy-done | bytes 524312
  15.1 0.0 copy-start.2
  15.1 0.7 %copy-done.2 = s32[32]{0:T(128)S(1)} copy-done((s32[32]{0:T(128)S(1)}, s32[32]{0:T(128)}, u32[]{:S(2)}) %copy-start.2) | copy-done | bytes 152
  15.7 2.7 %load.1 = (bf16[2048,128]{1,0:T(8,128)(2,1)S(1)}, bf16[2048,128]{1,0:T(8,128)(2,1)S(1)}, f32[128,2048]{1,0:T(8,128)S(1)}, f32[128,2048]{1,0:T(8,128)S(1)}, f32[2...) custom-call(s32[1]{0:T(128)} %bitcast.index_ref, s32[32]{0:T(128)S(1)} %copy-done.2, bf16[128,2048]{1,0:T(8,128)(2,1)S(1)} %copy-done, ...), custom_call_target="tpu_custom_call" | custom-call | flops 200000000 | tf_op jit(solution)/shard_map/load/pallas_call | solution.py:251
  18.5 0.0 collective-permute-done.near_b_ref
  18.5 0.8 %collective-permute-done.1.near_a_ref = bf16[256,128]{1,0:T(8,128)(2,1)S(1)} collective-permute-done((bf16[256,128]{1,0:T(8,128)(2,1)S(1)}, bf16[256,128]{1,0:T(8,128)(2,1)S(1)}, u32[]{:S(2)}, u32[]{:S(2)}) %collective-permute-start.1) | collective-permute-done | bytes 65568 | tf_op jit(solution)/shard_map/ppermute | solution.py:354
  19.3 3.0 %collective-permute-start.2 = (bf16[512,128]{1,0:T(8,128)(2,1)S(1)}, bf16[512,128]{1,0:T(8,128)(2,1)S(1)}, u32[]{:S(2)}, u32[]{:S(2)}) collective-permute-start(bf16[512,128]{1,0:T(8,128)(2,1)S(1)} %pad_maximum_fusion), channel_id=1, source_target_pairs={{0,8},{8,16},{16,24},{24,32},{32,40},{40,48},{48,56},{56,64},{64,7... | collective-permute-start | bytes 393224 | tf_op jit(solution)/shard_map/ppermute | solution.py:354
  22.3 0.9 %near_part.1 = (f32[256,2048]{1,0:T(8,128)S(1)}, f32[256,2048]{1,0:T(8,128)S(1)}, f32[8,2048]{1,0:T(8,128)S(1)}) custom-call(f32[256,256]{1,0:T(8,128)S(1)} %get-tuple-element.26.bias_ref, bf16[2048,128]{1,0:T(8,128)(2,1)S(1)} %get-tuple-element.24.query_ref, bf16[2048,128]{1,0:T(8,128)(2,1)S(1)} %get-tuple-element.25.grad_ref, ...), custom_call_target="tpu_custom_call" | custom-call | flops 400000000 | bytes 1000000 | tf_op jit(solution)/shard_map/near_part/pallas_call | solution.py:251
  23.3 5.0 %collective-permute-done.2 = bf16[512,128]{1,0:T(8,128)(2,1)S(1)} collective-permute-done((bf16[512,128]{1,0:T(8,128)(2,1)S(1)}, bf16[512,128]{1,0:T(8,128)(2,1)S(1)}, u32[]{:S(2)}, u32[]{:S(2)}) %collective-permute-start.2) | collective-permute-done | bytes 131104 | tf_op jit(solution)/shard_map/ppermute | solution.py:354
  28.3 2.5 %far_part.1 = (bf16[512,128]{1,0:T(8,128)(2,1)S(1)}, bf16[256,2048]{1,0:T(8,128)(2,1)S(1)}, bf16[128,2048]{1,0:T(8,128)(2,1)S(1)}, bf16[128,2048]{1,0:T(8,128)(2,1)S(1)}, f32[8,2048]{1,0:T(8,128)S(1)}) custom-call(f32[256,256]{1,0:T(8,128)S(1)} %get-tuple-element.32.bias_ref, bf16[2048,128]{1,0:T(8,128)(2,1)S(1)} %get-tuple-element.24.query_ref, ...), custom_call_target="tpu_custom_call" | custom-call | flops 600000000 | bytes 1000000 | tf_op jit(solution)/shard_map/far_part/pallas_call | solution.py:251
  30.9 1.9 %collective-permute-start.3 = (bf16[512,128]{1,0:T(8,128)(2,1)S(1)}, bf16[512,128]{1,0:T(8,128)(2,1)S(1)}, u32[]{:S(2)}, u32[]{:S(2)}) collective-permute-start(bf16[512,128]{1,0:T(8,128)(2,1)S(1)} %get-tuple-element.43), channel_id=1, source_target_pairs={{8,0},{16,8},{24,16},{32,24},{40,32},{48,40},{56,48},{64,56},{72,6... | collective-permute-start | bytes 393224 | tf_op jit(solution)/shard_map/ppermute | solution.py:354
  32.8 2.2 %rest_part.1 = (bf16[128,2048]{1,0:T(8,128)(2,1)}, f32[256,128]{1,0:T(8,128)S(1)}, f32[256,128]{1,0:T(8,128)S(1)}, f32[256,128]{1,0:T(8,128)S(1)}) custom-call(bf16[2048,128]{1,0:T(8,128)(2,1)S(1)} %get-tuple-element.24.query_ref, bf16[2048,128]{1,0:T(8,128)(2,1)S(1)} %get-tuple-element.25.grad_ref, f32[256,2048]{1,0:T(8,128)S(1)} %get-tuple-element.30.weight_ref, ...), custom_call_target="tpu_custom_call" | custom-call | flops 800000000 | bytes 1000000 | tf_op jit(solution)/shard_map/rest_part/pallas_call | solution.py:251
  35.0 2.8 %collective-permute-done.3 = bf16[512,128]{1,0:T(8,128)(2,1)S(1)} collective-permute-done((bf16[512,128]{1,0:T(8,128)(2,1)S(1)}, bf16[512,128]{1,0:T(8,128)(2,1)S(1)}, u32[]{:S(2)}, u32[]{:S(2)}) %collective-permute-start.3) | collective-permute-done | bytes 131104 | tf_op jit(solution)/shard_map/ppermute | solution.py:354
  37.8 4.0 %collective-permute-start.5 = (bf16[256,128]{1,0:T(8,128)(2,1)S(1)}, bf16[256,128]{1,0:T(8,128)(2,1)S(1)}, u32[]{:S(2)}, u32[]{:S(2)}) collective-permute-start(bf16[256,128]{1,0:T(8,128)(2,1)S(1)} %get-tuple-element.46), channel_id=1, source_target_pairs={{8,0},{16,8},{24,16},{32,24},{40,32},{48,40},{56,48},{64,56},{72,6... | collective-permute-start | bytes 196616 | tf_op jit(solution)/shard_map/ppermute | solution.py:354
  41.8 4.6 %collective-permute-start.4 = (bf16[256,128]{1,0:T(8,128)(2,1)S(1)}, bf16[256,128]{1,0:T(8,128)(2,1)S(1)}, u32[]{:S(2)}, u32[]{:S(2)}) collective-permute-start(bf16[256,128]{1,0:T(8,128)(2,1)S(1)} %get-tuple-element.45), channel_id=1, source_target_pairs={{24,0},{32,8},{40,16},{48,24},{56,32},{64,40},{72,48},{80,56},{88,... | collective-permute-start | bytes 196616 | tf_op jit(solution)/shard_map/ppermute | solution.py:354
  46.4 0.0 collective-permute-done.5
  46.4 3.3 %collective-permute-done.4 = bf16[256,128]{1,0:T(8,128)(2,1)S(1)} collective-permute-done((bf16[256,128]{1,0:T(8,128)(2,1)S(1)}, bf16[256,128]{1,0:T(8,128)(2,1)S(1)}, u32[]{:S(2)}, u32[]{:S(2)}) %collective-permute-start.4) | collective-permute-done | bytes 65568 | tf_op jit(solution)/shard_map/ppermute | solution.py:354
  49.8 0.6 %fusion.1 = (bf16[128,128]{1,0:T(8,128)(2,1)}, bf16[128,128]{1,0:T(8,128)(2,1)}) fusion(bf16[256,128]{1,0:T(8,128)(2,1)S(1)} %add_convert_fusion), kind=kLoop, calls=%fused_computation.6 | loop fusion | bytes 131072 | tf_op jit(solution)/shard_map/slice | solution.py:41
  (4 shorter events, 0.1 us)
Async XLA Ops:
  1.4 17.1 %collective-permute-start = (bf16[256,128]{1,0:T(8,128)(2,1)S(1)}, bf16[256,128]{1,0:T(8,128)(2,1)S(1)}, u32[]{:S(2)}, u32[]{:S(2)}) collective-permute-start(bf16[256,128]{1,0:T(8,128)(2,1)S(1)} %pad_maximum_fusion.1.own_ref), channel_id=1, source_target_pairs={{0,24},{8,32},{16,40},{24,48},{32,56},{40,64},{48,72},{56,80},{64,... | collective-permute-start | bytes 196616 | tf_op jit(solution)/shard_map/ppermute | solution.py:354
  7.9 11.3 %collective-permute-start.1 = (bf16[256,128]{1,0:T(8,128)(2,1)S(1)}, bf16[256,128]{1,0:T(8,128)(2,1)S(1)}, u32[]{:S(2)}, u32[]{:S(2)}) collective-permute-start(bf16[256,128]{1,0:T(8,128)(2,1)S(1)} %pad_maximum_fusion.1.own_ref), channel_id=1, source_target_pairs={{0,8},{8,16},{16,24},{24,32},{32,40},{40,48},{48,56},{56,64},{64,7... | collective-permute-start | bytes 196616 | tf_op jit(solution)/shard_map/ppermute | solution.py:354
  13.0 1.0 %copy-start = (bf16[128,2048]{1,0:T(8,128)(2,1)S(1)}, bf16[128,2048]{1,0:T(8,128)(2,1)}, u32[]{:S(2)}) copy-start(bf16[128,2048]{1,0:T(8,128)(2,1)} %query_hbm.1) | copy-start | bytes 1572868
  14.0 1.0 %copy-start.1 = (bf16[128,2048]{1,0:T(8,128)(2,1)S(1)}, bf16[128,2048]{1,0:T(8,128)(2,1)}, u32[]{:S(2)}) copy-start(bf16[128,2048]{1,0:T(8,128)(2,1)} %grad_hbm.1) | copy-start | bytes 1572868
  15.1 0.7 %copy-start.2 = (s32[32]{0:T(128)S(1)}, s32[32]{0:T(128)}, u32[]{:S(2)}) copy-start(s32[32]{0:T(128)} %lengths_ref.1) | copy-start | bytes 388
  19.3 9.0 %collective-permute-start.2 = (bf16[512,128]{1,0:T(8,128)(2,1)S(1)}, bf16[512,128]{1,0:T(8,128)(2,1)S(1)}, u32[]{:S(2)}, u32[]{:S(2)}) collective-permute-start(bf16[512,128]{1,0:T(8,128)(2,1)S(1)} %pad_maximum_fusion), channel_id=1, source_target_pairs={{0,8},{8,16},{16,24},{24,32},{32,40},{40,48},{48,56},{56,64},{64,7... | collective-permute-start | bytes 393224 | tf_op jit(solution)/shard_map/ppermute | solution.py:354
  30.9 6.9 %collective-permute-start.3 = (bf16[512,128]{1,0:T(8,128)(2,1)S(1)}, bf16[512,128]{1,0:T(8,128)(2,1)S(1)}, u32[]{:S(2)}, u32[]{:S(2)}) collective-permute-start(bf16[512,128]{1,0:T(8,128)(2,1)S(1)} %get-tuple-element.43), channel_id=1, source_target_pairs={{8,0},{16,8},{24,16},{32,24},{40,32},{48,40},{56,48},{64,56},{72,6... | collective-permute-start | bytes 393224 | tf_op jit(solution)/shard_map/ppermute | solution.py:354
  37.8 8.7 %collective-permute-start.5 = (bf16[256,128]{1,0:T(8,128)(2,1)S(1)}, bf16[256,128]{1,0:T(8,128)(2,1)S(1)}, u32[]{:S(2)}, u32[]{:S(2)}) collective-permute-start(bf16[256,128]{1,0:T(8,128)(2,1)S(1)} %get-tuple-element.46), channel_id=1, source_target_pairs={{8,0},{16,8},{24,16},{32,24},{40,32},{48,40},{56,48},{64,56},{72,6... | collective-permute-start | bytes 196616 | tf_op jit(solution)/shard_map/ppermute | solution.py:354
  41.8 8.0 %collective-permute-start.4 = (bf16[256,128]{1,0:T(8,128)(2,1)S(1)}, bf16[256,128]{1,0:T(8,128)(2,1)S(1)}, u32[]{:S(2)}, u32[]{:S(2)}) collective-permute-start(bf16[256,128]{1,0:T(8,128)(2,1)S(1)} %get-tuple-element.45), channel_id=1, source_target_pairs={{24,0},{32,8},{40,16},{48,24},{56,32},{64,40},{72,48},{80,56},{88,... | collective-permute-start | bytes 196616 | tf_op jit(solution)/shard_map/ppermute | solution.py:354

commit v3 on v2

--- a/solution.py
+++ b/solution.py
@@ -84,8 +84,8 @@
 def load_kernel(
     index_ref,
     lengths_ref,
-    query_hbm,
-    grad_hbm,
+    all_query_ref,
+    all_grad_ref,
     own_ref,
     query_ref,
     grad_ref,
@@ -93,19 +93,7 @@
     dprob_ref,
     near_bias_ref,
     far_bias_ref,
-    query_sems,
-    grad_sems,
 ):
-    def copies(head):
-        there, here = pl.ds(head * HEAD_DIM, HEAD_DIM), pl.ds(head * TOK, TOK)
-        return (
-            pltpu.make_async_copy(query_hbm.at[:, there], query_ref.at[here, :], query_sems.at[head]),
-            pltpu.make_async_copy(grad_hbm.at[:, there], grad_ref.at[here, :], grad_sems.at[head]),
-        )
-
-    for head in range(GROUP):
-        for copy in copies(head):
-            copy.start()
     key_pos, starts = positions(index_ref, lengths_ref)
     for at, back in enumerate(NEAR):
         near_bias_ref[at * TOK : (at + 1) * TOK, :] = bias_of(key_pos - back * TOK, starts)
@@ -113,8 +101,9 @@
     far_bias_ref[TOK:, :] = jnp.where(own_side(), bias_of(key_pos, starts), bias_of(key_pos - REACH * TOK, starts))
     for step in range(STEPS):
         for head in range(step * PAIR, (step + 1) * PAIR):
-            for copy in copies(head):
-                copy.wait()
+            there, here = slice(head * HEAD_DIM, (head + 1) * HEAD_DIM), slice(head * TOK, (head + 1) * TOK)
+            query_ref[here, :] = all_query_ref[:, there]
+            grad_ref[here, :] = all_grad_ref[:, there]
         at = columns(step)
         score_ref[:, at] = dot(key_of(own_ref), query_ref[at, :], NT)
         dprob_ref[:, at] = dot(value_of(own_ref), grad_ref[at, :], NT)
@@ -156,29 +145,42 @@
     keys = jnp.concatenate([key_of(far_a_ref), key_of(far_b_ref)], axis=0)
     values = jnp.concatenate([value_of(far_a_ref), value_of(far_b_ref)], axis=0)
 
-    def joined(fresh, mine):
-        return jnp.concatenate([fresh[:TOK], jnp.where(own, mine, fresh[TOK:])], axis=0)
-
+    halves = (slice(0, TOK), slice(TOK, 2 * TOK))
     for step in range(STEPS):
         at = columns(step)
-        scores = joined(dot(keys, query_ref[at, :], NT), score_ref[:, at]) * SCALE_LOG2E + bias_ref[...]
-        dprobs = joined(dot(values, grad_ref[at, :], NT), dprob_ref[:, at])
+        fresh_scores = dot(keys, query_ref[at, :], NT)
+        fresh_dprobs = dot(values, grad_ref[at, :], NT)
+        peaks, weights, dprobs, totals, products = [], [], [], [], []
+        for rows in halves:
+            scores, dprob = fresh_scores[rows], fresh_dprobs[rows]
+            if rows.start:
+                scores, dprob = jnp.where(own, score_ref[:, at], scores), jnp.where(own, dprob_ref[:, at], dprob)
+            scores = scores * SCALE_LOG2E + bias_ref[rows, :]
+            peak = top(scores)
+            weight = jnp.exp2(scores - peak)
+            peaks.append(peak)
+            weights.append(weight)
+            dprobs.append(dprob)
+            totals.append(total(weight))
+            products.append(total(weight * dprob))
         near_peak = near_stat_ref[0:1, at]
-        peak = jnp.maximum(top(scores), near_peak)
-        weights = jnp.exp2(scores - peak)
+        peak = jnp.maximum(jnp.maximum(peaks[0], peaks[1]), near_peak)
         near_factor = jnp.exp2(near_peak - peak)
-        inverse = 1.0 / (total(weights) + near_stat_ref[1:2, at] * near_factor)
-        delta = (total(weights * dprobs) + near_stat_ref[2:3, at] * near_factor) * inverse
+        factors = [jnp.exp2(part - peak) for part in peaks]
+        inverse = 1.0 / (totals[0] * factors[0] + totals[1] * factors[1] + near_stat_ref[1:2, at] * near_factor)
+        delta = products[0] * factors[0] + products[1] * factors[1] + near_stat_ref[2:3, at] * near_factor
+        delta = delta * inverse
         stat_ref[0:1, at] = near_factor * inverse
         stat_ref[1:2, at] = delta
-        probs = weights * inverse
-        dscores = probs * (dprobs - delta)
-        far_prob_ref[:TOK, at] = probs[:TOK].astype(BF16)
-        far_dscore_ref[:TOK, at] = dscores[:TOK].astype(BF16)
-        far_prob_ref[TOK:, at] = jnp.where(own, 0.0, probs[TOK:]).astype(BF16)
-        far_dscore_ref[TOK:, at] = jnp.where(own, 0.0, dscores[TOK:]).astype(BF16)
-        own_prob_ref[:, at] = jnp.where(own, probs[TOK:], 0.0).astype(BF16)
-        own_dscore_ref[:, at] = jnp.where(own, dscores[TOK:], 0.0).astype(BF16)
+        probs = weights[0] * (factors[0] * inverse)
+        far_prob_ref[:TOK, at] = probs.astype(BF16)
+        far_dscore_ref[:TOK, at] = (probs * (dprobs[0] - delta)).astype(BF16)
+        probs = weights[1] * (factors[1] * inverse)
+        dscores = probs * (dprobs[1] - delta)
+        far_prob_ref[TOK:, at] = jnp.where(own, 0.0, probs).astype(BF16)
+        far_dscore_ref[TOK:, at] = jnp.where(own, 0.0, dscores).astype(BF16)
+        own_prob_ref[:, at] = jnp.where(own, probs, 0.0).astype(BF16)
+        own_dscore_ref[:, at] = jnp.where(own, dscores, 0.0).astype(BF16)
     keys = (dot(far_dscore_ref[...], query_ref[...], NN) * SCALE).astype(BF16)
     values = dot(far_prob_ref[...], grad_ref[...], NN).astype(BF16)
     for at in range(len(NEAR)):
@@ -265,11 +267,11 @@
         load_kernel,
         "load",
         2 * 10**8,
-        [SCALARS] * 2 + [FAR, FAR, WHOLE],
+        [SCALARS] * 2 + [WHOLE] * 3,
         [((ROWS, HEAD_DIM), BF16, WHOLE)] * 2
         + [((TOK, ROWS), F32, WHOLE)] * 2
         + [((2 * TOK, WIDE), F32, WHOLE)] * 2,
-        [pltpu.SemaphoreType.DMA((GROUP,))] * 2,
+        [],
         index,
         lengths,
         queries,
@@ -378,7 +380,7 @@
     near_a_sums = (near_a_sums + far_sums[: 2 * TOK].astype(F32)).astype(BF16)
     near_b_sums = passed_along(near_b_sums, -NEAR[1])
     near_a_sums = passed_along(near_a_sums, -NEAR[0])
-    sums = (own_sums + near_b_sums.astype(F32) + near_a_sums.astype(F32)).astype(BF16)
+    sums = (own_sums + near_a_sums.astype(F32) + near_b_sums.astype(F32)).astype(BF16)
     return (grad_q, key_of(sums), value_of(sums))
 
 

time: 50.9 us -> 49.2 us (0.967)
  Pallas kernels: 8.38 us -> 6.42 us
  waiting for transfers between devices: 11.9 us -> 13 us
  starting transfers between devices: 25.2 us -> 24.5 us
    pallas_call x4, Pallas kernels: 8.38 us -> 6.42 us  [call(): pl.pallas_call(kernel, out_shape=[jax.ShapeDtypeStruct(shape, dtype) for...]
    ppermute x6, waiting for transfers between devices: 11.9 us -> 13 us  [passed_along(): return lax.ppermute(array, 'ctx', pairs)]
    ppermute x6, starting transfers between devices: 25.2 us -> 24.5 us  [passed_along(): return lax.ppermute(array, 'ctx', pairs)]
  transfers between devices with their start and end apart: 6 -> 6, of which waited for: 4 -> 5; matrix products, arithmetic and copies ran while one was open for 0% -> 0% of each run, Pallas kernels for 12% -> 9%
where the time goes in v3:
time: 49.2 us; the launch traced here: 48.8 us
  starting transfers between devices  24.5 us (50%)
  waiting for transfers between devices  13 us (26%)
  Pallas kernels  6.42 us (13%)
  local copies, waits for them, and re-layouts  3.37 us (7%)
  other arithmetic  0.85 us (2%)
  between operations  0.75 us (2%)
    ppermute x6, starting transfers between devices, passed_along(): return lax.ppermute(array, 'ctx', pairs)  24.5 us
    ppermute x6, waiting for transfers between devices, passed_along(): return lax.ppermute(array, 'ctx', pairs)  13 us
    pallas_call x4, Pallas kernels, call(): pl.pallas_call(kernel, out_shape=[jax.ShapeDtypeStruct(shape, dtype) for...  6.42 us
    unnamed x6, local copies, waits for them, and re-layouts  2.73 us
  transfers between devices with their start and end apart: 6, of which 5 were waited for; matrix products, arithmetic and copies ran while one was open for 0% of the time, Pallas kernels for 9%

profile of v3, /device:TPU:24, one launch (start us, length us, event | category | flops | bytes accessed | tf_op | source)
XLA Modules:
  0.0 48.8 jit_solution(14483377618994332442)
XLA Ops:
  0.6 0.8 %pad_maximum_fusion.1.own_ref = bf16[256,128]{1,0:T(8,128)(2,1)S(1)} fusion(bf16[128,128]{1,0:T(8,128)(2,1)} %param.7, bf16[128,128]{1,0:T(8,128)(2,1)} %param.6), kind=kLoop, calls=%fused_computation.4 | loop fusion | flops 131072 | bytes 131072 | tf_op jit(solution)/shard_map/max | solution.py:362
  1.4 6.5 %collective-permute-start = (bf16[256,128]{1,0:T(8,128)(2,1)S(1)}, bf16[256,128]{1,0:T(8,128)(2,1)S(1)}, u32[]{:S(2)}, u32[]{:S(2)}) collective-permute-start(bf16[256,128]{1,0:T(8,128)(2,1)S(1)} %pad_maximum_fusion.1.own_ref), channel_id=1, source_target_pairs={{0,24},{8,32},{16,40},{24,48},{32,56},{40,64},{48,72},{56,80},{64,... | collective-permute-start | bytes 196616 | tf_op jit(solution)/shard_map/ppermute | solution.py:356
  7.9 5.0 %collective-permute-start.1 = (bf16[256,128]{1,0:T(8,128)(2,1)S(1)}, bf16[256,128]{1,0:T(8,128)(2,1)S(1)}, u32[]{:S(2)}, u32[]{:S(2)}) collective-permute-start(bf16[256,128]{1,0:T(8,128)(2,1)S(1)} %pad_maximum_fusion.1.own_ref), channel_id=1, source_target_pairs={{0,8},{8,16},{16,24},{24,32},{32,40},{40,48},{48,56},{56,64},{64,7... | collective-permute-start | bytes 196616 | tf_op jit(solution)/shard_map/ppermute | solution.py:356
  13.0 0.0 copy-start
  13.0 1.0 %copy-done = bf16[128,2048]{1,0:T(8,128)(2,1)S(1)} copy-done((bf16[128,2048]{1,0:T(8,128)(2,1)S(1)}, bf16[128,2048]{1,0:T(8,128)(2,1)}, u32[]{:S(2)}) %copy-start) | copy-done | bytes 524312
  14.0 0.0 copy-start.1
  14.0 1.0 %copy-done.1 = bf16[128,2048]{1,0:T(8,128)(2,1)S(1)} copy-done((bf16[128,2048]{1,0:T(8,128)(2,1)S(1)}, bf16[128,2048]{1,0:T(8,128)(2,1)}, u32[]{:S(2)}) %copy-start.1) | copy-done | bytes 524312
  15.1 0.0 copy-start.2
  15.1 0.7 %copy-done.2 = s32[32]{0:T(128)S(1)} copy-done((s32[32]{0:T(128)S(1)}, s32[32]{0:T(128)}, u32[]{:S(2)}) %copy-start.2) | copy-done | bytes 152
  15.7 1.1 %load.1 = (bf16[2048,128]{1,0:T(8,128)(2,1)S(1)}, bf16[2048,128]{1,0:T(8,128)(2,1)S(1)}, f32[128,2048]{1,0:T(8,128)S(1)}, f32[128,2048]{1,0:T(8,128)S(1)}, f32[2...) custom-call(s32[1]{0:T(128)} %bitcast.index_ref, s32[32]{0:T(128)S(1)} %copy-done.2, bf16[128,2048]{1,0:T(8,128)(2,1)S(1)} %copy-done, ...), custom_call_target="tpu_custom_call" | custom-call | flops 200000000 | tf_op jit(solution)/shard_map/load/pallas_call | solution.py:253
  16.9 0.0 collective-permute-done.near_b_ref
  16.9 2.4 %collective-permute-done.1.near_a_ref = bf16[256,128]{1,0:T(8,128)(2,1)S(1)} collective-permute-done((bf16[256,128]{1,0:T(8,128)(2,1)S(1)}, bf16[256,128]{1,0:T(8,128)(2,1)S(1)}, u32[]{:S(2)}, u32[]{:S(2)}) %collective-permute-start.1) | collective-permute-done | bytes 65568 | tf_op jit(solution)/shard_map/ppermute | solution.py:356
  19.3 2.4 %collective-permute-start.2 = (bf16[512,128]{1,0:T(8,128)(2,1)S(1)}, bf16[512,128]{1,0:T(8,128)(2,1)S(1)}, u32[]{:S(2)}, u32[]{:S(2)}) collective-permute-start(bf16[512,128]{1,0:T(8,128)(2,1)S(1)} %pad_maximum_fusion), channel_id=1, source_target_pairs={{0,8},{8,16},{16,24},{24,32},{32,40},{40,48},{48,56},{56,64},{64,7... | collective-permute-start | bytes 393224 | tf_op jit(solution)/shard_map/ppermute | solution.py:356
  21.7 0.9 %near_part.1 = (f32[256,2048]{1,0:T(8,128)S(1)}, f32[256,2048]{1,0:T(8,128)S(1)}, f32[8,2048]{1,0:T(8,128)S(1)}) custom-call(f32[256,256]{1,0:T(8,128)S(1)} %get-tuple-element.26.bias_ref, bf16[2048,128]{1,0:T(8,128)(2,1)S(1)} %get-tuple-element.24.query_ref, bf16[2048,128]{1,0:T(8,128)(2,1)S(1)} %get-tuple-element.25.grad_ref, ...), custom_call_target="tpu_custom_call" | custom-call | flops 400000000 | bytes 1000000 | tf_op jit(solution)/shard_map/near_part/pallas_call | solution.py:253
  22.6 5.7 %collective-permute-done.2 = bf16[512,128]{1,0:T(8,128)(2,1)S(1)} collective-permute-done((bf16[512,128]{1,0:T(8,128)(2,1)S(1)}, bf16[512,128]{1,0:T(8,128)(2,1)S(1)}, u32[]{:S(2)}, u32[]{:S(2)}) %collective-permute-start.2) | collective-permute-done | bytes 131104 | tf_op jit(solution)/shard_map/ppermute | solution.py:356
  28.3 2.2 %far_part.1 = (bf16[512,128]{1,0:T(8,128)(2,1)S(1)}, bf16[256,2048]{1,0:T(8,128)(2,1)S(1)}, bf16[128,2048]{1,0:T(8,128)(2,1)S(1)}, bf16[128,2048]{1,0:T(8,128)(2,1)S(1)}, f32[8,2048]{1,0:T(8,128)S(1)}) custom-call(f32[256,256]{1,0:T(8,128)S(1)} %get-tuple-element.32.bias_ref, bf16[2048,128]{1,0:T(8,128)(2,1)S(1)} %get-tuple-element.24.query_ref, ...), custom_call_target="tpu_custom_call" | custom-call | flops 600000000 | bytes 1000000 | tf_op jit(solution)/shard_map/far_part/pallas_call | solution.py:253
  30.5 1.9 %collective-permute-start.3 = (bf16[512,128]{1,0:T(8,128)(2,1)S(1)}, bf16[512,128]{1,0:T(8,128)(2,1)S(1)}, u32[]{:S(2)}, u32[]{:S(2)}) collective-permute-start(bf16[512,128]{1,0:T(8,128)(2,1)S(1)} %get-tuple-element.43), channel_id=1, source_target_pairs={{8,0},{16,8},{24,16},{32,24},{40,32},{48,40},{56,48},{64,56},{72,6... | collective-permute-start | bytes 393224 | tf_op jit(solution)/shard_map/ppermute | solution.py:356
  32.4 2.2 %rest_part.1 = (bf16[128,2048]{1,0:T(8,128)(2,1)}, f32[256,128]{1,0:T(8,128)S(1)}, f32[256,128]{1,0:T(8,128)S(1)}, f32[256,128]{1,0:T(8,128)S(1)}) custom-call(bf16[2048,128]{1,0:T(8,128)(2,1)S(1)} %get-tuple-element.24.query_ref, bf16[2048,128]{1,0:T(8,128)(2,1)S(1)} %get-tuple-element.25.grad_ref, f32[256,2048]{1,0:T(8,128)S(1)} %get-tuple-element.30.weight_ref, ...), custom_call_target="tpu_custom_call" | custom-call | flops 800000000 | bytes 1000000 | tf_op jit(solution)/shard_map/rest_part/pallas_call | solution.py:253
  34.6 2.8 %collective-permute-done.3 = bf16[512,128]{1,0:T(8,128)(2,1)S(1)} collective-permute-done((bf16[512,128]{1,0:T(8,128)(2,1)S(1)}, bf16[512,128]{1,0:T(8,128)(2,1)S(1)}, u32[]{:S(2)}, u32[]{:S(2)}) %collective-permute-start.3) | collective-permute-done | bytes 131104 | tf_op jit(solution)/shard_map/ppermute | solution.py:356
  37.4 4.6 %collective-permute-start.5 = (bf16[256,128]{1,0:T(8,128)(2,1)S(1)}, bf16[256,128]{1,0:T(8,128)(2,1)S(1)}, u32[]{:S(2)}, u32[]{:S(2)}) collective-permute-start(bf16[256,128]{1,0:T(8,128)(2,1)S(1)} %get-tuple-element.46), channel_id=1, source_target_pairs={{24,0},{32,8},{40,16},{48,24},{56,32},{64,40},{72,48},{80,56},{88,... | collective-permute-start | bytes 196616 | tf_op jit(solution)/shard_map/ppermute | solution.py:356
  42.0 4.0 %collective-permute-start.4 = (bf16[256,128]{1,0:T(8,128)(2,1)S(1)}, bf16[256,128]{1,0:T(8,128)(2,1)S(1)}, u32[]{:S(2)}, u32[]{:S(2)}) collective-permute-start(bf16[256,128]{1,0:T(8,128)(2,1)S(1)} %get-tuple-element.45), channel_id=1, source_target_pairs={{8,0},{16,8},{24,16},{32,24},{40,32},{48,40},{56,48},{64,56},{72,6... | collective-permute-start | bytes 196616 | tf_op jit(solution)/shard_map/ppermute | solution.py:356
  46.0 1.0 %collective-permute-done.5 = bf16[256,128]{1,0:T(8,128)(2,1)S(1)} collective-permute-done((bf16[256,128]{1,0:T(8,128)(2,1)S(1)}, bf16[256,128]{1,0:T(8,128)(2,1)S(1)}, u32[]{:S(2)}, u32[]{:S(2)}) %collective-permute-start.5) | collective-permute-done | bytes 65568 | tf_op jit(solution)/shard_map/ppermute | solution.py:356
  47.1 1.1 %collective-permute-done.4 = bf16[256,128]{1,0:T(8,128)(2,1)S(1)} collective-permute-done((bf16[256,128]{1,0:T(8,128)(2,1)S(1)}, bf16[256,128]{1,0:T(8,128)(2,1)S(1)}, u32[]{:S(2)}, u32[]{:S(2)}) %collective-permute-start.4) | collective-permute-done | bytes 65568 | tf_op jit(solution)/shard_map/ppermute | solution.py:356
  48.2 0.6 %fusion.1 = (bf16[128,128]{1,0:T(8,128)(2,1)}, bf16[128,128]{1,0:T(8,128)(2,1)}) fusion(bf16[256,128]{1,0:T(8,128)(2,1)S(1)} %add_convert_fusion), kind=kLoop, calls=%fused_computation.6 | loop fusion | bytes 131072 | tf_op jit(solution)/shard_map/slice | solution.py:41
  (4 shorter events, 0.1 us)
Async XLA Ops:
  1.4 15.5 %collective-permute-start = (bf16[256,128]{1,0:T(8,128)(2,1)S(1)}, bf16[256,128]{1,0:T(8,128)(2,1)S(1)}, u32[]{:S(2)}, u32[]{:S(2)}) collective-permute-start(bf16[256,128]{1,0:T(8,128)(2,1)S(1)} %pad_maximum_fusion.1.own_ref), channel_id=1, source_target_pairs={{0,24},{8,32},{16,40},{24,48},{32,56},{40,64},{48,72},{56,80},{64,... | collective-permute-start | bytes 196616 | tf_op jit(solution)/shard_map/ppermute | solution.py:356
  7.9 11.3 %collective-permute-start.1 = (bf16[256,128]{1,0:T(8,128)(2,1)S(1)}, bf16[256,128]{1,0:T(8,128)(2,1)S(1)}, u32[]{:S(2)}, u32[]{:S(2)}) collective-permute-start(bf16[256,128]{1,0:T(8,128)(2,1)S(1)} %pad_maximum_fusion.1.own_ref), channel_id=1, source_target_pairs={{0,8},{8,16},{16,24},{24,32},{32,40},{40,48},{48,56},{56,64},{64,7... | collective-permute-start | bytes 196616 | tf_op jit(solution)/shard_map/ppermute | solution.py:356
  13.0 1.0 %copy-start = (bf16[128,2048]{1,0:T(8,128)(2,1)S(1)}, bf16[128,2048]{1,0:T(8,128)(2,1)}, u32[]{:S(2)}) copy-start(bf16[128,2048]{1,0:T(8,128)(2,1)} %all_query_ref.1) | copy-start | bytes 1572868
  14.0 1.0 %copy-start.1 = (bf16[128,2048]{1,0:T(8,128)(2,1)S(1)}, bf16[128,2048]{1,0:T(8,128)(2,1)}, u32[]{:S(2)}) copy-start(bf16[128,2048]{1,0:T(8,128)(2,1)} %all_grad_ref.1) | copy-start | bytes 1572868
  15.1 0.7 %copy-start.2 = (s32[32]{0:T(128)S(1)}, s32[32]{0:T(128)}, u32[]{:S(2)}) copy-start(s32[32]{0:T(128)} %lengths_ref.1) | copy-start | bytes 388
  19.3 9.0 %collective-permute-start.2 = (bf16[512,128]{1,0:T(8,128)(2,1)S(1)}, bf16[512,128]{1,0:T(8,128)(2,1)S(1)}, u32[]{:S(2)}, u32[]{:S(2)}) collective-permute-start(bf16[512,128]{1,0:T(8,128)(2,1)S(1)} %pad_maximum_fusion), channel_id=1, source_target_pairs={{0,8},{8,16},{16,24},{24,32},{32,40},{40,48},{48,56},{56,64},{64,7... | collective-permute-start | bytes 393224 | tf_op jit(solution)/shard_map/ppermute | solution.py:356
  30.5 6.9 %collective-permute-start.3 = (bf16[512,128]{1,0:T(8,128)(2,1)S(1)}, bf16[512,128]{1,0:T(8,128)(2,1)S(1)}, u32[]{:S(2)}, u32[]{:S(2)}) collective-permute-start(bf16[512,128]{1,0:T(8,128)(2,1)S(1)} %get-tuple-element.43), channel_id=1, source_target_pairs={{8,0},{16,8},{24,16},{32,24},{40,32},{48,40},{56,48},{64,56},{72,6... | collective-permute-start | bytes 393224 | tf_op jit(solution)/shard_map/ppermute | solution.py:356
  37.4 9.7 %collective-permute-start.5 = (bf16[256,128]{1,0:T(8,128)(2,1)S(1)}, bf16[256,128]{1,0:T(8,128)(2,1)S(1)}, u32[]{:S(2)}, u32[]{:S(2)}) collective-permute-start(bf16[256,128]{1,0:T(8,128)(2,1)S(1)} %get-tuple-element.46), channel_id=1, source_target_pairs={{24,0},{32,8},{40,16},{48,24},{56,32},{64,40},{72,48},{80,56},{88,... | collective-permute-start | bytes 196616 | tf_op jit(solution)/shard_map/ppermute | solution.py:356
  42.0 6.2 %collective-permute-start.4 = (bf16[256,128]{1,0:T(8,128)(2,1)S(1)}, bf16[256,128]{1,0:T(8,128)(2,1)S(1)}, u32[]{:S(2)}, u32[]{:S(2)}) collective-permute-start(bf16[256,128]{1,0:T(8,128)(2,1)S(1)} %get-tuple-element.45), channel_id=1, source_target_pairs={{8,0},{16,8},{24,16},{32,24},{40,32},{48,40},{56,48},{64,56},{72,6... | collective-permute-start | bytes 196616 | tf_op jit(solution)/shard_map/ppermute | solution.py:356

commit v4 on v3

v4 whole, which is shorter than its diff:
```python
import math

import jax
import jax.numpy as jnp
from jax import lax
from jax.experimental import pallas as pl
from jax.experimental.pallas import tpu as pltpu
from jax.sharding import PartitionSpec as P

HEADS = 128
KV_HEADS = 8
HEAD_DIM = 128
REACH = 4
TOK = 128
GROUP = HEADS // KV_HEADS
ROWS = GROUP * TOK
PAIR = 2
WIDE = PAIR * TOK
STEPS = GROUP // PAIR
DOCS = 32
SCALE = 1.0 / math.sqrt(HEAD_DIM)
SCALE_LOG2E = SCALE * math.log2(math.e)
MASKED = -1e30
F32 = jnp.float32
BF16 = jnp.bfloat16
NT = (((1,), (1,)), ((), ()))
NN = (((1,), (0,)), ((), ()))


def dot(a, b, dims):
    return lax.dot_general(a, b, dims, preferred_element_type=F32)


def key_of(block):
    return block[:TOK]


def value_of(block):
    return block[TOK:]


def columns(step):
    return slice(step * WIDE, (step + 1) * WIDE)


def doc_starts(lengths_ref, row):
    total = jnp.int32(0)
    starts = jnp.zeros_like(row)
    for doc in range(DOCS):
        total = total + lengths_ref[doc]
        starts = jnp.where(total <= row, total, starts)
    return starts


def positions(index_ref, lengths_ref):
    first = index_ref[0] * TOK
    query_pos = first + lax.broadcasted_iota(jnp.int32, (1, TOK), 1)
    starts = doc_starts(lengths_ref, query_pos)
    key_pos = first + lax.broadcasted_iota(jnp.int32, (TOK, TOK), 0)
    return key_pos, starts


def bias_of(key_pos, starts):
    bias = jnp.where(key_pos >= starts, 0.0, MASKED)
    return jnp.concatenate([bias] * PAIR, axis=1)


def top(x):
    return jnp.max(x, axis=0, keepdims=True)


def total(x):
    return jnp.sum(x, axis=0, keepdims=True)


def load_kernel(
    index_ref, lengths_ref, wide_query_ref, wide_grad_ref, query_ref, grad_ref, near_bias_ref, far_bias_ref
):
    key_pos, starts = positions(index_ref, lengths_ref)
    row = lax.broadcasted_iota(jnp.int32, (TOK, WIDE), 0)
    lane = lax.broadcasted_iota(jnp.int32, (TOK, WIDE), 1)
    near_bias_ref[:TOK, :] = bias_of(key_pos - TOK, starts)
    near_bias_ref[TOK : 2 * TOK, :] = bias_of(key_pos - 3 * TOK, starts)
    near_bias_ref[2 * TOK :, :] = jnp.where(row <= lax.rem(lane, TOK), bias_of(key_pos, starts), MASKED)
    far_bias_ref[:TOK, :] = bias_of(key_pos - 2 * TOK, starts)
    far_bias_ref[TOK:, :] = bias_of(key_pos - 4 * TOK, starts)
    for head in range(GROUP):
        there, here = slice(head * HEAD_DIM, (head + 1) * HEAD_DIM), slice(head * TOK, (head + 1) * TOK)
        query_ref[here, :] = wide_query_ref[:, there]
        grad_ref[here, :] = wide_grad_ref[:, there]


def near_kernel(bias_ref, query_ref, grad_ref, one_ref, three_ref, own_ref, weight_ref, dprob_ref, stat_ref):
    blocks = (one_ref, three_ref, own_ref)
    keys = jnp.concatenate([key_of(block) for block in blocks], axis=0)
    values = jnp.concatenate([value_of(block) for block in blocks], axis=0)
    for step in range(STEPS):
        at = columns(step)
        scores = dot(keys, query_ref[at, :], NT) * SCALE_LOG2E + bias_ref[...]
        dprobs = dot(values, grad_ref[at, :], NT)
        peak = top(scores)
        weights = jnp.exp2(scores - peak)
        weight_ref[:, at] = weights
        dprob_ref[:, at] = dprobs
        stat_ref[0:1, at] = peak
        stat_ref[1:2, at] = total(weights)
        stat_ref[2:3, at] = total(weights * dprobs)


def far_kernel(
    bias_ref, query_ref, grad_ref, near_stat_ref, two_ref, four_ref, sums_ref, dscore_ref, stat_ref, prob_ref
):
    keys = jnp.concatenate([key_of(two_ref), key_of(four_ref)], axis=0)
    values = jnp.concatenate([value_of(two_ref), value_of(four_ref)], axis=0)
    halves = (slice(0, TOK), slice(TOK, 2 * TOK))
    for step in range(STEPS):
        at = columns(step)
        fresh_scores = dot(keys, query_ref[at, :], NT)
        fresh_dprobs = dot(values, grad_ref[at, :], NT)
        peaks, weights, dprobs, totals, products = [], [], [], [], []
        for rows in halves:
            scores, dprob = fresh_scores[rows] * SCALE_LOG2E + bias_ref[rows, :], fresh_dprobs[rows]
            peak = top(scores)
            weight = jnp.exp2(scores - peak)
            peaks.append(peak)
            weights.append(weight)
            dprobs.append(dprob)
            totals.append(total(weight))
            products.append(total(weight * dprob))
        near_peak = near_stat_ref[0:1, at]
        peak = jnp.maximum(jnp.maximum(peaks[0], peaks[1]), near_peak)
        near_factor = jnp.exp2(near_peak - peak)
        factors = [jnp.exp2(part - peak) for part in peaks]
        inverse = 1.0 / (totals[0] * factors[0] + totals[1] * factors[1] + near_stat_ref[1:2, at] * near_factor)
        delta = products[0] * factors[0] + products[1] * factors[1] + near_stat_ref[2:3, at] * near_factor
        delta = delta * inverse
        stat_ref[0:1, at] = near_factor * inverse
        stat_ref[1:2, at] = delta
        for rows, weight, dprob, factor in zip(halves, weights, dprobs, factors):
            probs = weight * (factor * inverse)
            prob_ref[rows, at] = probs.astype(BF16)
            dscore_ref[rows, at] = (probs * (dprob - delta)).astype(BF16)
    keys = (dot(dscore_ref[...], query_ref[...], NN) * SCALE).astype(BF16)
    values = dot(prob_ref[...], grad_ref[...], NN).astype(BF16)
    for at, rows in enumerate(halves):
        sums_ref[2 * at * TOK : (2 * at + 1) * TOK] = keys[rows]
        sums_ref[(2 * at + 1) * TOK : (2 * at + 2) * TOK] = values[rows]


def rest_kernel(
    query_ref,
    grad_ref,
    weight_ref,
    dprob_ref,
    stat_ref,
    far_dscore_ref,
    one_ref,
    two_ref,
    three_ref,
    four_ref,
    own_ref,
    grad_query_hbm,
    one_sums_ref,
    three_sums_ref,
    own_sums_ref,
    prob_ref,
    dscore_ref,
    grad_query_ref,
    out_sems,
):
    far_keys = jnp.concatenate([key_of(two_ref), key_of(four_ref)], axis=0).T
    near_keys = jnp.concatenate([key_of(one_ref), key_of(three_ref), key_of(own_ref)], axis=0).T

    def out_copy(step):
        at = pl.ds(step * WIDE, WIDE)
        return pltpu.make_async_copy(grad_query_ref.at[:, at], grad_query_hbm.at[:, at], out_sems.at[step])

    for step in range(STEPS):
        at = columns(step)
        probs = weight_ref[:, at] * stat_ref[0:1, at]
        dscores = (probs * (dprob_ref[:, at] - stat_ref[1:2, at])).astype(BF16)
        prob_ref[:, at] = probs.astype(BF16)
        dscore_ref[:, at] = dscores
        grad_query = dot(far_keys, far_dscore_ref[:, at], NN) + dot(near_keys, dscores, NN)
        grad_query = (grad_query * SCALE).T.astype(BF16)
        for h in range(PAIR):
            head = slice((step * PAIR + h) * HEAD_DIM, (step * PAIR + h + 1) * HEAD_DIM)
            grad_query_ref[:, head] = grad_query[h * TOK : (h + 1) * TOK]
        out_copy(step).start()
    keys = dot(dscore_ref[...], query_ref[...], NN) * SCALE
    values = dot(prob_ref[...], grad_ref[...], NN)
    for at, sums_ref in enumerate((one_sums_ref, three_sums_ref, own_sums_ref)):
        rows = slice(at * TOK, (at + 1) * TOK)
        sums_ref[:TOK] = keys[rows]
        sums_ref[TOK:] = values[rows]
    for step in range(STEPS):
        out_copy(step).wait()


WHOLE = pl.BlockSpec(memory_space=pltpu.VMEM)
SCALARS = pl.BlockSpec(memory_space=pltpu.SMEM)
FAR = pl.BlockSpec(memory_space=pl.ANY)


def call(kernel, name, flops, in_specs, outs, scratch, *args):
    return pl.pallas_call(
        kernel,
        out_shape=[jax.ShapeDtypeStruct(shape, dtype) for shape, dtype, _ in outs],
        in_specs=in_specs,
        out_specs=[spec for _, _, spec in outs],
        scratch_shapes=scratch,
        compiler_params=pltpu.CompilerParams(vmem_limit_bytes=16 * 1024 * 1024),
        cost_estimate=pl.CostEstimate(flops=flops, bytes_accessed=10**6, transcendentals=10**5),
        name=name,
    )(*args)


STACKED = ((ROWS, HEAD_DIM), BF16, WHOLE)
STATS = ((8, ROWS), F32, WHOLE)


def scores_of(blocks, dtype):
    return ((blocks * TOK, ROWS), dtype, WHOLE)


def load(*args):
    outs = [STACKED] * 2 + [((blocks * TOK, WIDE), F32, WHOLE) for blocks in (3, 2)]
    return call(load_kernel, "load", 2 * 10**8, [SCALARS] * 2 + [WHOLE] * 2, outs, [], *args)


def near_part(*args):
    return call(near_kernel, "near_part", 4 * 10**8, [WHOLE] * 6, [scores_of(3, F32)] * 2 + [STATS], [], *args)


def far_part(*args):
    outs = [((4 * TOK, HEAD_DIM), BF16, WHOLE), scores_of(2, BF16), STATS]
    scratch = [pltpu.VMEM((2 * TOK, ROWS), BF16)]
    return call(far_kernel, "far_part", 6 * 10**8, [WHOLE] * 6, outs, scratch, *args)


def rest_part(*args):
    outs = [((TOK, GROUP * HEAD_DIM), BF16, FAR)] + [((2 * TOK, HEAD_DIM), F32, WHOLE)] * 3
    scratch = [
        pltpu.VMEM((3 * TOK, ROWS), BF16),
        pltpu.VMEM((3 * TOK, ROWS), BF16),
        pltpu.VMEM((TOK, GROUP * HEAD_DIM), BF16),
        pltpu.SemaphoreType.DMA((STEPS,)),
    ]
    return call(rest_kernel, "rest_part", 8 * 10**8, [WHOLE] * 11, outs, scratch, *args)


def passed_along(array, by):
    devices = lax.axis_size("ctx")
    pairs = [(i, i + by) for i in range(devices) if 0 <= i + by < devices]
    return lax.ppermute(array, "ctx", pairs)


def local(queries, keys, values, grad_out, doc_lengths):
    index = lax.axis_index("ctx").astype(jnp.int32).reshape(1)
    low = jnp.array(-jnp.inf, BF16)
    own = lax.max(
        lax.pad(keys, low, ((0, TOK, 0), (0, 0, 0))), lax.pad(values, low, ((TOK, 0, 0), (0, 0, 0)))
    )
    three = passed_along(own, 3)
    one = passed_along(own, 1)
    query, grad, near_bias, far_bias = load(index, doc_lengths, queries, grad_out)
    one, three, far_bias = lax.optimization_barrier((one, three, far_bias))
    far = passed_along(jnp.concatenate([one, three], axis=0), 1)
    weight, dprob, near_stat = near_part(near_bias, query, grad, one, three, own)
    two, four = far[: 2 * TOK], far[2 * TOK :]
    far_sums, far_dscore, stat = far_part(far_bias, query, grad, near_stat, two, four)
    far_sums = passed_along(far_sums, -1)
    grad_q, one_sums, three_sums, own_sums = rest_part(
        query, grad, weight, dprob, stat, far_dscore, one, two, three, four, own
    )
    three_sums = (three_sums + far_sums[2 * TOK :].astype(F32)).astype(BF16)
    one_sums = (one_sums + far_sums[: 2 * TOK].astype(F32)).astype(BF16)
    three_sums = passed_along(three_sums, -3)
    one_sums = passed_along(one_sums, -1)
    sums = (own_sums + three_sums.astype(F32) + one_sums.astype(F32)).astype(BF16)
    return (grad_q, key_of(sums), value_of(sums))


def solution(mesh):
    placed = (P("ctx", "tp"), P("ctx", "tp"), P("ctx", "tp"), P("ctx", "tp"), P())
    return jax.shard_map(
        local,
        mesh=mesh,
        in_specs=placed,
        out_specs=(P("ctx", "tp"), P("ctx", "tp"), P("ctx", "tp")),
        check_vma=False,
    )
```

time: 49.2 us -> 48.9 us (level)
  no operation moved by 1% of the time
where the time goes in v4:
time: 48.9 us; the launch traced here: 48.4 us
  starting transfers between devices  24.5 us (50%)
  waiting for transfers between devices  12.8 us (26%)
  Pallas kernels  6.17 us (13%)
  local copies, waits for them, and re-layouts  3.37 us (7%)
  other arithmetic  0.85 us (2%)
  between operations  0.74 us (2%)
    ppermute x6, starting transfers between devices, passed_along(): return lax.ppermute(array, 'ctx', pairs)  24.5 us
    ppermute x6, waiting for transfers between devices, passed_along(): return lax.ppermute(array, 'ctx', pairs)  12.8 us
    pallas_call x4, Pallas kernels, call(): pl.pallas_call(kernel, out_shape=[jax.ShapeDtypeStruct(shape, dtype) for...  6.17 us
    unnamed x6, local copies, waits for them, and re-layouts  2.73 us
  transfers between devices with their start and end apart: 6, of which 5 were waited for; matrix products, arithmetic and copies ran while one was open for 0% of the time, Pallas kernels for 9%

profile of v4, /device:TPU:24, one launch (start us, length us, event | category | flops | bytes accessed | tf_op | source)
XLA Modules:
  0.0 48.4 jit_solution(15258109149953084935)
XLA Ops:
  0.6 0.8 %pad_maximum_fusion.1.own_ref = bf16[256,128]{1,0:T(8,128)(2,1)S(1)} fusion(bf16[128,128]{1,0:T(8,128)(2,1)} %param.7, bf16[128,128]{1,0:T(8,128)(2,1)} %param.6), kind=kLoop, calls=%fused_computation.4 | loop fusion | flops 131072 | bytes 131072 | tf_op jit(solution)/shard_map/max | solution.py:261
  1.4 6.5 %collective-permute-start.1 = (bf16[256,128]{1,0:T(8,128)(2,1)S(1)}, bf16[256,128]{1,0:T(8,128)(2,1)S(1)}, u32[]{:S(2)}, u32[]{:S(2)}) collective-permute-start(bf16[256,128]{1,0:T(8,128)(2,1)S(1)} %pad_maximum_fusion.1.own_ref), channel_id=1, source_target_pairs={{0,24},{8,32},{16,40},{24,48},{32,56},{40,64},{48,72},{56,80},{64,... | collective-permute-start | bytes 196616 | tf_op jit(solution)/shard_map/ppermute | solution.py:255
  7.9 5.0 %collective-permute-start = (bf16[256,128]{1,0:T(8,128)(2,1)S(1)}, bf16[256,128]{1,0:T(8,128)(2,1)S(1)}, u32[]{:S(2)}, u32[]{:S(2)}) collective-permute-start(bf16[256,128]{1,0:T(8,128)(2,1)S(1)} %pad_maximum_fusion.1.own_ref), channel_id=1, source_target_pairs={{0,8},{8,16},{16,24},{24,32},{32,40},{40,48},{48,56},{56,64},{64,7... | collective-permute-start | bytes 196616 | tf_op jit(solution)/shard_map/ppermute | solution.py:255
  13.0 0.0 copy-start
  13.0 1.0 %copy-done = bf16[128,2048]{1,0:T(8,128)(2,1)S(1)} copy-done((bf16[128,2048]{1,0:T(8,128)(2,1)S(1)}, bf16[128,2048]{1,0:T(8,128)(2,1)}, u32[]{:S(2)}) %copy-start) | copy-done | bytes 524312
  14.0 0.0 copy-start.1
  14.0 1.0 %copy-done.1 = bf16[128,2048]{1,0:T(8,128)(2,1)S(1)} copy-done((bf16[128,2048]{1,0:T(8,128)(2,1)S(1)}, bf16[128,2048]{1,0:T(8,128)(2,1)}, u32[]{:S(2)}) %copy-start.1) | copy-done | bytes 524312
  15.1 0.0 copy-start.2
  15.1 0.7 %copy-done.2 = s32[32]{0:T(128)S(1)} copy-done((s32[32]{0:T(128)S(1)}, s32[32]{0:T(128)}, u32[]{:S(2)}) %copy-start.2) | copy-done | bytes 152
  15.7 0.8 %load.1 = (bf16[2048,128]{1,0:T(8,128)(2,1)S(1)}, bf16[2048,128]{1,0:T(8,128)(2,1)S(1)}, f32[384,256]{1,0:T(8,128)S(1)}, f32[256,256]{1,0:T(8,128)S(1)}) custom-call(s32[1]{0:T(128)} %bitcast.index_ref, s32[32]{0:T(128)S(1)} %copy-done.2, bf16[128,2048]{1,0:T(8,128)(2,1)S(1)} %copy-done, bf16[128,2048]{1,0:T(8,128)(2,1)S(1)} %copy-done.1), custom_call_target="tpu_custom_call" | custom-call | flops 200000000 | bytes 1000000 | tf_op jit(solution)/shard_map/load/pallas_call | solution.py:206
  16.5 0.0 collective-permute-done.1.three_ref
  16.5 2.8 %collective-permute-done.one_ref = bf16[256,128]{1,0:T(8,128)(2,1)S(1)} collective-permute-done((bf16[256,128]{1,0:T(8,128)(2,1)S(1)}, bf16[256,128]{1,0:T(8,128)(2,1)S(1)}, u32[]{:S(2)}, u32[]{:S(2)}) %collective-permute-start) | collective-permute-done | bytes 65568 | tf_op jit(solution)/shard_map/ppermute | solution.py:255
  19.3 2.4 %collective-permute-start.2 = (bf16[512,128]{1,0:T(8,128)(2,1)S(1)}, bf16[512,128]{1,0:T(8,128)(2,1)S(1)}, u32[]{:S(2)}, u32[]{:S(2)}) collective-permute-start(bf16[512,128]{1,0:T(8,128)(2,1)S(1)} %pad_maximum_fusion), channel_id=1, source_target_pairs={{0,8},{8,16},{16,24},{24,32},{32,40},{40,48},{48,56},{56,64},{64,7... | collective-permute-start | bytes 393224 | tf_op jit(solution)/shard_map/ppermute | solution.py:255
  21.7 1.4 %near_part.1 = (f32[384,2048]{1,0:T(8,128)S(1)}, f32[384,2048]{1,0:T(8,128)S(1)}, f32[8,2048]{1,0:T(8,128)S(1)}) custom-call(f32[384,256]{1,0:T(8,128)S(1)} %get-tuple-element.22.bias_ref, bf16[2048,128]{1,0:T(8,128)(2,1)S(1)} %get-tuple-element.20.query_ref, bf16[2048,128]{1,0:T(8,128)(2,1)S(1)} %get-tuple-element.21.grad_ref, ...), custom_call_target="tpu_custom_call" | custom-call | flops 400000000 | bytes 1000000 | tf_op jit(solution)/shard_map/near_part/pallas_call | solution.py:206
  23.0 5.3 %collective-permute-done.2 = bf16[512,128]{1,0:T(8,128)(2,1)S(1)} collective-permute-done((bf16[512,128]{1,0:T(8,128)(2,1)S(1)}, bf16[512,128]{1,0:T(8,128)(2,1)S(1)}, u32[]{:S(2)}, u32[]{:S(2)}) %collective-permute-start.2) | collective-permute-done | bytes 131104 | tf_op jit(solution)/shard_map/ppermute | solution.py:255
  28.3 1.8 %far_part.1 = (bf16[512,128]{1,0:T(8,128)(2,1)S(1)}, bf16[256,2048]{1,0:T(8,128)(2,1)S(1)}, f32[8,2048]{1,0:T(8,128)S(1)}) custom-call(f32[256,256]{1,0:T(8,128)S(1)} %get-tuple-element.28.bias_ref, bf16[2048,128]{1,0:T(8,128)(2,1)S(1)} %get-tuple-element.20.query_ref, bf16[2048,128]{1,0:T(8,128)(2,1)S(1)} %get-tuple-element.21.grad_ref, ...), custom_call_target="tpu_custom_call" | custom-call | flops 600000000 | bytes 1000000 | tf_op jit(solution)/shard_map/far_part/pallas_call | solution.py:206
  30.1 1.9 %collective-permute-start.3 = (bf16[512,128]{1,0:T(8,128)(2,1)S(1)}, bf16[512,128]{1,0:T(8,128)(2,1)S(1)}, u32[]{:S(2)}, u32[]{:S(2)}) collective-permute-start(bf16[512,128]{1,0:T(8,128)(2,1)S(1)} %get-tuple-element.35), channel_id=1, source_target_pairs={{8,0},{16,8},{24,16},{32,24},{40,32},{48,40},{56,48},{64,56},{72,6... | collective-permute-start | bytes 393224 | tf_op jit(solution)/shard_map/ppermute | solution.py:255
  32.0 2.2 %rest_part.1 = (bf16[128,2048]{1,0:T(8,128)(2,1)}, f32[256,128]{1,0:T(8,128)S(1)}, f32[256,128]{1,0:T(8,128)S(1)}, f32[256,128]{1,0:T(8,128)S(1)}) custom-call(bf16[2048,128]{1,0:T(8,128)(2,1)S(1)} %get-tuple-element.20.query_ref, bf16[2048,128]{1,0:T(8,128)(2,1)S(1)} %get-tuple-element.21.grad_ref, f32[384,2048]{1,0:T(8,128)S(1)} %get-tuple-element.26.weight_ref, ...), custom_call_target="tpu_custom_call" | custom-call | flops 800000000 | bytes 1000000 | tf_op jit(solution)/shard_map/rest_part/pallas_call | solution.py:206
  34.3 2.7 %collective-permute-done.3 = bf16[512,128]{1,0:T(8,128)(2,1)S(1)} collective-permute-done((bf16[512,128]{1,0:T(8,128)(2,1)S(1)}, bf16[512,128]{1,0:T(8,128)(2,1)S(1)}, u32[]{:S(2)}, u32[]{:S(2)}) %collective-permute-start.3) | collective-permute-done | bytes 131104 | tf_op jit(solution)/shard_map/ppermute | solution.py:255
  37.0 4.6 %collective-permute-start.4 = (bf16[256,128]{1,0:T(8,128)(2,1)S(1)}, bf16[256,128]{1,0:T(8,128)(2,1)S(1)}, u32[]{:S(2)}, u32[]{:S(2)}) collective-permute-start(bf16[256,128]{1,0:T(8,128)(2,1)S(1)} %get-tuple-element.37), channel_id=1, source_target_pairs={{24,0},{32,8},{40,16},{48,24},{56,32},{64,40},{72,48},{80,56},{88,... | collective-permute-start | bytes 196616 | tf_op jit(solution)/shard_map/ppermute | solution.py:255
  41.6 4.0 %collective-permute-start.5 = (bf16[256,128]{1,0:T(8,128)(2,1)S(1)}, bf16[256,128]{1,0:T(8,128)(2,1)S(1)}, u32[]{:S(2)}, u32[]{:S(2)}) collective-permute-start(bf16[256,128]{1,0:T(8,128)(2,1)S(1)} %get-tuple-element.38), channel_id=1, source_target_pairs={{8,0},{16,8},{24,16},{32,24},{40,32},{48,40},{56,48},{64,56},{72,6... | collective-permute-start | bytes 196616 | tf_op jit(solution)/shard_map/ppermute | solution.py:255
  45.7 1.2 %collective-permute-done.4 = bf16[256,128]{1,0:T(8,128)(2,1)S(1)} collective-permute-done((bf16[256,128]{1,0:T(8,128)(2,1)S(1)}, bf16[256,128]{1,0:T(8,128)(2,1)S(1)}, u32[]{:S(2)}, u32[]{:S(2)}) %collective-permute-start.4) | collective-permute-done | bytes 65568 | tf_op jit(solution)/shard_map/ppermute | solution.py:255
  46.8 0.9 %collective-permute-done.5 = bf16[256,128]{1,0:T(8,128)(2,1)S(1)} collective-permute-done((bf16[256,128]{1,0:T(8,128)(2,1)S(1)}, bf16[256,128]{1,0:T(8,128)(2,1)S(1)}, u32[]{:S(2)}, u32[]{:S(2)}) %collective-permute-start.5) | collective-permute-done | bytes 65568 | tf_op jit(solution)/shard_map/ppermute | solution.py:255
  47.8 0.6 %fusion.1 = (bf16[128,128]{1,0:T(8,128)(2,1)}, bf16[128,128]{1,0:T(8,128)(2,1)}) fusion(bf16[256,128]{1,0:T(8,128)(2,1)S(1)} %add_convert_fusion), kind=kLoop, calls=%fused_computation.6 | loop fusion | bytes 131072 | tf_op jit(solution)/shard_map/slice | solution.py:39
  (4 shorter events, 0.1 us)
Async XLA Ops:
  1.4 15.1 %collective-permute-start.1 = (bf16[256,128]{1,0:T(8,128)(2,1)S(1)}, bf16[256,128]{1,0:T(8,128)(2,1)S(1)}, u32[]{:S(2)}, u32[]{:S(2)}) collective-permute-start(bf16[256,128]{1,0:T(8,128)(2,1)S(1)} %pad_maximum_fusion.1.own_ref), channel_id=1, source_target_pairs={{0,24},{8,32},{16,40},{24,48},{32,56},{40,64},{48,72},{56,80},{64,... | collective-permute-start | bytes 196616 | tf_op jit(solution)/shard_map/ppermute | solution.py:255
  7.9 11.3 %collective-permute-start = (bf16[256,128]{1,0:T(8,128)(2,1)S(1)}, bf16[256,128]{1,0:T(8,128)(2,1)S(1)}, u32[]{:S(2)}, u32[]{:S(2)}) collective-permute-start(bf16[256,128]{1,0:T(8,128)(2,1)S(1)} %pad_maximum_fusion.1.own_ref), channel_id=1, source_target_pairs={{0,8},{8,16},{16,24},{24,32},{32,40},{40,48},{48,56},{56,64},{64,7... | collective-permute-start | bytes 196616 | tf_op jit(solution)/shard_map/ppermute | solution.py:255
  13.0 1.0 %copy-start = (bf16[128,2048]{1,0:T(8,128)(2,1)S(1)}, bf16[128,2048]{1,0:T(8,128)(2,1)}, u32[]{:S(2)}) copy-start(bf16[128,2048]{1,0:T(8,128)(2,1)} %wide_query_ref.1) | copy-start | bytes 1572868
  14.0 1.0 %copy-start.1 = (bf16[128,2048]{1,0:T(8,128)(2,1)S(1)}, bf16[128,2048]{1,0:T(8,128)(2,1)}, u32[]{:S(2)}) copy-start(bf16[128,2048]{1,0:T(8,128)(2,1)} %wide_grad_ref.1) | copy-start | bytes 1572868
  15.1 0.7 %copy-start.2 = (s32[32]{0:T(128)S(1)}, s32[32]{0:T(128)}, u32[]{:S(2)}) copy-start(s32[32]{0:T(128)} %lengths_ref.1) | copy-start | bytes 388
  19.3 9.0 %collective-permute-start.2 = (bf16[512,128]{1,0:T(8,128)(2,1)S(1)}, bf16[512,128]{1,0:T(8,128)(2,1)S(1)}, u32[]{:S(2)}, u32[]{:S(2)}) collective-permute-start(bf16[512,128]{1,0:T(8,128)(2,1)S(1)} %pad_maximum_fusion), channel_id=1, source_target_pairs={{0,8},{8,16},{16,24},{24,32},{32,40},{40,48},{48,56},{56,64},{64,7... | collective-permute-start | bytes 393224 | tf_op jit(solution)/shard_map/ppermute | solution.py:255
  30.1 6.9 %collective-permute-start.3 = (bf16[512,128]{1,0:T(8,128)(2,1)S(1)}, bf16[512,128]{1,0:T(8,128)(2,1)S(1)}, u32[]{:S(2)}, u32[]{:S(2)}) collective-permute-start(bf16[512,128]{1,0:T(8,128)(2,1)S(1)} %get-tuple-element.35), channel_id=1, source_target_pairs={{8,0},{16,8},{24,16},{32,24},{40,32},{48,40},{56,48},{64,56},{72,6... | collective-permute-start | bytes 393224 | tf_op jit(solution)/shard_map/ppermute | solution.py:255
  37.0 9.8 %collective-permute-start.4 = (bf16[256,128]{1,0:T(8,128)(2,1)S(1)}, bf16[256,128]{1,0:T(8,128)(2,1)S(1)}, u32[]{:S(2)}, u32[]{:S(2)}) collective-permute-start(bf16[256,128]{1,0:T(8,128)(2,1)S(1)} %get-tuple-element.37), channel_id=1, source_target_pairs={{24,0},{32,8},{40,16},{48,24},{56,32},{64,40},{72,48},{80,56},{88,... | collective-permute-start | bytes 196616 | tf_op jit(solution)/shard_map/ppermute | solution.py:255
  41.6 6.2 %collective-permute-start.5 = (bf16[256,128]{1,0:T(8,128)(2,1)S(1)}, bf16[256,128]{1,0:T(8,128)(2,1)S(1)}, u32[]{:S(2)}, u32[]{:S(2)}) collective-permute-start(bf16[256,128]{1,0:T(8,128)(2,1)S(1)} %get-tuple-element.38), channel_id=1, source_target_pairs={{8,0},{16,8},{24,16},{32,24},{40,32},{48,40},{56,48},{64,56},{72,6... | collective-permute-start | bytes 196616 | tf_op jit(solution)/shard_map/ppermute | solution.py:255

commit v5 on v4

--- a/solution.py
+++ b/solution.py
@@ -73,25 +73,30 @@
     return jnp.sum(x, axis=0, keepdims=True)
 
 
+def hold_kernel(block_ref, out_ref):
+    out_ref[...] = block_ref[...]
+
+
 def load_kernel(
     index_ref, lengths_ref, wide_query_ref, wide_grad_ref, query_ref, grad_ref, near_bias_ref, far_bias_ref
 ):
     key_pos, starts = positions(index_ref, lengths_ref)
     row = lax.broadcasted_iota(jnp.int32, (TOK, WIDE), 0)
     lane = lax.broadcasted_iota(jnp.int32, (TOK, WIDE), 1)
-    near_bias_ref[:TOK, :] = bias_of(key_pos - TOK, starts)
-    near_bias_ref[TOK : 2 * TOK, :] = bias_of(key_pos - 3 * TOK, starts)
-    near_bias_ref[2 * TOK :, :] = jnp.where(row <= lax.rem(lane, TOK), bias_of(key_pos, starts), MASKED)
-    far_bias_ref[:TOK, :] = bias_of(key_pos - 2 * TOK, starts)
-    far_bias_ref[TOK:, :] = bias_of(key_pos - 4 * TOK, starts)
+    for at, back in enumerate((2, 1, 3)):
+        near_bias_ref[at * TOK : (at + 1) * TOK, :] = bias_of(key_pos - back * TOK, starts)
+    near_bias_ref[3 * TOK :, :] = jnp.where(row <= lax.rem(lane, TOK), bias_of(key_pos, starts), MASKED)
+    far_bias_ref[...] = bias_of(key_pos - 4 * TOK, starts)
     for head in range(GROUP):
         there, here = slice(head * HEAD_DIM, (head + 1) * HEAD_DIM), slice(head * TOK, (head + 1) * TOK)
         query_ref[here, :] = wide_query_ref[:, there]
         grad_ref[here, :] = wide_grad_ref[:, there]
 
 
-def near_kernel(bias_ref, query_ref, grad_ref, one_ref, three_ref, own_ref, weight_ref, dprob_ref, stat_ref):
-    blocks = (one_ref, three_ref, own_ref)
+def near_kernel(
+    bias_ref, query_ref, grad_ref, two_ref, one_ref, three_ref, own_ref, weight_ref, dprob_ref, stat_ref
+):
+    blocks = (two_ref, one_ref, three_ref, own_ref)
     keys = jnp.concatenate([key_of(block) for block in blocks], axis=0)
     values = jnp.concatenate([value_of(block) for block in blocks], axis=0)
     for step in range(STEPS):
@@ -108,41 +113,41 @@
 
 
 def far_kernel(
-    bias_ref, query_ref, grad_ref, near_stat_ref, two_ref, four_ref, sums_ref, dscore_ref, stat_ref, prob_ref
+    bias_ref,
+    query_ref,
+    grad_ref,
+    near_weight_ref,
+    near_dprob_ref,
+    near_stat_ref,
+    four_ref,
+    sums_ref,
+    dscore_ref,
+    stat_ref,
+    prob_ref,
 ):
-    keys = jnp.concatenate([key_of(two_ref), key_of(four_ref)], axis=0)
-    values = jnp.concatenate([value_of(two_ref), value_of(four_ref)], axis=0)
-    halves = (slice(0, TOK), slice(TOK, 2 * TOK))
+    two, four = slice(0, TOK), slice(TOK, 2 * TOK)
     for step in range(STEPS):
         at = columns(step)
-        fresh_scores = dot(keys, query_ref[at, :], NT)
-        fresh_dprobs = dot(values, grad_ref[at, :], NT)
-        peaks, weights, dprobs, totals, products = [], [], [], [], []
-        for rows in halves:
-            scores, dprob = fresh_scores[rows] * SCALE_LOG2E + bias_ref[rows, :], fresh_dprobs[rows]
-            peak = top(scores)
-            weight = jnp.exp2(scores - peak)
-            peaks.append(peak)
-            weights.append(weight)
-            dprobs.append(dprob)
-            totals.append(total(weight))
-            products.append(total(weight * dprob))
+        scores = dot(key_of(four_ref), query_ref[at, :], NT) * SCALE_LOG2E + bias_ref[...]
+        dprobs = dot(value_of(four_ref), grad_ref[at, :], NT)
         near_peak = near_stat_ref[0:1, at]
-        peak = jnp.maximum(jnp.maximum(peaks[0], peaks[1]), near_peak)
+        peak = jnp.maximum(top(scores), near_peak)
+        weights = jnp.exp2(scores - peak)
         near_factor = jnp.exp2(near_peak - peak)
-        factors = [jnp.exp2(part - peak) for part in peaks]
-        inverse = 1.0 / (totals[0] * factors[0] + totals[1] * factors[1] + near_stat_ref[1:2, at] * near_factor)
-        delta = products[0] * factors[0] + products[1] * factors[1] + near_stat_ref[2:3, at] * near_factor
-        delta = delta * inverse
-        stat_ref[0:1, at] = near_factor * inverse
+        inverse = 1.0 / (total(weights) + near_stat_ref[1:2, at] * near_factor)
+        delta = (total(weights * dprobs) + near_stat_ref[2:3, at] * near_factor) * inverse
+        near_factor = near_factor * inverse
+        stat_ref[0:1, at] = near_factor
         stat_ref[1:2, at] = delta
-        for rows, weight, dprob, factor in zip(halves, weights, dprobs, factors):
-            probs = weight * (factor * inverse)
-            prob_ref[rows, at] = probs.astype(BF16)
-            dscore_ref[rows, at] = (probs * (dprob - delta)).astype(BF16)
+        probs = near_weight_ref[two, at] * near_factor
+        prob_ref[two, at] = probs.astype(BF16)
+        dscore_ref[two, at] = (probs * (near_dprob_ref[two, at] - delta)).astype(BF16)
+        probs = weights * inverse
+        prob_ref[four, at] = probs.astype(BF16)
+        dscore_ref[four, at] = (probs * (dprobs - delta)).astype(BF16)
     keys = (dot(dscore_ref[...], query_ref[...], NN) * SCALE).astype(BF16)
     values = dot(prob_ref[...], grad_ref[...], NN).astype(BF16)
-    for at, rows in enumerate(halves):
+    for at, rows in enumerate((two, four)):
         sums_ref[2 * at * TOK : (2 * at + 1) * TOK] = keys[rows]
         sums_ref[(2 * at + 1) * TOK : (2 * at + 2) * TOK] = values[rows]
 
@@ -177,8 +182,8 @@
 
     for step in range(STEPS):
         at = columns(step)
-        probs = weight_ref[:, at] * stat_ref[0:1, at]
-        dscores = (probs * (dprob_ref[:, at] - stat_ref[1:2, at])).astype(BF16)
+        probs = weight_ref[TOK:, at] * stat_ref[0:1, at]
+        dscores = (probs * (dprob_ref[TOK:, at] - stat_ref[1:2, at])).astype(BF16)
         prob_ref[:, at] = probs.astype(BF16)
         dscore_ref[:, at] = dscores
         grad_query = dot(far_keys, far_dscore_ref[:, at], NN) + dot(near_keys, dscores, NN)
@@ -223,19 +228,23 @@
     return ((blocks * TOK, ROWS), dtype, WHOLE)
 
 
+def hold(block):
+    return call(hold_kernel, "hold_part", 10**10, [WHOLE], [((2 * TOK, HEAD_DIM), BF16, WHOLE)], [], block)[0]
+
+
 def load(*args):
-    outs = [STACKED] * 2 + [((blocks * TOK, WIDE), F32, WHOLE) for blocks in (3, 2)]
+    outs = [STACKED] * 2 + [((blocks * TOK, WIDE), F32, WHOLE) for blocks in (4, 1)]
     return call(load_kernel, "load", 2 * 10**8, [SCALARS] * 2 + [WHOLE] * 2, outs, [], *args)
 
 
 def near_part(*args):
-    return call(near_kernel, "near_part", 4 * 10**8, [WHOLE] * 6, [scores_of(3, F32)] * 2 + [STATS], [], *args)
+    return call(near_kernel, "near_part", 5 * 10**8, [WHOLE] * 7, [scores_of(4, F32)] * 2 + [STATS], [], *args)
 
 
 def far_part(*args):
     outs = [((4 * TOK, HEAD_DIM), BF16, WHOLE), scores_of(2, BF16), STATS]
     scratch = [pltpu.VMEM((2 * TOK, ROWS), BF16)]
-    return call(far_kernel, "far_part", 6 * 10**8, [WHOLE] * 6, outs, scratch, *args)
+    return call(far_kernel, "far_part", 6 * 10**8, [WHOLE] * 7, outs, scratch, *args)
 
 
 def rest_part(*args):
@@ -261,14 +270,14 @@
     own = lax.max(
         lax.pad(keys, low, ((0, TOK, 0), (0, 0, 0))), lax.pad(values, low, ((TOK, 0, 0), (0, 0, 0)))
     )
+    own = hold(own)
     three = passed_along(own, 3)
     one = passed_along(own, 1)
+    two = passed_along(own, 2)
     query, grad, near_bias, far_bias = load(index, doc_lengths, queries, grad_out)
-    one, three, far_bias = lax.optimization_barrier((one, three, far_bias))
-    far = passed_along(jnp.concatenate([one, three], axis=0), 1)
-    weight, dprob, near_stat = near_part(near_bias, query, grad, one, three, own)
-    two, four = far[: 2 * TOK], far[2 * TOK :]
-    far_sums, far_dscore, stat = far_part(far_bias, query, grad, near_stat, two, four)
+    four = passed_along(three, 1)
+    weight, dprob, near_stat = near_part(near_bias, query, grad, two, one, three, own)
+    far_sums, far_dscore, stat = far_part(far_bias, query, grad, weight, dprob, near_stat, four)
     far_sums = passed_along(far_sums, -1)
     grad_q, one_sums, three_sums, own_sums = rest_part(
         query, grad, weight, dprob, stat, far_dscore, one, two, three, four, own

time: 48.9 us -> 47.8 us (0.978)
  starting transfers between devices: 24.5 us -> 32.5 us
  waiting for transfers between devices: 12.8 us -> 6.26 us
  local copies, waits for them, and re-layouts: 3.37 us -> 0.64 us
    ppermute x6 -> x7, starting transfers between devices: 24.5 us -> 32.5 us  [passed_along(): return lax.ppermute(array, 'ctx', pairs)]
    ppermute x6 -> x7, waiting for transfers between devices: 12.8 us -> 6.26 us  [passed_along(): return lax.ppermute(array, 'ctx', pairs)]
    unnamed x6, local copies, waits for them, and re-layouts: 2.73 us -> 0.01 us
    pallas_call x4 -> x5, Pallas kernels: 6.17 us -> 6.43 us  [call(): pl.pallas_call(kernel, out_shape=[jax.ShapeDtypeStruct(shape, dtype) for...]
  transfers between devices with their start and end apart: 6 -> 7, of which waited for: 5 -> 4; matrix products, arithmetic and copies ran while one was open for 0% -> 0% of each run, Pallas kernels for 9% -> 11%
where the time goes in v5:
time: 47.8 us; the launch traced here: 47.5 us
  starting transfers between devices  32.5 us (68%)
  Pallas kernels  6.43 us (13%)
  waiting for transfers between devices  6.26 us (13%)
  other arithmetic  0.84 us (2%)
  between operations  0.8 us (2%)
  local copies, waits for them, and re-layouts  0.64 us (1%)
    ppermute x7, starting transfers between devices, passed_along(): return lax.ppermute(array, 'ctx', pairs)  32.5 us
    pallas_call x5, Pallas kernels, call(): pl.pallas_call(kernel, out_shape=[jax.ShapeDtypeStruct(shape, dtype) for...  6.43 us
    ppermute x7, waiting for transfers between devices, passed_along(): return lax.ppermute(array, 'ctx', pairs)  6.26 us
  transfers between devices with their start and end apart: 7, of which 4 were waited for; matrix products, arithmetic and copies ran while one was open for 0% of the time, Pallas kernels for 11%

profile of v5, /device:TPU:24, one launch (start us, length us, event | category | flops | bytes accessed | tf_op | source)
XLA Modules:
  0.0 47.5 jit_solution(2045326740310366164)
XLA Ops:
  0.6 0.8 %pad_maximum_fusion.block_ref = bf16[256,128]{1,0:T(8,128)(2,1)S(1)} fusion(bf16[128,128]{1,0:T(8,128)(2,1)} %param.7, bf16[128,128]{1,0:T(8,128)(2,1)} %param.6), kind=kLoop, calls=%fused_computation.3 | loop fusion | flops 131072 | bytes 131072 | tf_op jit(solution)/shard_map/max | solution.py:270
  1.4 0.0 copy-start
  1.4 0.0 copy-start.1
  1.4 0.0 copy-start.2
  1.4 6.7 %collective-permute-start.2 = (bf16[256,128]{1,0:T(8,128)(2,1)S(1)}, bf16[256,128]{1,0:T(8,128)(2,1)S(1)}, u32[]{:S(2)}, u32[]{:S(2)}) collective-permute-start(bf16[256,128]{1,0:T(8,128)(2,1)S(1)} %hold_part.1.own_ref), channel_id=1, source_target_pairs={{0,24},{8,32},{16,40},{24,48},{32,56},{40,64},{48,72},{56,80},{64,... | collective-permute-start | bytes 196616 | tf_op jit(solution)/shard_map/ppermute | solution.py:264
  8.1 5.0 %collective-permute-start.1 = (bf16[256,128]{1,0:T(8,128)(2,1)S(1)}, bf16[256,128]{1,0:T(8,128)(2,1)S(1)}, u32[]{:S(2)}, u32[]{:S(2)}) collective-permute-start(bf16[256,128]{1,0:T(8,128)(2,1)S(1)} %hold_part.1.own_ref), channel_id=1, source_target_pairs={{0,8},{8,16},{16,24},{24,32},{32,40},{40,48},{48,56},{56,64},{64,7... | collective-permute-start | bytes 196616 | tf_op jit(solution)/shard_map/ppermute | solution.py:264
  13.2 5.2 %collective-permute-start = (bf16[256,128]{1,0:T(8,128)(2,1)S(1)}, bf16[256,128]{1,0:T(8,128)(2,1)S(1)}, u32[]{:S(2)}, u32[]{:S(2)}) collective-permute-start(bf16[256,128]{1,0:T(8,128)(2,1)S(1)} %hold_part.1.own_ref), channel_id=1, source_target_pairs={{0,16},{8,24},{16,32},{24,40},{32,48},{40,56},{48,64},{56,72},{64,... | collective-permute-start | bytes 196616 | tf_op jit(solution)/shard_map/ppermute | solution.py:264
  18.4 0.0 collective-permute-done.2.three_ref
  18.4 3.8 %collective-permute-start.3 = (bf16[256,128]{1,0:T(8,128)(2,1)S(1)}, bf16[256,128]{1,0:T(8,128)(2,1)S(1)}, u32[]{:S(2)}, u32[]{:S(2)}) collective-permute-start(bf16[256,128]{1,0:T(8,128)(2,1)S(1)} %collective-permute-done.2.three_ref), channel_id=1, source_target_pairs={{0,8},{8,16},{16,24},{24,32},{32,40},{40,48},{48,56},{56,64},{64,7... | collective-permute-start | bytes 196616 | tf_op jit(solution)/shard_map/ppermute | solution.py:264
  22.2 0.0 copy-done
  22.2 0.0 copy-done.1
  22.2 0.0 copy-done.2
  22.2 0.8 %load.1 = (bf16[2048,128]{1,0:T(8,128)(2,1)S(1)}, bf16[2048,128]{1,0:T(8,128)(2,1)S(1)}, f32[512,256]{1,0:T(8,128)S(1)}, f32[128,256]{1,0:T(8,128)S(1)}) custom-call(s32[1]{0:T(128)} %bitcast.index_ref, s32[32]{0:T(128)S(1)} %copy-done.2, bf16[128,2048]{1,0:T(8,128)(2,1)S(1)} %copy-done, bf16[128,2048]{1,0:T(8,128)(2,1)S(1)} %copy-done.1), custom_call_target="tpu_custom_call" | custom-call | flops 200000000 | bytes 1000000 | tf_op jit(solution)/shard_map/load/pallas_call | solution.py:211
  23.0 0.0 collective-permute-done.1.one_ref
  23.0 0.1 collective-permute-done.two_ref
  23.1 2.0 %near_part.1 = (f32[512,2048]{1,0:T(8,128)S(1)}, f32[512,2048]{1,0:T(8,128)S(1)}, f32[8,2048]{1,0:T(8,128)S(1)}) custom-call(f32[512,256]{1,0:T(8,128)S(1)} %get-tuple-element.19.bias_ref, bf16[2048,128]{1,0:T(8,128)(2,1)S(1)} %get-tuple-element.17.query_ref, bf16[2048,128]{1,0:T(8,128)(2,1)S(1)} %get-tuple-element.18.grad_ref, ...), custom_call_target="tpu_custom_call" | custom-call | flops 500000000 | bytes 1000000 | tf_op jit(solution)/shard_map/near_part/pallas_call | solution.py:211
  25.1 1.5 %collective-permute-done.3.four_ref = bf16[256,128]{1,0:T(8,128)(2,1)S(1)} collective-permute-done((bf16[256,128]{1,0:T(8,128)(2,1)S(1)}, bf16[256,128]{1,0:T(8,128)(2,1)S(1)}, u32[]{:S(2)}, u32[]{:S(2)}) %collective-permute-start.3) | collective-permute-done | bytes 65568 | tf_op jit(solution)/shard_map/ppermute | solution.py:264
  26.6 1.4 %far_part.1 = (bf16[512,128]{1,0:T(8,128)(2,1)S(1)}, bf16[256,2048]{1,0:T(8,128)(2,1)S(1)}, f32[8,2048]{1,0:T(8,128)S(1)}) custom-call(f32[128,256]{1,0:T(8,128)S(1)} %get-tuple-element.22.bias_ref, bf16[2048,128]{1,0:T(8,128)(2,1)S(1)} %get-tuple-element.17.query_ref, bf16[2048,128]{1,0:T(8,128)(2,1)S(1)} %get-tuple-element.18.grad_ref, ...), custom_call_target="tpu_custom_call" | custom-call | flops 600000000 | bytes 1000000 | tf_op jit(solution)/shard_map/far_part/pallas_call | solution.py:211
  28.1 2.5 %collective-permute-start.4 = (bf16[512,128]{1,0:T(8,128)(2,1)S(1)}, bf16[512,128]{1,0:T(8,128)(2,1)S(1)}, u32[]{:S(2)}, u32[]{:S(2)}) collective-permute-start(bf16[512,128]{1,0:T(8,128)(2,1)S(1)} %get-tuple-element.29), channel_id=1, source_target_pairs={{8,0},{16,8},{24,16},{32,24},{40,32},{48,40},{56,48},{64,56},{72,6... | collective-permute-start | bytes 393224 | tf_op jit(solution)/shard_map/ppermute | solution.py:264
  30.6 2.2 %rest_part.1 = (bf16[128,2048]{1,0:T(8,128)(2,1)}, f32[256,128]{1,0:T(8,128)S(1)}, f32[256,128]{1,0:T(8,128)S(1)}, f32[256,128]{1,0:T(8,128)S(1)}) custom-call(bf16[2048,128]{1,0:T(8,128)(2,1)S(1)} %get-tuple-element.17.query_ref, bf16[2048,128]{1,0:T(8,128)(2,1)S(1)} %get-tuple-element.18.grad_ref, ...), custom_call_target="tpu_custom_call" | custom-call | flops 800000000 | bytes 1000000 | tf_op jit(solution)/shard_map/rest_part/pallas_call | solution.py:211
  32.9 2.1 %collective-permute-done.4 = bf16[512,128]{1,0:T(8,128)(2,1)S(1)} collective-permute-done((bf16[512,128]{1,0:T(8,128)(2,1)S(1)}, bf16[512,128]{1,0:T(8,128)(2,1)S(1)}, u32[]{:S(2)}, u32[]{:S(2)}) %collective-permute-start.4) | collective-permute-done | bytes 131104 | tf_op jit(solution)/shard_map/ppermute | solution.py:264
  34.9 5.7 %collective-permute-start.5 = (bf16[256,128]{1,0:T(8,128)(2,1)S(1)}, bf16[256,128]{1,0:T(8,128)(2,1)S(1)}, u32[]{:S(2)}, u32[]{:S(2)}) collective-permute-start(bf16[256,128]{1,0:T(8,128)(2,1)S(1)} %get-tuple-element.31), channel_id=1, source_target_pairs={{24,0},{32,8},{40,16},{48,24},{56,32},{64,40},{72,48},{80,56},{88,... | collective-permute-start | bytes 196616 | tf_op jit(solution)/shard_map/ppermute | solution.py:264
  40.7 3.6 %collective-permute-start.6 = (bf16[256,128]{1,0:T(8,128)(2,1)S(1)}, bf16[256,128]{1,0:T(8,128)(2,1)S(1)}, u32[]{:S(2)}, u32[]{:S(2)}) collective-permute-start(bf16[256,128]{1,0:T(8,128)(2,1)S(1)} %get-tuple-element.32), channel_id=1, source_target_pairs={{8,0},{16,8},{24,16},{32,24},{40,32},{48,40},{56,48},{64,56},{72,6... | collective-permute-start | bytes 196616 | tf_op jit(solution)/shard_map/ppermute | solution.py:264
  44.2 0.0 collective-permute-done.5
  44.3 2.6 %collective-permute-done.6 = bf16[256,128]{1,0:T(8,128)(2,1)S(1)} collective-permute-done((bf16[256,128]{1,0:T(8,128)(2,1)S(1)}, bf16[256,128]{1,0:T(8,128)(2,1)S(1)}, u32[]{:S(2)}, u32[]{:S(2)}) %collective-permute-start.6) | collective-permute-done | bytes 65568 | tf_op jit(solution)/shard_map/ppermute | solution.py:264
  46.9 0.6 %fusion = (bf16[128,128]{1,0:T(8,128)(2,1)}, bf16[128,128]{1,0:T(8,128)(2,1)}) fusion(bf16[256,128]{1,0:T(8,128)(2,1)S(1)} %add_convert_fusion), kind=kLoop, calls=%fused_computation.4 | loop fusion | bytes 131072 | tf_op jit(solution)/shard_map/slice | solution.py:39
  (3 shorter events, 0.1 us)
Async XLA Ops:
  1.4 20.8 %copy-start = (bf16[128,2048]{1,0:T(8,128)(2,1)S(1)}, bf16[128,2048]{1,0:T(8,128)(2,1)}, u32[]{:S(2)}) copy-start(bf16[128,2048]{1,0:T(8,128)(2,1)} %wide_query_ref.1) | copy-start | bytes 1572868
  1.4 20.8 %copy-start.1 = (bf16[128,2048]{1,0:T(8,128)(2,1)S(1)}, bf16[128,2048]{1,0:T(8,128)(2,1)}, u32[]{:S(2)}) copy-start(bf16[128,2048]{1,0:T(8,128)(2,1)} %wide_grad_ref.1) | copy-start | bytes 1572868
  1.4 20.8 %copy-start.2 = (s32[32]{0:T(128)S(1)}, s32[32]{0:T(128)}, u32[]{:S(2)}) copy-start(s32[32]{0:T(128)} %lengths_ref.1) | copy-start | bytes 388
  1.4 16.9 %collective-permute-start.2 = (bf16[256,128]{1,0:T(8,128)(2,1)S(1)}, bf16[256,128]{1,0:T(8,128)(2,1)S(1)}, u32[]{:S(2)}, u32[]{:S(2)}) collective-permute-start(bf16[256,128]{1,0:T(8,128)(2,1)S(1)} %hold_part.1.own_ref), channel_id=1, source_target_pairs={{0,24},{8,32},{16,40},{24,48},{32,56},{40,64},{48,72},{56,80},{64,... | collective-permute-start | bytes 196616 | tf_op jit(solution)/shard_map/ppermute | solution.py:264
  8.1 14.9 %collective-permute-start.1 = (bf16[256,128]{1,0:T(8,128)(2,1)S(1)}, bf16[256,128]{1,0:T(8,128)(2,1)S(1)}, u32[]{:S(2)}, u32[]{:S(2)}) collective-permute-start(bf16[256,128]{1,0:T(8,128)(2,1)S(1)} %hold_part.1.own_ref), channel_id=1, source_target_pairs={{0,8},{8,16},{16,24},{24,32},{32,40},{40,48},{48,56},{56,64},{64,7... | collective-permute-start | bytes 196616 | tf_op jit(solution)/shard_map/ppermute | solution.py:264
  13.2 10.0 %collective-permute-start = (bf16[256,128]{1,0:T(8,128)(2,1)S(1)}, bf16[256,128]{1,0:T(8,128)(2,1)S(1)}, u32[]{:S(2)}, u32[]{:S(2)}) collective-permute-start(bf16[256,128]{1,0:T(8,128)(2,1)S(1)} %hold_part.1.own_ref), channel_id=1, source_target_pairs={{0,16},{8,24},{16,32},{24,40},{32,48},{40,56},{48,64},{56,72},{64,... | collective-permute-start | bytes 196616 | tf_op jit(solution)/shard_map/ppermute | solution.py:264
  18.4 8.3 %collective-permute-start.3 = (bf16[256,128]{1,0:T(8,128)(2,1)S(1)}, bf16[256,128]{1,0:T(8,128)(2,1)S(1)}, u32[]{:S(2)}, u32[]{:S(2)}) collective-permute-start(bf16[256,128]{1,0:T(8,128)(2,1)S(1)} %collective-permute-done.2.three_ref), channel_id=1, source_target_pairs={{0,8},{8,16},{16,24},{24,32},{32,40},{40,48},{48,56},{56,64},{64,7... | collective-permute-start | bytes 196616 | tf_op jit(solution)/shard_map/ppermute | solution.py:264
  28.1 6.9 %collective-permute-start.4 = (bf16[512,128]{1,0:T(8,128)(2,1)S(1)}, bf16[512,128]{1,0:T(8,128)(2,1)S(1)}, u32[]{:S(2)}, u32[]{:S(2)}) collective-permute-start(bf16[512,128]{1,0:T(8,128)(2,1)S(1)} %get-tuple-element.29), channel_id=1, source_target_pairs={{8,0},{16,8},{24,16},{32,24},{40,32},{48,40},{56,48},{64,56},{72,6... | collective-permute-start | bytes 393224 | tf_op jit(solution)/shard_map/ppermute | solution.py:264
  34.9 9.3 %collective-permute-start.5 = (bf16[256,128]{1,0:T(8,128)(2,1)S(1)}, bf16[256,128]{1,0:T(8,128)(2,1)S(1)}, u32[]{:S(2)}, u32[]{:S(2)}) collective-permute-start(bf16[256,128]{1,0:T(8,128)(2,1)S(1)} %get-tuple-element.31), channel_id=1, source_target_pairs={{24,0},{32,8},{40,16},{48,24},{56,32},{64,40},{72,48},{80,56},{88,... | collective-permute-start | bytes 196616 | tf_op jit(solution)/shard_map/ppermute | solution.py:264
  40.7 6.2 %collective-permute-start.6 = (bf16[256,128]{1,0:T(8,128)(2,1)S(1)}, bf16[256,128]{1,0:T(8,128)(2,1)S(1)}, u32[]{:S(2)}, u32[]{:S(2)}) collective-permute-start(bf16[256,128]{1,0:T(8,128)(2,1)S(1)} %get-tuple-element.32), channel_id=1, source_target_pairs={{8,0},{16,8},{24,16},{32,24},{40,32},{48,40},{56,48},{64,56},{72,6... | collective-permute-start | bytes 196616 | tf_op jit(solution)/shard_map/ppermute | solution.py:264

commit v6 on v5

--- a/solution.py
+++ b/solution.py
@@ -94,7 +94,7 @@
 
 
 def near_kernel(
-    bias_ref, query_ref, grad_ref, two_ref, one_ref, three_ref, own_ref, weight_ref, dprob_ref, stat_ref
+    bias_ref, query_ref, grad_ref, one_ref, two_ref, three_ref, own_ref, weight_ref, dprob_ref, stat_ref
 ):
     blocks = (two_ref, one_ref, three_ref, own_ref)
     keys = jnp.concatenate([key_of(block) for block in blocks], axis=0)
@@ -276,7 +276,7 @@
     two = passed_along(own, 2)
     query, grad, near_bias, far_bias = load(index, doc_lengths, queries, grad_out)
     four = passed_along(three, 1)
-    weight, dprob, near_stat = near_part(near_bias, query, grad, two, one, three, own)
+    weight, dprob, near_stat = near_part(near_bias, query, grad, one, two, three, own)
     far_sums, far_dscore, stat = far_part(far_bias, query, grad, weight, dprob, near_stat, four)
     far_sums = passed_along(far_sums, -1)
     grad_q, one_sums, three_sums, own_sums = rest_part(

time: 47.8 us -> 47.8 us (level)
  waiting for transfers between devices: 6.26 us -> 4.59 us
  starting transfers between devices: 32.5 us -> 34.1 us
    ppermute x7, waiting for transfers between devices: 6.26 us -> 4.59 us  [passed_along(): return lax.ppermute(array, 'ctx', pairs)]
    ppermute x7, starting transfers between devices: 32.5 us -> 34.1 us  [passed_along(): return lax.ppermute(array, 'ctx', pairs)]
  transfers between devices with their start and end apart: 7 -> 7, of which waited for: 4 -> 3; matrix products, arithmetic and copies ran while one was open for 0% -> 0% of each run, Pallas kernels for 11% -> 11%
where the time goes in v6:
time: 47.8 us; the launch traced here: 47.4 us
  starting transfers between devices  34.1 us (71%)
  Pallas kernels  6.43 us (13%)
  waiting for transfers between devices  4.59 us (10%)
  other arithmetic  0.84 us (2%)
  between operations  0.8 us (2%)
  local copies, waits for them, and re-layouts  0.64 us (1%)
    ppermute x7, starting transfers between devices, passed_along(): return lax.ppermute(array, 'ctx', pairs)  34.1 us
    pallas_call x5, Pallas kernels, call(): pl.pallas_call(kernel, out_shape=[jax.ShapeDtypeStruct(shape, dtype) for...  6.43 us
    ppermute x7, waiting for transfers between devices, passed_along(): return lax.ppermute(array, 'ctx', pairs)  4.59 us
  transfers between devices with their start and end apart: 7, of which 3 were waited for; matrix products, arithmetic and copies ran while one was open for 0% of the time, Pallas kernels for 11%

profile of v6, /device:TPU:24, one launch (start us, length us, event | category | flops | bytes accessed | tf_op | source)
XLA Modules:
  0.0 47.4 jit_solution(5588678554852586499)
XLA Ops:
  0.6 0.8 %pad_maximum_fusion.block_ref = bf16[256,128]{1,0:T(8,128)(2,1)S(1)} fusion(bf16[128,128]{1,0:T(8,128)(2,1)} %param.7, bf16[128,128]{1,0:T(8,128)(2,1)} %param.6), kind=kLoop, calls=%fused_computation.3 | loop fusion | flops 131072 | bytes 131072 | tf_op jit(solution)/shard_map/max | solution.py:270
  1.4 0.0 copy-start
  1.4 0.0 copy-start.1
  1.4 0.0 copy-start.2
  1.4 6.7 %collective-permute-start.2 = (bf16[256,128]{1,0:T(8,128)(2,1)S(1)}, bf16[256,128]{1,0:T(8,128)(2,1)S(1)}, u32[]{:S(2)}, u32[]{:S(2)}) collective-permute-start(bf16[256,128]{1,0:T(8,128)(2,1)S(1)} %hold_part.1.own_ref), channel_id=1, source_target_pairs={{0,24},{8,32},{16,40},{24,48},{32,56},{40,64},{48,72},{56,80},{64,... | collective-permute-start | bytes 196616 | tf_op jit(solution)/shard_map/ppermute | solution.py:264
  8.1 6.4 %collective-permute-start.1 = (bf16[256,128]{1,0:T(8,128)(2,1)S(1)}, bf16[256,128]{1,0:T(8,128)(2,1)S(1)}, u32[]{:S(2)}, u32[]{:S(2)}) collective-permute-start(bf16[256,128]{1,0:T(8,128)(2,1)S(1)} %hold_part.1.own_ref), channel_id=1, source_target_pairs={{0,16},{8,24},{16,32},{24,40},{32,48},{40,56},{48,64},{56,72},{64,... | collective-permute-start | bytes 196616 | tf_op jit(solution)/shard_map/ppermute | solution.py:264
  14.5 3.8 %collective-permute-start = (bf16[256,128]{1,0:T(8,128)(2,1)S(1)}, bf16[256,128]{1,0:T(8,128)(2,1)S(1)}, u32[]{:S(2)}, u32[]{:S(2)}) collective-permute-start(bf16[256,128]{1,0:T(8,128)(2,1)S(1)} %hold_part.1.own_ref), channel_id=1, source_target_pairs={{0,8},{8,16},{16,24},{24,32},{32,40},{40,48},{48,56},{56,64},{64,7... | collective-permute-start | bytes 196616 | tf_op jit(solution)/shard_map/ppermute | solution.py:264
  18.4 0.0 collective-permute-done.2.three_ref
  18.4 4.2 %collective-permute-start.3 = (bf16[256,128]{1,0:T(8,128)(2,1)S(1)}, bf16[256,128]{1,0:T(8,128)(2,1)S(1)}, u32[]{:S(2)}, u32[]{:S(2)}) collective-permute-start(bf16[256,128]{1,0:T(8,128)(2,1)S(1)} %collective-permute-done.2.three_ref), channel_id=1, source_target_pairs={{0,8},{8,16},{16,24},{24,32},{32,40},{40,48},{48,56},{56,64},{64,7... | collective-permute-start | bytes 196616 | tf_op jit(solution)/shard_map/ppermute | solution.py:264
  22.6 0.0 copy-done
  22.6 0.0 copy-done.1
  22.6 0.0 copy-done.2
  22.6 0.8 %load.1 = (bf16[2048,128]{1,0:T(8,128)(2,1)S(1)}, bf16[2048,128]{1,0:T(8,128)(2,1)S(1)}, f32[512,256]{1,0:T(8,128)S(1)}, f32[128,256]{1,0:T(8,128)S(1)}) custom-call(s32[1]{0:T(128)} %bitcast.index_ref, s32[32]{0:T(128)S(1)} %copy-done.2, bf16[128,2048]{1,0:T(8,128)(2,1)S(1)} %copy-done, bf16[128,2048]{1,0:T(8,128)(2,1)S(1)} %copy-done.1), custom_call_target="tpu_custom_call" | custom-call | flops 200000000 | bytes 1000000 | tf_op jit(solution)/shard_map/load/pallas_call | solution.py:211
  23.4 0.0 collective-permute-done.1.two_ref
  23.4 0.0 collective-permute-done.one_ref
  23.4 2.0 %near_part.1 = (f32[512,2048]{1,0:T(8,128)S(1)}, f32[512,2048]{1,0:T(8,128)S(1)}, f32[8,2048]{1,0:T(8,128)S(1)}) custom-call(f32[512,256]{1,0:T(8,128)S(1)} %get-tuple-element.19.bias_ref, bf16[2048,128]{1,0:T(8,128)(2,1)S(1)} %get-tuple-element.17.query_ref, bf16[2048,128]{1,0:T(8,128)(2,1)S(1)} %get-tuple-element.18.grad_ref, ...), custom_call_target="tpu_custom_call" | custom-call | flops 500000000 | bytes 1000000 | tf_op jit(solution)/shard_map/near_part/pallas_call | solution.py:211
  25.4 1.3 %collective-permute-done.3.four_ref = bf16[256,128]{1,0:T(8,128)(2,1)S(1)} collective-permute-done((bf16[256,128]{1,0:T(8,128)(2,1)S(1)}, bf16[256,128]{1,0:T(8,128)(2,1)S(1)}, u32[]{:S(2)}, u32[]{:S(2)}) %collective-permute-start.3) | collective-permute-done | bytes 65568 | tf_op jit(solution)/shard_map/ppermute | solution.py:264
  26.6 1.4 %far_part.1 = (bf16[512,128]{1,0:T(8,128)(2,1)S(1)}, bf16[256,2048]{1,0:T(8,128)(2,1)S(1)}, f32[8,2048]{1,0:T(8,128)S(1)}) custom-call(f32[128,256]{1,0:T(8,128)S(1)} %get-tuple-element.22.bias_ref, bf16[2048,128]{1,0:T(8,128)(2,1)S(1)} %get-tuple-element.17.query_ref, bf16[2048,128]{1,0:T(8,128)(2,1)S(1)} %get-tuple-element.18.grad_ref, ...), custom_call_target="tpu_custom_call" | custom-call | flops 600000000 | bytes 1000000 | tf_op jit(solution)/shard_map/far_part/pallas_call | solution.py:211
  28.1 3.1 %collective-permute-start.4 = (bf16[512,128]{1,0:T(8,128)(2,1)S(1)}, bf16[512,128]{1,0:T(8,128)(2,1)S(1)}, u32[]{:S(2)}, u32[]{:S(2)}) collective-permute-start(bf16[512,128]{1,0:T(8,128)(2,1)S(1)} %get-tuple-element.29), channel_id=1, source_target_pairs={{8,0},{16,8},{24,16},{32,24},{40,32},{48,40},{56,48},{64,56},{72,6... | collective-permute-start | bytes 393224 | tf_op jit(solution)/shard_map/ppermute | solution.py:264
  31.2 2.2 %rest_part.1 = (bf16[128,2048]{1,0:T(8,128)(2,1)}, f32[256,128]{1,0:T(8,128)S(1)}, f32[256,128]{1,0:T(8,128)S(1)}, f32[256,128]{1,0:T(8,128)S(1)}) custom-call(bf16[2048,128]{1,0:T(8,128)(2,1)S(1)} %get-tuple-element.17.query_ref, bf16[2048,128]{1,0:T(8,128)(2,1)S(1)} %get-tuple-element.18.grad_ref, ...), custom_call_target="tpu_custom_call" | custom-call | flops 800000000 | bytes 1000000 | tf_op jit(solution)/shard_map/rest_part/pallas_call | solution.py:211
  33.5 1.5 %collective-permute-done.4 = bf16[512,128]{1,0:T(8,128)(2,1)S(1)} collective-permute-done((bf16[512,128]{1,0:T(8,128)(2,1)S(1)}, bf16[512,128]{1,0:T(8,128)(2,1)S(1)}, u32[]{:S(2)}, u32[]{:S(2)}) %collective-permute-start.4) | collective-permute-done | bytes 131104 | tf_op jit(solution)/shard_map/ppermute | solution.py:264
  34.9 5.6 %collective-permute-start.5 = (bf16[256,128]{1,0:T(8,128)(2,1)S(1)}, bf16[256,128]{1,0:T(8,128)(2,1)S(1)}, u32[]{:S(2)}, u32[]{:S(2)}) collective-permute-start(bf16[256,128]{1,0:T(8,128)(2,1)S(1)} %get-tuple-element.31), channel_id=1, source_target_pairs={{24,0},{32,8},{40,16},{48,24},{56,32},{64,40},{72,48},{80,56},{88,... | collective-permute-start | bytes 196616 | tf_op jit(solution)/shard_map/ppermute | solution.py:264
  40.6 4.3 %collective-permute-start.6 = (bf16[256,128]{1,0:T(8,128)(2,1)S(1)}, bf16[256,128]{1,0:T(8,128)(2,1)S(1)}, u32[]{:S(2)}, u32[]{:S(2)}) collective-permute-start(bf16[256,128]{1,0:T(8,128)(2,1)S(1)} %get-tuple-element.32), channel_id=1, source_target_pairs={{8,0},{16,8},{24,16},{32,24},{40,32},{48,40},{56,48},{64,56},{72,6... | collective-permute-start | bytes 196616 | tf_op jit(solution)/shard_map/ppermute | solution.py:264
  44.9 0.0 collective-permute-done.5
  44.9 1.9 %collective-permute-done.6 = bf16[256,128]{1,0:T(8,128)(2,1)S(1)} collective-permute-done((bf16[256,128]{1,0:T(8,128)(2,1)S(1)}, bf16[256,128]{1,0:T(8,128)(2,1)S(1)}, u32[]{:S(2)}, u32[]{:S(2)}) %collective-permute-start.6) | collective-permute-done | bytes 65568 | tf_op jit(solution)/shard_map/ppermute | solution.py:264
  46.8 0.6 %fusion = (bf16[128,128]{1,0:T(8,128)(2,1)}, bf16[128,128]{1,0:T(8,128)(2,1)}) fusion(bf16[256,128]{1,0:T(8,128)(2,1)S(1)} %add_convert_fusion), kind=kLoop, calls=%fused_computation.4 | loop fusion | bytes 131072 | tf_op jit(solution)/shard_map/slice | solution.py:39
  (3 shorter events, 0.1 us)
Async XLA Ops:
  1.4 21.1 %copy-start = (bf16[128,2048]{1,0:T(8,128)(2,1)S(1)}, bf16[128,2048]{1,0:T(8,128)(2,1)}, u32[]{:S(2)}) copy-start(bf16[128,2048]{1,0:T(8,128)(2,1)} %wide_query_ref.1) | copy-start | bytes 1572868
  1.4 21.1 %copy-start.1 = (bf16[128,2048]{1,0:T(8,128)(2,1)S(1)}, bf16[128,2048]{1,0:T(8,128)(2,1)}, u32[]{:S(2)}) copy-start(bf16[128,2048]{1,0:T(8,128)(2,1)} %wide_grad_ref.1) | copy-start | bytes 1572868
  1.4 21.2 %copy-start.2 = (s32[32]{0:T(128)S(1)}, s32[32]{0:T(128)}, u32[]{:S(2)}) copy-start(s32[32]{0:T(128)} %lengths_ref.1) | copy-start | bytes 388
  1.4 16.9 %collective-permute-start.2 = (bf16[256,128]{1,0:T(8,128)(2,1)S(1)}, bf16[256,128]{1,0:T(8,128)(2,1)S(1)}, u32[]{:S(2)}, u32[]{:S(2)}) collective-permute-start(bf16[256,128]{1,0:T(8,128)(2,1)S(1)} %hold_part.1.own_ref), channel_id=1, source_target_pairs={{0,24},{8,32},{16,40},{24,48},{32,56},{40,64},{48,72},{56,80},{64,... | collective-permute-start | bytes 196616 | tf_op jit(solution)/shard_map/ppermute | solution.py:264
  8.1 15.2 %collective-permute-start.1 = (bf16[256,128]{1,0:T(8,128)(2,1)S(1)}, bf16[256,128]{1,0:T(8,128)(2,1)S(1)}, u32[]{:S(2)}, u32[]{:S(2)}) collective-permute-start(bf16[256,128]{1,0:T(8,128)(2,1)S(1)} %hold_part.1.own_ref), channel_id=1, source_target_pairs={{0,16},{8,24},{16,32},{24,40},{32,48},{40,56},{48,64},{56,72},{64,... | collective-permute-start | bytes 196616 | tf_op jit(solution)/shard_map/ppermute | solution.py:264
  14.5 8.9 %collective-permute-start = (bf16[256,128]{1,0:T(8,128)(2,1)S(1)}, bf16[256,128]{1,0:T(8,128)(2,1)S(1)}, u32[]{:S(2)}, u32[]{:S(2)}) collective-permute-start(bf16[256,128]{1,0:T(8,128)(2,1)S(1)} %hold_part.1.own_ref), channel_id=1, source_target_pairs={{0,8},{8,16},{16,24},{24,32},{32,40},{40,48},{48,56},{56,64},{64,7... | collective-permute-start | bytes 196616 | tf_op jit(solution)/shard_map/ppermute | solution.py:264
  18.4 8.3 %collective-permute-start.3 = (bf16[256,128]{1,0:T(8,128)(2,1)S(1)}, bf16[256,128]{1,0:T(8,128)(2,1)S(1)}, u32[]{:S(2)}, u32[]{:S(2)}) collective-permute-start(bf16[256,128]{1,0:T(8,128)(2,1)S(1)} %collective-permute-done.2.three_ref), channel_id=1, source_target_pairs={{0,8},{8,16},{16,24},{24,32},{32,40},{40,48},{48,56},{56,64},{64,7... | collective-permute-start | bytes 196616 | tf_op jit(solution)/shard_map/ppermute | solution.py:264
  28.1 6.9 %collective-permute-start.4 = (bf16[512,128]{1,0:T(8,128)(2,1)S(1)}, bf16[512,128]{1,0:T(8,128)(2,1)S(1)}, u32[]{:S(2)}, u32[]{:S(2)}) collective-permute-start(bf16[512,128]{1,0:T(8,128)(2,1)S(1)} %get-tuple-element.29), channel_id=1, source_target_pairs={{8,0},{16,8},{24,16},{32,24},{40,32},{48,40},{56,48},{64,56},{72,6... | collective-permute-start | bytes 393224 | tf_op jit(solution)/shard_map/ppermute | solution.py:264
  34.9 9.9 %collective-permute-start.5 = (bf16[256,128]{1,0:T(8,128)(2,1)S(1)}, bf16[256,128]{1,0:T(8,128)(2,1)S(1)}, u32[]{:S(2)}, u32[]{:S(2)}) collective-permute-start(bf16[256,128]{1,0:T(8,128)(2,1)S(1)} %get-tuple-element.31), channel_id=1, source_target_pairs={{24,0},{32,8},{40,16},{48,24},{56,32},{64,40},{72,48},{80,56},{88,... | collective-permute-start | bytes 196616 | tf_op jit(solution)/shard_map/ppermute | solution.py:264
  40.6 6.2 %collective-permute-start.6 = (bf16[256,128]{1,0:T(8,128)(2,1)S(1)}, bf16[256,128]{1,0:T(8,128)(2,1)S(1)}, u32[]{:S(2)}, u32[]{:S(2)}) collective-permute-start(bf16[256,128]{1,0:T(8,128)(2,1)S(1)} %get-tuple-element.32), channel_id=1, source_target_pairs={{8,0},{16,8},{24,16},{32,24},{40,32},{48,40},{56,48},{64,56},{72,6... | collective-permute-start | bytes 196616 | tf_op jit(solution)/shard_map/ppermute | solution.py:264

commit v7 on v5

--- a/solution.py
+++ b/solution.py
@@ -286,8 +286,9 @@
     one_sums = (one_sums + far_sums[: 2 * TOK].astype(F32)).astype(BF16)
     three_sums = passed_along(three_sums, -3)
     one_sums = passed_along(one_sums, -1)
-    sums = (own_sums + three_sums.astype(F32) + one_sums.astype(F32)).astype(BF16)
-    return (grad_q, key_of(sums), value_of(sums))
+    parts = (own_sums, three_sums.astype(F32), one_sums.astype(F32))
+    grad_k, grad_v = [(of(parts[0]) + of(parts[1]) + of(parts[2])).astype(BF16) for of in (key_of, value_of)]
+    return (grad_q, grad_k, grad_v)
 
 
 def solution(mesh):

time: 47.8 us -> 47.8 us (level)
  other arithmetic: 0.84 us -> 1.49 us
  local copies, waits for them, and re-layouts: 0.64 us -> 0.01 us
    convert_element_type x1 -> x3, other arithmetic: 0.03 us -> 0.68 us  [the longest x1 0.66 us: local(): (of(parts[0]) + of(parts[1]) + of(parts[2])).astype(BF16)]
    slice x1 -> x0, local copies, waits for them, and re-layouts: 0.63 us -> none  [value_of(): return block[TOK:]]
where the time goes in v7:
time: 47.8 us; the launch traced here: 47.5 us
  starting transfers between devices  32.5 us (68%)
  Pallas kernels  6.43 us (13%)
  waiting for transfers between devices  6.24 us (13%)
  other arithmetic  1.49 us (3%)
  between operations  0.8 us (2%)
    ppermute x7, starting transfers between devices, passed_along(): return lax.ppermute(array, 'ctx', pairs)  32.5 us
    pallas_call x5, Pallas kernels, call(): pl.pallas_call(kernel, out_shape=[jax.ShapeDtypeStruct(shape, dtype) for...  6.43 us
    ppermute x7, waiting for transfers between devices, passed_along(): return lax.ppermute(array, 'ctx', pairs)  6.24 us
  transfers between devices with their start and end apart: 7, of which 4 were waited for; matrix products, arithmetic and copies ran while one was open for 0% of the time, Pallas kernels for 11%

profile of v7, /device:TPU:24, one launch (start us, length us, event | category | flops | bytes accessed | tf_op | source)
XLA Modules:
  0.0 47.5 jit_solution(13898556879505118790)
XLA Ops:
  0.6 0.8 %pad_maximum_fusion.block_ref = bf16[256,128]{1,0:T(8,128)(2,1)S(1)} fusion(bf16[128,128]{1,0:T(8,128)(2,1)} %param.7, bf16[128,128]{1,0:T(8,128)(2,1)} %param.6), kind=kLoop, calls=%fused_computation.8 | loop fusion | flops 131072 | bytes 131072 | tf_op jit(solution)/shard_map/max | solution.py:270
  1.4 0.0 copy-start
  1.4 0.0 copy-start.1
  1.4 0.0 copy-start.2
  1.4 6.7 %collective-permute-start.2 = (bf16[256,128]{1,0:T(8,128)(2,1)S(1)}, bf16[256,128]{1,0:T(8,128)(2,1)S(1)}, u32[]{:S(2)}, u32[]{:S(2)}) collective-permute-start(bf16[256,128]{1,0:T(8,128)(2,1)S(1)} %hold_part.1.own_ref), channel_id=1, source_target_pairs={{0,24},{8,32},{16,40},{24,48},{32,56},{40,64},{48,72},{56,80},{64,... | collective-permute-start | bytes 196616 | tf_op jit(solution)/shard_map/ppermute | solution.py:264
  8.1 5.0 %collective-permute-start.1 = (bf16[256,128]{1,0:T(8,128)(2,1)S(1)}, bf16[256,128]{1,0:T(8,128)(2,1)S(1)}, u32[]{:S(2)}, u32[]{:S(2)}) collective-permute-start(bf16[256,128]{1,0:T(8,128)(2,1)S(1)} %hold_part.1.own_ref), channel_id=1, source_target_pairs={{0,8},{8,16},{16,24},{24,32},{32,40},{40,48},{48,56},{56,64},{64,7... | collective-permute-start | bytes 196616 | tf_op jit(solution)/shard_map/ppermute | solution.py:264
  13.2 5.2 %collective-permute-start = (bf16[256,128]{1,0:T(8,128)(2,1)S(1)}, bf16[256,128]{1,0:T(8,128)(2,1)S(1)}, u32[]{:S(2)}, u32[]{:S(2)}) collective-permute-start(bf16[256,128]{1,0:T(8,128)(2,1)S(1)} %hold_part.1.own_ref), channel_id=1, source_target_pairs={{0,16},{8,24},{16,32},{24,40},{32,48},{40,56},{48,64},{56,72},{64,... | collective-permute-start | bytes 196616 | tf_op jit(solution)/shard_map/ppermute | solution.py:264
  18.4 0.0 collective-permute-done.2.three_ref
  18.4 3.8 %collective-permute-start.3 = (bf16[256,128]{1,0:T(8,128)(2,1)S(1)}, bf16[256,128]{1,0:T(8,128)(2,1)S(1)}, u32[]{:S(2)}, u32[]{:S(2)}) collective-permute-start(bf16[256,128]{1,0:T(8,128)(2,1)S(1)} %collective-permute-done.2.three_ref), channel_id=1, source_target_pairs={{0,8},{8,16},{16,24},{24,32},{32,40},{40,48},{48,56},{56,64},{64,7... | collective-permute-start | bytes 196616 | tf_op jit(solution)/shard_map/ppermute | solution.py:264
  22.2 0.0 copy-done
  22.2 0.0 copy-done.1
  22.2 0.0 copy-done.2
  22.2 0.8 %load.1 = (bf16[2048,128]{1,0:T(8,128)(2,1)S(1)}, bf16[2048,128]{1,0:T(8,128)(2,1)S(1)}, f32[512,256]{1,0:T(8,128)S(1)}, f32[128,256]{1,0:T(8,128)S(1)}) custom-call(s32[1]{0:T(128)} %bitcast.index_ref, s32[32]{0:T(128)S(1)} %copy-done.2, bf16[128,2048]{1,0:T(8,128)(2,1)S(1)} %copy-done, bf16[128,2048]{1,0:T(8,128)(2,1)S(1)} %copy-done.1), custom_call_target="tpu_custom_call" | custom-call | flops 200000000 | bytes 1000000 | tf_op jit(solution)/shard_map/load/pallas_call | solution.py:211
  23.0 0.0 collective-permute-done.1.one_ref
  23.0 0.1 collective-permute-done.two_ref
  23.1 2.0 %near_part.1 = (f32[512,2048]{1,0:T(8,128)S(1)}, f32[512,2048]{1,0:T(8,128)S(1)}, f32[8,2048]{1,0:T(8,128)S(1)}) custom-call(f32[512,256]{1,0:T(8,128)S(1)} %get-tuple-element.19.bias_ref, bf16[2048,128]{1,0:T(8,128)(2,1)S(1)} %get-tuple-element.17.query_ref, bf16[2048,128]{1,0:T(8,128)(2,1)S(1)} %get-tuple-element.18.grad_ref, ...), custom_call_target="tpu_custom_call" | custom-call | flops 500000000 | bytes 1000000 | tf_op jit(solution)/shard_map/near_part/pallas_call | solution.py:211
  25.1 1.5 %collective-permute-done.3.four_ref = bf16[256,128]{1,0:T(8,128)(2,1)S(1)} collective-permute-done((bf16[256,128]{1,0:T(8,128)(2,1)S(1)}, bf16[256,128]{1,0:T(8,128)(2,1)S(1)}, u32[]{:S(2)}, u32[]{:S(2)}) %collective-permute-start.3) | collective-permute-done | bytes 65568 | tf_op jit(solution)/shard_map/ppermute | solution.py:264
  26.6 1.4 %far_part.1 = (bf16[512,128]{1,0:T(8,128)(2,1)S(1)}, bf16[256,2048]{1,0:T(8,128)(2,1)S(1)}, f32[8,2048]{1,0:T(8,128)S(1)}) custom-call(f32[128,256]{1,0:T(8,128)S(1)} %get-tuple-element.22.bias_ref, bf16[2048,128]{1,0:T(8,128)(2,1)S(1)} %get-tuple-element.17.query_ref, bf16[2048,128]{1,0:T(8,128)(2,1)S(1)} %get-tuple-element.18.grad_ref, ...), custom_call_target="tpu_custom_call" | custom-call | flops 600000000 | bytes 1000000 | tf_op jit(solution)/shard_map/far_part/pallas_call | solution.py:211
  28.1 2.5 %collective-permute-start.4 = (bf16[512,128]{1,0:T(8,128)(2,1)S(1)}, bf16[512,128]{1,0:T(8,128)(2,1)S(1)}, u32[]{:S(2)}, u32[]{:S(2)}) collective-permute-start(bf16[512,128]{1,0:T(8,128)(2,1)S(1)} %get-tuple-element.29), channel_id=1, source_target_pairs={{8,0},{16,8},{24,16},{32,24},{40,32},{48,40},{56,48},{64,56},{72,6... | collective-permute-start | bytes 393224 | tf_op jit(solution)/shard_map/ppermute | solution.py:264
  30.6 2.2 %rest_part.1 = (bf16[128,2048]{1,0:T(8,128)(2,1)}, f32[256,128]{1,0:T(8,128)S(1)}, f32[256,128]{1,0:T(8,128)S(1)}, f32[256,128]{1,0:T(8,128)S(1)}) custom-call(bf16[2048,128]{1,0:T(8,128)(2,1)S(1)} %get-tuple-element.17.query_ref, bf16[2048,128]{1,0:T(8,128)(2,1)S(1)} %get-tuple-element.18.grad_ref, ...), custom_call_target="tpu_custom_call" | custom-call | flops 800000000 | bytes 1000000 | tf_op jit(solution)/shard_map/rest_part/pallas_call | solution.py:211
  32.9 2.1 %collective-permute-done.4 = bf16[512,128]{1,0:T(8,128)(2,1)S(1)} collective-permute-done((bf16[512,128]{1,0:T(8,128)(2,1)S(1)}, bf16[512,128]{1,0:T(8,128)(2,1)S(1)}, u32[]{:S(2)}, u32[]{:S(2)}) %collective-permute-start.4) | collective-permute-done | bytes 131104 | tf_op jit(solution)/shard_map/ppermute | solution.py:264
  34.9 5.7 %collective-permute-start.5 = (bf16[256,128]{1,0:T(8,128)(2,1)S(1)}, bf16[256,128]{1,0:T(8,128)(2,1)S(1)}, u32[]{:S(2)}, u32[]{:S(2)}) collective-permute-start(bf16[256,128]{1,0:T(8,128)(2,1)S(1)} %get-tuple-element.33), channel_id=1, source_target_pairs={{24,0},{32,8},{40,16},{48,24},{56,32},{64,40},{72,48},{80,56},{88,... | collective-permute-start | bytes 196616 | tf_op jit(solution)/shard_map/ppermute | solution.py:264
  40.7 3.6 %collective-permute-start.6 = (bf16[256,128]{1,0:T(8,128)(2,1)S(1)}, bf16[256,128]{1,0:T(8,128)(2,1)S(1)}, u32[]{:S(2)}, u32[]{:S(2)}) collective-permute-start(bf16[256,128]{1,0:T(8,128)(2,1)S(1)} %get-tuple-element.34), channel_id=1, source_target_pairs={{8,0},{16,8},{24,16},{32,24},{40,32},{48,40},{56,48},{64,56},{72,6... | collective-permute-start | bytes 196616 | tf_op jit(solution)/shard_map/ppermute | solution.py:264
  44.2 0.0 collective-permute-done.5
  44.3 2.5 %collective-permute-done.6 = bf16[256,128]{1,0:T(8,128)(2,1)S(1)} collective-permute-done((bf16[256,128]{1,0:T(8,128)(2,1)S(1)}, bf16[256,128]{1,0:T(8,128)(2,1)S(1)}, u32[]{:S(2)}, u32[]{:S(2)}) %collective-permute-start.6) | collective-permute-done | bytes 65568 | tf_op jit(solution)/shard_map/ppermute | solution.py:264
  46.8 0.7 %fusion = (bf16[128,128]{1,0:T(8,128)(2,1)}, bf16[128,128]{1,0:T(8,128)(2,1)}) fusion(f32[256,128]{1,0:T(8,128)S(1)} %convert_element_type.29, f32[256,128]{1,0:T(8,128)S(1)} %convert_element_type.26, f32[256,128]{1,0:T(8,128)S(1)} %get-tuple-element.27), kind=kLoop, calls=%fused_computation.3 | loop fusion | flops 98304 | bytes 458752 | tf_op jit(solution)/shard_map/convert_element_type | solution.py:290
  (4 shorter events, 0.1 us)
Async XLA Ops:
  1.4 20.8 %copy-start = (bf16[128,2048]{1,0:T(8,128)(2,1)S(1)}, bf16[128,2048]{1,0:T(8,128)(2,1)}, u32[]{:S(2)}) copy-start(bf16[128,2048]{1,0:T(8,128)(2,1)} %wide_query_ref.1) | copy-start | bytes 1572868
  1.4 20.8 %copy-start.1 = (bf16[128,2048]{1,0:T(8,128)(2,1)S(1)}, bf16[128,2048]{1,0:T(8,128)(2,1)}, u32[]{:S(2)}) copy-start(bf16[128,2048]{1,0:T(8,128)(2,1)} %wide_grad_ref.1) | copy-start | bytes 1572868
  1.4 20.8 %copy-start.2 = (s32[32]{0:T(128)S(1)}, s32[32]{0:T(128)}, u32[]{:S(2)}) copy-start(s32[32]{0:T(128)} %lengths_ref.1) | copy-start | bytes 388
  1.4 16.9 %collective-permute-start.2 = (bf16[256,128]{1,0:T(8,128)(2,1)S(1)}, bf16[256,128]{1,0:T(8,128)(2,1)S(1)}, u32[]{:S(2)}, u32[]{:S(2)}) collective-permute-start(bf16[256,128]{1,0:T(8,128)(2,1)S(1)} %hold_part.1.own_ref), channel_id=1, source_target_pairs={{0,24},{8,32},{16,40},{24,48},{32,56},{40,64},{48,72},{56,80},{64,... | collective-permute-start | bytes 196616 | tf_op jit(solution)/shard_map/ppermute | solution.py:264
  8.1 14.9 %collective-permute-start.1 = (bf16[256,128]{1,0:T(8,128)(2,1)S(1)}, bf16[256,128]{1,0:T(8,128)(2,1)S(1)}, u32[]{:S(2)}, u32[]{:S(2)}) collective-permute-start(bf16[256,128]{1,0:T(8,128)(2,1)S(1)} %hold_part.1.own_ref), channel_id=1, source_target_pairs={{0,8},{8,16},{16,24},{24,32},{32,40},{40,48},{48,56},{56,64},{64,7... | collective-permute-start | bytes 196616 | tf_op jit(solution)/shard_map/ppermute | solution.py:264
  13.2 10.0 %collective-permute-start = (bf16[256,128]{1,0:T(8,128)(2,1)S(1)}, bf16[256,128]{1,0:T(8,128)(2,1)S(1)}, u32[]{:S(2)}, u32[]{:S(2)}) collective-permute-start(bf16[256,128]{1,0:T(8,128)(2,1)S(1)} %hold_part.1.own_ref), channel_id=1, source_target_pairs={{0,16},{8,24},{16,32},{24,40},{32,48},{40,56},{48,64},{56,72},{64,... | collective-permute-start | bytes 196616 | tf_op jit(solution)/shard_map/ppermute | solution.py:264
  18.4 8.3 %collective-permute-start.3 = (bf16[256,128]{1,0:T(8,128)(2,1)S(1)}, bf16[256,128]{1,0:T(8,128)(2,1)S(1)}, u32[]{:S(2)}, u32[]{:S(2)}) collective-permute-start(bf16[256,128]{1,0:T(8,128)(2,1)S(1)} %collective-permute-done.2.three_ref), channel_id=1, source_target_pairs={{0,8},{8,16},{16,24},{24,32},{32,40},{40,48},{48,56},{56,64},{64,7... | collective-permute-start | bytes 196616 | tf_op jit(solution)/shard_map/ppermute | solution.py:264
  28.1 6.9 %collective-permute-start.4 = (bf16[512,128]{1,0:T(8,128)(2,1)S(1)}, bf16[512,128]{1,0:T(8,128)(2,1)S(1)}, u32[]{:S(2)}, u32[]{:S(2)}) collective-permute-start(bf16[512,128]{1,0:T(8,128)(2,1)S(1)} %get-tuple-element.29), channel_id=1, source_target_pairs={{8,0},{16,8},{24,16},{32,24},{40,32},{48,40},{56,48},{64,56},{72,6... | collective-permute-start | bytes 393224 | tf_op jit(solution)/shard_map/ppermute | solution.py:264
  34.9 9.3 %collective-permute-start.5 = (bf16[256,128]{1,0:T(8,128)(2,1)S(1)}, bf16[256,128]{1,0:T(8,128)(2,1)S(1)}, u32[]{:S(2)}, u32[]{:S(2)}) collective-permute-start(bf16[256,128]{1,0:T(8,128)(2,1)S(1)} %get-tuple-element.33), channel_id=1, source_target_pairs={{24,0},{32,8},{40,16},{48,24},{56,32},{64,40},{72,48},{80,56},{88,... | collective-permute-start | bytes 196616 | tf_op jit(solution)/shard_map/ppermute | solution.py:264
  40.7 6.2 %collective-permute-start.6 = (bf16[256,128]{1,0:T(8,128)(2,1)S(1)}, bf16[256,128]{1,0:T(8,128)(2,1)S(1)}, u32[]{:S(2)}, u32[]{:S(2)}) collective-permute-start(bf16[256,128]{1,0:T(8,128)(2,1)S(1)} %get-tuple-element.34), channel_id=1, source_target_pairs={{8,0},{16,8},{24,16},{32,24},{40,32},{48,40},{56,48},{64,56},{72,6... | collective-permute-start | bytes 196616 | tf_op jit(solution)/shard_map/ppermute | solution.py:264
